TPU v7x, 256 devices: a whole 4x4x8 slice. The times are simulated.
256 devices in a mesh: shot: 64 (over x, z, y_hi), xline: 4 (over y_lo, core).
Axes of the slice: x: 4, y: 4 (y_hi: 2, y_lo: 2; y = y_hi * 2 + y_lo), z: 8, core: 2. Of those that a mesh axis runs over, the one named last changes fastest.
Arguments:
- surface_gathers: bfloat16 [2, 8, 16, 4096, 512], P(None, None, 'xline', 'shot'), may hold values from -6 to 6
- source_gathers: bfloat16 [2, 8, 8192, 16, 320], P(None, None, 'shot', 'xline'), may hold values from -0.09375 to 0.09375
- aperture: int32 [8192, 2], P('shot'), may hold values from -128 to 4223, as said below
- live: int32 [16, 4096], P('xline', 'shot'), may hold values from 128 to 512
Outputs:
- predicted: bfloat16 [2, 8, 8192, 512], P(None, None, 'shot', 'xline')
Inputs may be any that keep to these rules, and one draw needn't show every extreme that they name: Shot s with j = s % 128 sits at inline point c = (s // 128) * 64 + j % 64; aperture[s, 0] lies in c - 128 to c - 64, aperture[s, 1] in c + 64 to c + 128, both ends reached by the shots j = 0 and j = 127 of every block.
All inputs are finite; a program needn't handle non-finite values.
Results may differ from a plain program's by a relative error of at most 0.001.
Values may be sent and summed in bfloat16 or wider, within the bound.
No kernel may reach another device: no remote copies, remote signals or barrier semaphores. Data moves between devices by JAX's collectives and lax.ppermute only.
A program may use at most 192 MiB of HBM per device.

v0:
```python
import jax
import jax.numpy as jnp
from jax import lax
from jax.sharding import PartitionSpec as P


def passed_along(block, axis, distance):
    devices = range(lax.axis_size(axis))
    route = [(i - distance, i) for i in devices if i - distance in devices]
    return lax.ppermute(block, axis, route)


def complex_terms(shot_part, window):

    def contract(leading_operand, trailing_operand):
        return jnp.einsum(
            "ginu,gnuw->giw", leading_operand, trailing_operand, preferred_element_type=jnp.float32
        )

    real_part = contract(shot_part[0], window[0]) - contract(shot_part[1], window[1])
    imag_part = contract(shot_part[0], window[1]) + contract(shot_part[1], window[0])
    return (real_part, imag_part)


def on_device(surface_gathers, source_gathers, aperture, live):
    block_pts = surface_gathers.shape[3]
    spread = source_gathers.shape[4]
    reach_blocks = (spread // block_pts - 1) // 2
    receiver_ids = lax.broadcasted_iota(jnp.int32, surface_gathers.shape[2:], 2)
    silenced_gathers = jnp.where(
        receiver_ids < live[:, :, None], surface_gathers, jnp.zeros((), surface_gathers.dtype)
    )
    first_point = lax.axis_index("shot") * block_pts - reach_blocks * block_pts
    inline = first_point + lax.iota(jnp.int32, spread)
    inside = (inline[None, :] >= aperture[:, 0:1]) & (inline[None, :] < aperture[:, 1:2])
    masked_shots = jnp.where(
        inside[None, None, :, None, :], source_gathers, jnp.zeros((), source_gathers.dtype)
    )
    pieces = {0: silenced_gathers}
    for offset in range(1, reach_blocks + 1):
        for heading in (1, -1):
            pieces[heading * offset] = passed_along(silenced_gathers, "shot", -heading * offset)
    window = jnp.concatenate(
        [pieces[offset] for offset in range(-reach_blocks, reach_blocks + 1)], axis=3
    )
    real_sum, imag_sum = complex_terms(masked_shots, window)
    partials = jnp.stack([real_sum, imag_sum])
    summed_total = lax.psum_scatter(partials, "xline", scatter_dimension=3, tiled=True)
    return summed_total.astype(jnp.bfloat16)


def solution(mesh):
    return jax.shard_map(
        on_device,
        mesh=mesh,
        in_specs=(
            P(None, None, "xline", "shot", None),
            P(None, None, "shot", "xline", None),
            P("shot", None),
            P("xline", "shot"),
        ),
        out_specs=P(None, None, "shot", "xline"),
        check_vma=False,
    )
```

profile of v0, /device:TPU:6, one launch (start us, length us, event | category | flops | bytes accessed | tf_op | source)
XLA Modules:
  0.0 300.4 jit_solution(11706239291673601561)
XLA Ops:
  6.5 0.0 reduce-scatter.2.cloned.1.call-start
  6.5 0.8 iota_compare_fusion
  7.4 0.0 copy-start.1
  7.4 4.7 %broadcast_select_fusion.1 = bf16[2,8,4,64,512]{4,3,2,1,0:T(8,128)(2,1)} fusion(bf16[2,8,4,64,512]{4,3,2,1,0:T(8,128)(2,1)} %param.4, pred[4,64,512]{2,1,0:T(8,128)(4,1)S(1)} %iota_compare_fusion), kind=kLoop, calls=%fused_computation.8 | loop fusion | flops 2097152 | bytes 8519680 | tf_op jit(solution)/shard_map/jit(_where)/select_n | solution.py:30
  12.1 3.8 %collective-permute-start = (bf16[2,8,4,64,512]{4,3,2,1,0:T(8,128)(2,1)}, bf16[2,8,4,64,512]{4,3,2,1,0:T(8,128)(2,1)}, u32[]{:S(2)}, u32[]{:S(2)}) collective-permute-start(bf16[2,8,4,64,512]{4,3,2,1,0:T(8,128)(2,1)} %broadcast_select_fusion.1), channel_id=1, source_target_pairs={{0,8},{4,12},{8,16},{12,20},{16,24},{20,28},{24,32},{28,36},{32,40... | collective-permute-start | bytes 12582920 | tf_op jit(solution)/shard_map/ppermute | solution.py:10
  15.9 5.1 %collective-permute-start.1 = (bf16[2,8,4,64,512]{4,3,2,1,0:T(8,128)(2,1)}, bf16[2,8,4,64,512]{4,3,2,1,0:T(8,128)(2,1)}, u32[]{:S(2)}, u32[]{:S(2)}) collective-permute-start(bf16[2,8,4,64,512]{4,3,2,1,0:T(8,128)(2,1)} %broadcast_select_fusion.1), channel_id=1, source_target_pairs={{0,4},{4,8},{8,12},{12,16},{16,20},{20,24},{24,28},{28,32},{32,36}... | collective-permute-start | bytes 12582920 | tf_op jit(solution)/shard_map/ppermute | solution.py:10
  21.0 5.6 %collective-permute-start.2 = (bf16[2,8,4,64,512]{4,3,2,1,0:T(8,128)(2,1)}, bf16[2,8,4,64,512]{4,3,2,1,0:T(8,128)(2,1)}, u32[]{:S(2)}, u32[]{:S(2)}) collective-permute-start(bf16[2,8,4,64,512]{4,3,2,1,0:T(8,128)(2,1)} %broadcast_select_fusion.1), channel_id=1, source_target_pairs={{4,0},{8,4},{12,8},{16,12},{20,16},{24,20},{28,24},{32,28},{36,32}... | collective-permute-start | bytes 12582920 | tf_op jit(solution)/shard_map/ppermute | solution.py:10
  26.6 3.9 %collective-permute-start.3 = (bf16[2,8,4,64,512]{4,3,2,1,0:T(8,128)(2,1)}, bf16[2,8,4,64,512]{4,3,2,1,0:T(8,128)(2,1)}, u32[]{:S(2)}, u32[]{:S(2)}) collective-permute-start(bf16[2,8,4,64,512]{4,3,2,1,0:T(8,128)(2,1)} %broadcast_select_fusion.1), channel_id=1, source_target_pairs={{8,0},{12,4},{16,8},{20,12},{24,16},{28,20},{32,24},{36,28},{40,32... | collective-permute-start | bytes 12582920 | tf_op jit(solution)/shard_map/ppermute | solution.py:10
  30.6 0.0 copy-done.1
  30.6 0.1 compare_and_fusion
  30.7 2.9 broadcast_select_fusion
  33.6 77.4 %collective-permute-done = bf16[2,8,4,64,512]{4,3,2,1,0:T(8,128)(2,1)} collective-permute-done((bf16[2,8,4,64,512]{4,3,2,1,0:T(8,128)(2,1)}, bf16[2,8,4,64,512]{4,3,2,1,0:T(8,128)(2,1)}, u32[]{:S(2)}, u32[]{:S(2)}) %collective-permute-start) | collective-permute-done | bytes 4194336 | tf_op jit(solution)/shard_map/ppermute | solution.py:10
  111.0 4.8 %constant_dynamic-update-slice_fusion.4 = bf16[2,8,4,320,512]{4,3,2,1,0:T(8,128)(2,1)} fusion(bf16[2,8,4,64,512]{4,3,2,1,0:T(8,128)(2,1)} %collective-permute-done), kind=kLoop, calls=%fused_computation.21 | loop fusion | bytes 8388608
  115.8 0.0 copy-start
  115.8 87.9 %collective-permute-done.1 = bf16[2,8,4,64,512]{4,3,2,1,0:T(8,128)(2,1)} collective-permute-done((bf16[2,8,4,64,512]{4,3,2,1,0:T(8,128)(2,1)}, bf16[2,8,4,64,512]{4,3,2,1,0:T(8,128)(2,1)}, u32[]{:S(2)}, u32[]{:S(2)}) %collective-permute-start.1) | collective-permute-done | bytes 4194336 | tf_op jit(solution)/shard_map/ppermute | solution.py:10
  203.6 4.7 %constant_dynamic-update-slice_fusion.3 = bf16[2,8,4,320,512]{4,3,2,1,0:T(8,128)(2,1)} fusion(bf16[2,8,4,320,512]{4,3,2,1,0:T(8,128)(2,1)} %constant_dynamic-update-slice_fusion.4, bf16[2,8,4,64,512]{4,3,2,1,0:T(8,128)(2,1)} %collective-permute-done.1), kind=kLoop, calls=%fused_computation.20 | loop fusion | bytes 8388608
  208.3 0.0 copy-done
  208.3 3.2 %constant_dynamic-update-slice_fusion.2 = bf16[2,8,4,320,512]{4,3,2,1,0:T(8,128)(2,1)} fusion(bf16[2,8,4,320,512]{4,3,2,1,0:T(8,128)(2,1)} %constant_dynamic-update-slice_fusion.3, bf16[2,8,4,64,512]{4,3,2,1,0:T(8,128)(2,1)S(1)} %copy-done, pred[4,64,512]{2,1,0:T(8,128)(4,1)S(1)} %iota_compare_fusion), kind=kLoop, calls=%fused_computation.19 | loop fusion | flops 2097152 | bytes 8519680
  211.5 0.0 collective-permute-done.2
  211.5 4.7 %constant_dynamic-update-slice_fusion.1 = bf16[2,8,4,320,512]{4,3,2,1,0:T(8,128)(2,1)} fusion(bf16[2,8,4,320,512]{4,3,2,1,0:T(8,128)(2,1)} %constant_dynamic-update-slice_fusion.2, bf16[2,8,4,64,512]{4,3,2,1,0:T(8,128)(2,1)} %collective-permute-done.2), kind=kLoop, calls=%fused_computation.18 | loop fusion | bytes 8388608
  216.1 0.0 collective-permute-done.3
  216.1 4.7 %constant_dynamic-update-slice_fusion = bf16[2,8,4,320,512]{4,3,2,1,0:T(8,128)(2,1)} fusion(bf16[2,8,4,320,512]{4,3,2,1,0:T(8,128)(2,1)} %constant_dynamic-update-slice_fusion.1, bf16[2,8,4,64,512]{4,3,2,1,0:T(8,128)(2,1)} %collective-permute-done.3), kind=kLoop, calls=%fused_computation.17 | loop fusion | bytes 8388608 | tf_op jit(solution)/shard_map/concatenate | solution.py:43
  220.8 5.0 %fusion.1 = f32[8,128,512,1]{2,1,3,0:T(8,128)S(1)} fusion(bf16[2,8,4,320,512]{4,3,2,1,0:T(8,128)(2,1)} %constant_dynamic-update-slice_fusion, bf16[2,8,128,4,320]{2,4,3,1,0:T(8,128)(2,1)S(1)} %broadcast_select_fusion), kind=kOutput, calls=%fused_computation.3 | convolution fusion | flops 1342177280 | bytes 15204352 | tf_op jit(solution)/shard_map/ginu,gnuw->giw/dot_general | solution.py:16
  225.9 5.0 %fusion.2 = f32[8,128,512,1]{2,1,3,0:T(8,128)S(1)} fusion(bf16[2,8,4,320,512]{4,3,2,1,0:T(8,128)(2,1)} %constant_dynamic-update-slice_fusion, bf16[2,8,128,4,320]{2,4,3,1,0:T(8,128)(2,1)S(1)} %broadcast_select_fusion), kind=kOutput, calls=%fused_computation.4 | convolution fusion | flops 1342177280 | bytes 15204352 | tf_op jit(solution)/shard_map/ginu,gnuw->giw/dot_general | solution.py:16
  230.9 5.1 %fusion.5 = f32[1,8,128,512]{3,2,1,0:T(8,128)S(1)} fusion(f32[8,128,512,1]{2,1,3,0:T(8,128)S(1)} %fusion.1, bf16[2,8,4,320,512]{4,3,2,1,0:T(8,128)(2,1)} %constant_dynamic-update-slice_fusion, bf16[2,8,128,4,320]{2,4,3,1,0:T(8,128)(2,1)S(1)} %broadcast_select_fusion), kind=kOutput, calls=%fused_computation.14 | convolution fusion | flops 1342701568 | bytes 17301504 | tf_op jit(solution)/shard_map/ginu,gnuw->giw/dot_general | solution.py:16
  236.0 5.1 %fusion.4 = f32[1,8,128,512]{3,2,1,0:T(8,128)S(1)} fusion(f32[8,128,512,1]{2,1,3,0:T(8,128)S(1)} %fusion.2, bf16[2,8,4,320,512]{4,3,2,1,0:T(8,128)(2,1)} %constant_dynamic-update-slice_fusion, bf16[2,8,128,4,320]{2,4,3,1,0:T(8,128)(2,1)S(1)} %broadcast_select_fusion), kind=kOutput, calls=%fused_computation.12 | convolution fusion | flops 1342701568 | bytes 17301504 | tf_op jit(solution)/shard_map/ginu,gnuw->giw/dot_general | solution.py:16
  241.0 2.4 pad_maximum_fusion
  243.4 0.0 reduce-scatter.2.cloned.1.call-update
  243.4 48.0 %reduce-scatter.2.cloned.1.call-done = f32[2,8,128,128]{3,2,1,0:T(8,128)} async-done(((f32[2,8,128,512]{3,2,1,0:T(8,128)}), f32[2,8,128,128]{3,2,1,0:T(8,128)}) %reduce-scatter.2.cloned.1.call-update) | async-done | bytes 1048592 | tf_op jit(solution)/shard_map/reduce_scatter | solution.py:48
  291.4 2.1 convert_element_type.3
  (2 shorter events, 0.0 us)
Async XLA Ops:
  6.5 284.9 %reduce-scatter.2.cloned.1.call-start = ((), (), s32[]{:S(2)}) async-start(), calls=%async_computation.1 | async-start | bytes 5242880 | tf_op jit(solution)/shard_map/reduce_scatter | solution.py:48
  7.4 23.2 %copy-start.1 = (s32[128,2]{0,1:T(2,128)S(1)}, s32[128,2]{0,1:T(2,128)}, u32[]{:S(2)}) copy-start(s32[128,2]{0,1:T(2,128)} %param.6) | copy-start | bytes 3076
  12.1 98.9 %collective-permute-start = (bf16[2,8,4,64,512]{4,3,2,1,0:T(8,128)(2,1)}, bf16[2,8,4,64,512]{4,3,2,1,0:T(8,128)(2,1)}, u32[]{:S(2)}, u32[]{:S(2)}) collective-permute-start(bf16[2,8,4,64,512]{4,3,2,1,0:T(8,128)(2,1)} %broadcast_select_fusion.1), channel_id=1, source_target_pairs={{0,8},{4,12},{8,16},{12,20},{16,24},{20,28},{24,32},{28,36},{32,40... | collective-permute-start | bytes 12582920 | tf_op jit(solution)/shard_map/ppermute | solution.py:10
  15.9 187.7 %collective-permute-start.1 = (bf16[2,8,4,64,512]{4,3,2,1,0:T(8,128)(2,1)}, bf16[2,8,4,64,512]{4,3,2,1,0:T(8,128)(2,1)}, u32[]{:S(2)}, u32[]{:S(2)}) collective-permute-start(bf16[2,8,4,64,512]{4,3,2,1,0:T(8,128)(2,1)} %broadcast_select_fusion.1), channel_id=1, source_target_pairs={{0,4},{4,8},{8,12},{12,16},{16,20},{20,24},{24,28},{28,32},{32,36}... | collective-permute-start | bytes 12582920 | tf_op jit(solution)/shard_map/ppermute | solution.py:10
  21.0 190.4 %collective-permute-start.2 = (bf16[2,8,4,64,512]{4,3,2,1,0:T(8,128)(2,1)}, bf16[2,8,4,64,512]{4,3,2,1,0:T(8,128)(2,1)}, u32[]{:S(2)}, u32[]{:S(2)}) collective-permute-start(bf16[2,8,4,64,512]{4,3,2,1,0:T(8,128)(2,1)} %broadcast_select_fusion.1), channel_id=1, source_target_pairs={{4,0},{8,4},{12,8},{16,12},{20,16},{24,20},{28,24},{32,28},{36,32}... | collective-permute-start | bytes 12582920 | tf_op jit(solution)/shard_map/ppermute | solution.py:10
  26.6 189.5 %collective-permute-start.3 = (bf16[2,8,4,64,512]{4,3,2,1,0:T(8,128)(2,1)}, bf16[2,8,4,64,512]{4,3,2,1,0:T(8,128)(2,1)}, u32[]{:S(2)}, u32[]{:S(2)}) collective-permute-start(bf16[2,8,4,64,512]{4,3,2,1,0:T(8,128)(2,1)} %broadcast_select_fusion.1), channel_id=1, source_target_pairs={{8,0},{12,4},{16,8},{20,12},{24,16},{28,20},{32,24},{36,28},{40,32... | collective-permute-start | bytes 12582920 | tf_op jit(solution)/shard_map/ppermute | solution.py:10
  115.8 92.5 %copy-start = (bf16[2,8,4,64,512]{4,3,2,1,0:T(8,128)(2,1)S(1)}, bf16[2,8,4,64,512]{4,3,2,1,0:T(8,128)(2,1)}, u32[]{:S(2)}) copy-start(bf16[2,8,4,64,512]{4,3,2,1,0:T(8,128)(2,1)} %param.4) | copy-start | bytes 12582916
Sparse Core Ops, SparseCore 0:
  243.6 47.8 reduce-scatter.1
where the time goes:
time: 302 us; the launch traced here: 300 us
  waiting for transfers between devices  213 us (71%)
  matrix products  20.2 us (7%)
  local copies, waits for them, and re-layouts  18.8 us (6%)
  starting transfers between devices  18.4 us (6%)
  other arithmetic  16.2 us (5%)
  between operations  13.5 us (4%)
    ppermute x4, waiting for transfers between devices, passed_along(): return lax.ppermute(block, axis, route)  165 us
    reduce_scatter x1, waiting for transfers between devices, on_device(): lax.psum_scatter(partials, 'xline', scatter_dimension=3, tiled=True)  48 us
    dot_general x4, matrix products, contract(): jnp.einsum('ginu,gnuw->giw', leading_operand, trailing_operand, preferred...  20.2 us
    ppermute x4, starting transfers between devices, passed_along(): return lax.ppermute(block, axis, route)  18.4 us
    unnamed x7, local copies, waits for them, and re-layouts  14.1 us
  transfers between devices with their start and end apart: 5, of which 3 were waited for; matrix products, arithmetic and copies ran while one was open for 7% of the time, Pallas kernels for 0%

commit v1 on v0

v1 whole, which is shorter than its diff:
```python
import functools

import jax
import jax.numpy as jnp
from jax import lax
from jax.experimental import pallas as pl
from jax.experimental.pallas import tpu as pltpu
from jax.sharding import Mesh, PartitionSpec as P

CHUNKS = (2, 2, 2, 2)
SHOT = ("sup", "half")
XLINE = ("side", "core")
RING = ("half", "side")


def shifted(block, distance):
    n = lax.axis_size("sup")
    return lax.ppermute(
        block, "sup", [(i, i + distance) for i in range(n) if 0 <= i + distance < n]
    )


def swapped(block, axis):
    return lax.ppermute(block, axis, [(0, 1), (1, 0)])


def products_kernel(place, below, here, above, own, cross, keep, send):
    half, core = place[0], place[1]
    upper = half == 1
    pts, recv = below.shape[3], below.shape[4]
    shots = own.shape[4]
    rows = below.shape[2] * pts

    def flat(values):
        return values.reshape(rows, shots)

    lefts = []
    for part in range(2):
        mine = [flat(own[part, 0, :, 2 * k * pts : (2 * k + 1) * pts, :]) for k in range(3)]
        low, high = (flat(cross[part, 0, :, k * pts : (k + 1) * pts, :]) for k in range(2))
        none = jnp.zeros_like(low)
        theirs = [
            jnp.where(upper, low, none),
            jnp.where(upper, high, low),
            jnp.where(upper, none, high),
        ]
        lefts.append([jnp.concatenate(pair, axis=1) for pair in zip(mine, theirs)])
    total = jnp.zeros((4 * shots, recv), jnp.float32)
    for k, window in enumerate((below, here, above)):
        real, imag = lefts[0][k], lefts[1][k]
        for part, left in enumerate(
            (jnp.concatenate([real, imag], axis=1), jnp.concatenate([-imag, real], axis=1))
        ):
            total += lax.dot_general(
                left,
                window[part, 0].reshape(rows, recv),
                (((0,), (0,)), ((), ())),
                preferred_element_type=jnp.float32,
            )
    width = recv // 4
    for side in range(2):
        even = total[:, 2 * side * width : (2 * side + 1) * width]
        odd = total[:, (2 * side + 1) * width : (2 * side + 2) * width]
        stays = jnp.where(core == 0, even, odd)
        leaves = jnp.where(core == 0, odd, even)
        for part in range(2):
            for block, to in enumerate((half, 1 - half)):
                first = (2 * part + block) * shots
                keep[to, side, part, 0] = stays[first : first + shots]
                send[to, side, part, 0] = leaves[first : first + shots]


def products(place, below, here, above, own, cross, first):
    freqs, xs, pts, recv = here.shape[1:]
    spread, shots = own.shape[3:]

    def of_freq(shape, offset=0):
        return pl.BlockSpec((2, 1) + shape, lambda f: (0, f + offset, 0, 0, 0))

    window = of_freq((xs, pts, recv))
    out = jax.ShapeDtypeStruct((2, 2, 2, freqs, shots, recv // 4), jnp.float32)
    out_spec = pl.BlockSpec((2, 2, 2, 1, shots, recv // 4), lambda f: (0, 0, 0, f, 0, 0))
    flops = freqs * 2 * (4 * shots) * (6 * xs * pts) * recv
    return pl.pallas_call(
        products_kernel,
        grid=(freqs,),
        in_specs=[
            pl.BlockSpec(memory_space=pltpu.SMEM),
            window,
            window,
            window,
            of_freq((xs, spread, shots), first),
            of_freq((xs, 2 * pts, shots)),
        ],
        out_specs=[out_spec, out_spec],
        out_shape=[out, out],
        compiler_params=pltpu.CompilerParams(vmem_limit_bytes=24 * 2**20),
        cost_estimate=pl.CostEstimate(
            flops=flops, bytes_accessed=freqs * 4 * 2**20, transcendentals=0
        ),
    )(place, below, here, above, own, cross)


def on_device(surface_gathers, source_gathers, aperture, live):
    pts, recv = surface_gathers.shape[3:]
    spread = source_gathers.shape[4]
    half, core = lax.axis_index("half"), lax.axis_index("core")
    place = jnp.stack([half, core]).astype(jnp.int32)
    heard = lax.broadcasted_iota(jnp.int32, surface_gathers.shape[2:], 2) < live[:, :, None]
    chunks = [(sum(CHUNKS[:i]), size) for i, size in enumerate(CHUNKS)]

    here, below, above = [], [], []
    for first, size in chunks:
        gathers = surface_gathers[:, first : first + size]
        here.append(jnp.where(heard, gathers, jnp.zeros((), gathers.dtype)))
        below.append(shifted(here[-1], 1))
        above.append(shifted(here[-1], -1))

    first_point = (2 * lax.axis_index("sup") + half) * pts - (spread - pts) // 2
    inline = first_point + lax.broadcasted_iota(jnp.int32, (spread, aperture.shape[0]), 0)
    inside = (inline >= aperture[:, 0][None, :]) & (inline < aperture[:, 1][None, :])
    shots = source_gathers.transpose(0, 1, 3, 4, 2)
    masked = jnp.where(inside, shots, jnp.zeros((), shots.dtype))
    crossing = jnp.concatenate(
        [masked[:, :, :, pts : 2 * pts], masked[:, :, :, 3 * pts : 4 * pts]], axis=3
    )
    cross = [swapped(crossing[:, first : first + size], "half") for first, size in chunks]

    predicted = []
    for i, (first, size) in enumerate(chunks):
        keep, send = products(place, below[i], here[i], above[i], masked, cross[i], first)
        partial = keep + swapped(send, "core")
        partial = partial.reshape((4,) + partial.shape[2:])
        terms = lax.all_to_all(partial, RING, 0, 0, tiled=True)
        predicted.append(terms.sum(axis=0).astype(jnp.bfloat16))
    return jnp.concatenate(predicted, axis=1)


def solution(mesh):
    fine = Mesh(
        mesh.devices.reshape(mesh.shape["shot"] // 2, 2, mesh.shape["xline"] // 2, 2),
        SHOT + XLINE,
    )
    return jax.shard_map(
        on_device,
        mesh=fine,
        in_specs=(
            P(None, None, XLINE, SHOT, None),
            P(None, None, SHOT, XLINE, None),
            P(SHOT, None),
            P(XLINE, SHOT),
        ),
        out_specs=P(None, None, SHOT, XLINE),
        check_vma=False,
    )
```

time: 302 us -> 160 us (0.53)
  waiting for transfers between devices: 213 us -> 47.3 us
  starting transfers between devices: 18.4 us -> 60.5 us
  matrix products: 20.2 us -> 0 us
  Pallas kernels: 0 us -> 16.4 us
  between operations: 13.5 us -> 0.24 us
  local copies, waits for them, and re-layouts: 18.8 us -> 13.6 us
  other arithmetic: 16.2 us -> 20.3 us
    ppermute x4 -> x16, waiting for transfers between devices: 165 us -> 20.5 us  [the longest x8 13.1 us: swapped(): return lax.ppermute(block, axis, [(0, 1), (1, 0)])]
    reduce_scatter x1 -> x0, waiting for transfers between devices: 48 us -> none  [on_device(): lax.psum_scatter(partials, 'xline', scatter_dimension=3, tiled=True)]
    all_to_all x0 -> x4, waiting for transfers between devices: none -> 26.8 us  [on_device(): terms = lax.all_to_all(partial, RING, 0, 0, tiled=True)]
    ppermute x4 -> x16, starting transfers between devices: 18.4 us -> 44 us  [the longest x8 31.1 us: shifted(): lax.ppermute(block, 'sup', [(i, i + distance) for i in range(n) if 0 <= i...]
    dot_general x4 -> x0, matrix products: 20.2 us -> none  [contract(): jnp.einsum('ginu,gnuw->giw', leading_operand, trailing_operand, preferred...]
    all_to_all x0 -> x4, starting transfers between devices: none -> 16.5 us  [on_device(): terms = lax.all_to_all(partial, RING, 0, 0, tiled=True)]
    pallas_call x0 -> x4, Pallas kernels: none -> 16.4 us  [products(): pl.pallas_call(products_kernel, grid=(freqs,), in_specs=[pl.BlockSpec(mem...]
    add x1 -> x5, other arithmetic: 0.01 us -> 7.62 us  [the longest x4 7.62 us: on_device(): partial = keep + swapped(send, 'core')]
  transfers between devices with their start and end apart: 5 -> 20, of which waited for: 3 -> 8; matrix products, arithmetic and copies ran while one was open for 7% -> 10% of each run, Pallas kernels for 0% -> 10%
where the time goes in v1:
time: 160 us; the launch traced here: 158 us
  starting transfers between devices  60.5 us (38%)
  waiting for transfers between devices  47.3 us (30%)
  other arithmetic  20.3 us (13%)
  Pallas kernels  16.4 us (10%)
  local copies, waits for them, and re-layouts  13.6 us (8%)
    ppermute x8, starting transfers between devices, shifted(): lax.ppermute(block, 'sup', [(i, i + distance) for i in range(n) if 0 <= i...  31.1 us
    all_to_all x4, waiting for transfers between devices, on_device(): terms = lax.all_to_all(partial, RING, 0, 0, tiled=True)  26.8 us
    all_to_all x4, starting transfers between devices, on_device(): terms = lax.all_to_all(partial, RING, 0, 0, tiled=True)  16.5 us
    pallas_call x4, Pallas kernels, products(): pl.pallas_call(products_kernel, grid=(freqs,), in_specs=[pl.BlockSpec(mem...  16.4 us
    unnamed x22, local copies, waits for them, and re-layouts  13.4 us
    ppermute x8, waiting for transfers between devices, swapped(): return lax.ppermute(block, axis, [(0, 1), (1, 0)])  13.1 us
    ppermute x8, starting transfers between devices, swapped(): return lax.ppermute(block, axis, [(0, 1), (1, 0)])  12.9 us
    add x4, other arithmetic, on_device(): partial = keep + swapped(send, 'core')  7.62 us
  transfers between devices with their start and end apart: 20, of which 8 were waited for; matrix products, arithmetic and copies ran while one was open for 10% of the time, Pallas kernels for 10%

profile of v1, /device:TPU:6, one launch (start us, length us, event | category | flops | bytes accessed | tf_op | source)
XLA Modules:
  0.0 158.3 jit_solution(13014203001342106773)
XLA Ops:
  0.8 3.5 %slice_select_fusion.3 = (bf16[2,2,4,64,512]{4,3,2,1,0:T(8,128)(2,1)}, bf16[2,2,4,64,512]{4,3,2,1,0:T(8,128)(2,1)S(1)}, bf16[2,2,4,64,512]{4,3,2,1,0:T(8,128)(2,1)S(1)}, bf16[2,2,4,64,512]{4,3,2,1,0:T(8,128)(2,1)S(1)}) fusion(bf16[2,8,4,64,512]{4,3,2,1,0:T(8,128)(2,1)} %param.4, pred[4,64,512]{2,1,0:T(8,128)(4,1)S(1)} %iota_compare_fusion), kind=kLoop, calls=%fused_computation.10 | loop fusion | flops 2097152 | bytes 8519680 | tf_op jit(solution)/shard_map/jit(_where)/select_n | solution.py:115
  4.4 3.8 %collective-permute-start = (bf16[2,2,4,64,512]{4,3,2,1,0:T(8,128)(2,1)}, bf16[2,2,4,64,512]{4,3,2,1,0:T(8,128)(2,1)}, u32[]{:S(2)}, u32[]{:S(2)}) collective-permute-start(bf16[2,2,4,64,512]{4,3,2,1,0:T(8,128)(2,1)} %get-tuple-element.23.here), channel_id=1, source_target_pairs={{0,8},{8,16},{16,24},{24,32},{32,40},{40,48},{48,56},{56,64},{64,7... | collective-permute-start | bytes 3145736 | tf_op jit(solution)/shard_map/ppermute | solution.py:18
  8.2 6.1 %collective-permute-start.1 = (bf16[2,2,4,64,512]{4,3,2,1,0:T(8,128)(2,1)}, bf16[2,2,4,64,512]{4,3,2,1,0:T(8,128)(2,1)}, u32[]{:S(2)}, u32[]{:S(2)}) collective-permute-start(bf16[2,2,4,64,512]{4,3,2,1,0:T(8,128)(2,1)} %get-tuple-element.23.here), channel_id=1, source_target_pairs={{8,0},{16,8},{24,16},{32,24},{40,32},{48,40},{56,48},{64,56},{72,6... | collective-permute-start | bytes 3145736 | tf_op jit(solution)/shard_map/ppermute | solution.py:18
  14.5 2.9 %bitcast_select_fusion.own = bf16[2,8,4,320,128]{4,3,2,1,0:T(8,128)(2,1)S(1)} fusion(bf16[2,8,128,4,320]{2,4,3,1,0:T(8,128)(2,1)} %param.5, pred[320,128]{1,0:T(8,128)(4,1)S(1)} %compare_and_fusion), kind=kLoop, calls=%fused_computation | loop fusion | flops 2621440 | bytes 10526720 | tf_op jit(solution)/shard_map/jit(_where)/select_n | solution.py:123
  20.3 3.2 %collective-permute-start.2 = (bf16[2,2,4,128,128]{4,3,2,1,0:T(8,128)(2,1)}, bf16[2,2,4,128,128]{4,3,2,1,0:T(8,128)(2,1)}, u32[]{:S(2)}, u32[]{:S(2)}) collective-permute-start(bf16[2,2,4,128,128]{4,3,2,1,0:T(8,128)(2,1)} %get-tuple-element.27), channel_id=1, source_target_pairs={{0,4},{4,0},{1,5},{5,1},{2,6},{6,2},{3,7},{7,3},{8,12},{12,8},{9,1... | collective-permute-start | bytes 1572872 | tf_op jit(solution)/shard_map/ppermute | solution.py:24
  25.4 6.0 %collective-permute-start.5 = (bf16[2,2,4,64,512]{4,3,2,1,0:T(8,128)(2,1)S(1)}, bf16[2,2,4,64,512]{4,3,2,1,0:T(8,128)(2,1)}, u32[]{:S(2)}, u32[]{:S(2)}) collective-permute-start(bf16[2,2,4,64,512]{4,3,2,1,0:T(8,128)(2,1)S(1)} %get-tuple-element.24.here), channel_id=1, source_target_pairs={{8,0},{16,8},{24,16},{32,24},{40,32},{48,40},{56,48},{64,56},{72,6... | collective-permute-start | bytes 3145736 | tf_op jit(solution)/shard_map/ppermute | solution.py:18
  31.6 4.0 %collective-permute-done.2.cross = bf16[2,2,4,128,128]{4,3,2,1,0:T(8,128)(2,1)} collective-permute-done((bf16[2,2,4,128,128]{4,3,2,1,0:T(8,128)(2,1)}, bf16[2,2,4,128,128]{4,3,2,1,0:T(8,128)(2,1)}, u32[]{:S(2)}, u32[]{:S(2)}) %collective-permute-start.2) | collective-permute-done | bytes 524320 | tf_op jit(solution)/shard_map/ppermute | solution.py:24
  35.5 3.2 %collective-permute-start.6 = (bf16[2,2,4,128,128]{4,3,2,1,0:T(8,128)(2,1)}, bf16[2,2,4,128,128]{4,3,2,1,0:T(8,128)(2,1)S(1)}, u32[]{:S(2)}, u32[]{:S(2)}) collective-permute-start(bf16[2,2,4,128,128]{4,3,2,1,0:T(8,128)(2,1)} %get-tuple-element.28), channel_id=1, source_target_pairs={{0,4},{4,0},{1,5},{5,1},{2,6},{6,2},{3,7},{7,3},{8,12},{12,8},{9,1... | collective-permute-start | bytes 1572872 | tf_op jit(solution)/shard_map/ppermute | solution.py:24
  38.7 2.5 %copy-done.1 = bf16[2,8,4,320,128]{4,3,2,1,0:T(8,128)(2,1)S(1)} copy-done((bf16[2,8,4,320,128]{4,3,2,1,0:T(8,128)(2,1)S(1)}, bf16[2,8,4,320,128]{4,3,2,1,0:T(8,128)(2,1)}, u32[]{:S(2)}) %copy-start.1) | copy-done | bytes 5242904
  41.2 3.7 %shard_map.46 = (f32[2,2,2,2,128,128]{5,4,3,2,1,0:T(8,128)S(1)}, f32[2,2,2,2,128,128]{5,4,3,2,1,0:T(8,128)S(1)}) custom-call(s32[2]{0:T(128)S(1)} %pad_add_fusion.place, bf16[2,2,4,64,512]{4,3,2,1,0:T(8,128)(2,1)} %collective-permute-done.below, bf16[2,2,4,64,512]{4,3,2,1,0:T(8,128)(2,1)} %get-tuple-element.23.here, ...), custom_call_target="tpu_custom_call" | custom-call | flops 1610612736 | bytes 8388608 | tf_op jit(solution)/shard_map/pallas_call | solution.py:84
  45.0 1.9 %collective-permute-start.8 = (bf16[2,2,4,64,512]{4,3,2,1,0:T(8,128)(2,1)S(1)}, bf16[2,2,4,64,512]{4,3,2,1,0:T(8,128)(2,1)}, u32[]{:S(2)}, u32[]{:S(2)}) collective-permute-start(bf16[2,2,4,64,512]{4,3,2,1,0:T(8,128)(2,1)S(1)} %get-tuple-element.26.here), channel_id=1, source_target_pairs={{0,8},{8,16},{16,24},{24,32},{32,40},{40,48},{48,56},{56,64},{64,7... | collective-permute-start | bytes 3145736 | tf_op jit(solution)/shard_map/ppermute | solution.py:18
  47.0 2.7 %collective-permute-done.6.cross = bf16[2,2,4,128,128]{4,3,2,1,0:T(8,128)(2,1)S(1)} collective-permute-done((bf16[2,2,4,128,128]{4,3,2,1,0:T(8,128)(2,1)}, bf16[2,2,4,128,128]{4,3,2,1,0:T(8,128)(2,1)S(1)}, u32[]{:S(2)}, u32[]{:S(2)}) %collective-permute-start.6) | collective-permute-done | bytes 524320 | tf_op jit(solution)/shard_map/ppermute | solution.py:24
  49.7 3.3 %collective-permute-start.9 = (bf16[2,2,4,64,512]{4,3,2,1,0:T(8,128)(2,1)S(1)}, bf16[2,2,4,64,512]{4,3,2,1,0:T(8,128)(2,1)}, u32[]{:S(2)}, u32[]{:S(2)}) collective-permute-start(bf16[2,2,4,64,512]{4,3,2,1,0:T(8,128)(2,1)S(1)} %get-tuple-element.26.here), channel_id=1, source_target_pairs={{8,0},{16,8},{24,16},{32,24},{40,32},{48,40},{56,48},{64,56},{72,6... | collective-permute-start | bytes 3145736 | tf_op jit(solution)/shard_map/ppermute | solution.py:18
  53.1 6.1 %collective-permute-done.4.below = bf16[2,2,4,64,512]{4,3,2,1,0:T(8,128)(2,1)} collective-permute-done((bf16[2,2,4,64,512]{4,3,2,1,0:T(8,128)(2,1)S(1)}, bf16[2,2,4,64,512]{4,3,2,1,0:T(8,128)(2,1)}, u32[]{:S(2)}, u32[]{:S(2)}) %collective-permute-start.4) | collective-permute-done | bytes 1048608 | tf_op jit(solution)/shard_map/ppermute | solution.py:18
  59.1 3.2 %collective-permute-start.10 = (bf16[2,2,4,128,128]{4,3,2,1,0:T(8,128)(2,1)}, bf16[2,2,4,128,128]{4,3,2,1,0:T(8,128)(2,1)}, u32[]{:S(2)}, u32[]{:S(2)}) collective-permute-start(bf16[2,2,4,128,128]{4,3,2,1,0:T(8,128)(2,1)} %get-tuple-element.30), channel_id=1, source_target_pairs={{0,4},{4,0},{1,5},{5,1},{2,6},{6,2},{3,7},{7,3},{8,12},{12,8},{9,1... | collective-permute-start | bytes 1572872 | tf_op jit(solution)/shard_map/ppermute | solution.py:24
  62.3 4.3 %shard_map.47 = (f32[2,2,2,2,128,128]{5,4,3,2,1,0:T(8,128)S(1)}, f32[2,2,2,2,128,128]{5,4,3,2,1,0:T(8,128)}) custom-call(s32[2]{0:T(128)S(1)} %pad_add_fusion.place, bf16[2,2,4,64,512]{4,3,2,1,0:T(8,128)(2,1)} %collective-permute-done.4.below, bf16[2,2,4,64,512]{4,3,2,1,0:T(8,128)(2,1)S(1)} %get-tuple-element.24.here, ...), custom_call_target="tpu_custom_call" | custom-call | flops 1610612736 | bytes 8388608 | tf_op jit(solution)/shard_map/pallas_call | solution.py:84
  68.7 4.3 %all-to-all-start = ((f32[4,2,2,128,128]{4,3,2,1,0:T(8,128)}), f32[4,2,2,128,128]{4,3,2,1,0:T(8,128)}, u32[]{:S(2)}, u32[]{:S(2)}) async-start(f32[4,2,2,128,128]{4,3,2,1,0:T(8,128)} %bitcast.5), calls=%async_computation | async-start | bytes 2097152 | tf_op jit(solution)/shard_map/all_to_all | solution.py:134
  73.0 1.9 %collective-permute-start.12 = (bf16[2,2,4,64,512]{4,3,2,1,0:T(8,128)(2,1)S(1)}, bf16[2,2,4,64,512]{4,3,2,1,0:T(8,128)(2,1)S(1)}, u32[]{:S(2)}, u32[]{:S(2)}) collective-permute-start(bf16[2,2,4,64,512]{4,3,2,1,0:T(8,128)(2,1)S(1)} %get-tuple-element.25.here), channel_id=1, source_target_pairs={{0,8},{8,16},{16,24},{24,32},{32,40},{40,48},{48,56},{56,64},{64,7... | collective-permute-start | bytes 3145736 | tf_op jit(solution)/shard_map/ppermute | solution.py:18
  74.9 6.0 %collective-permute-start.13 = (bf16[2,2,4,64,512]{4,3,2,1,0:T(8,128)(2,1)S(1)}, bf16[2,2,4,64,512]{4,3,2,1,0:T(8,128)(2,1)}, u32[]{:S(2)}, u32[]{:S(2)}) collective-permute-start(bf16[2,2,4,64,512]{4,3,2,1,0:T(8,128)(2,1)S(1)} %get-tuple-element.25.here), channel_id=1, source_target_pairs={{8,0},{16,8},{24,16},{32,24},{40,32},{48,40},{56,48},{64,56},{72,6... | collective-permute-start | bytes 3145736 | tf_op jit(solution)/shard_map/ppermute | solution.py:18
  82.4 2.5 %copy-done.2 = bf16[2,8,4,320,128]{4,3,2,1,0:T(8,128)(2,1)S(1)} copy-done((bf16[2,8,4,320,128]{4,3,2,1,0:T(8,128)(2,1)S(1)}, bf16[2,8,4,320,128]{4,3,2,1,0:T(8,128)(2,1)}, u32[]{:S(2)}) %copy-start.2) | copy-done | bytes 5242904
  84.8 4.3 %shard_map.48 = (f32[2,2,2,2,128,128]{5,4,3,2,1,0:T(8,128)S(1)}, f32[2,2,2,2,128,128]{5,4,3,2,1,0:T(8,128)}) custom-call(s32[2]{0:T(128)S(1)} %pad_add_fusion.place, bf16[2,2,4,64,512]{4,3,2,1,0:T(8,128)(2,1)} %collective-permute-done.8.below, bf16[2,2,4,64,512]{4,3,2,1,0:T(8,128)(2,1)S(1)} %get-tuple-element.26.here, ...), custom_call_target="tpu_custom_call" | custom-call | flops 1610612736 | bytes 8388608 | tf_op jit(solution)/shard_map/pallas_call | solution.py:84
  90.1 3.2 %collective-permute-start.14 = (bf16[2,2,4,128,128]{4,3,2,1,0:T(8,128)(2,1)}, bf16[2,2,4,128,128]{4,3,2,1,0:T(8,128)(2,1)S(1)}, u32[]{:S(2)}, u32[]{:S(2)}) collective-permute-start(bf16[2,2,4,128,128]{4,3,2,1,0:T(8,128)(2,1)} %get-tuple-element.29), channel_id=1, source_target_pairs={{0,4},{4,0},{1,5},{5,1},{2,6},{6,2},{3,7},{7,3},{8,12},{12,8},{9,1... | collective-permute-start | bytes 1572872 | tf_op jit(solution)/shard_map/ppermute | solution.py:24
  93.3 2.7 %add.27 = f32[2,2,2,2,128,128]{5,4,3,2,1,0:T(8,128)} add(f32[2,2,2,2,128,128]{5,4,3,2,1,0:T(8,128)} %copy-done.4, f32[2,2,2,2,128,128]{5,4,3,2,1,0:T(8,128)} %collective-permute-done.7) | non-fusion elementwise | flops 262144 | bytes 3145728 | tf_op jit(solution)/shard_map/add | solution.py:132
  96.0 4.2 %all-to-all-start.1 = ((f32[4,2,2,128,128]{4,3,2,1,0:T(8,128)}), f32[4,2,2,128,128]{4,3,2,1,0:T(8,128)}, u32[]{:S(2)}, u32[]{:S(2)}) async-start(f32[4,2,2,128,128]{4,3,2,1,0:T(8,128)} %bitcast.12), calls=%async_computation.1 | async-start | bytes 2097152 | tf_op jit(solution)/shard_map/all_to_all | solution.py:134
  100.2 6.3 %collective-permute-done.14.cross = bf16[2,2,4,128,128]{4,3,2,1,0:T(8,128)(2,1)S(1)} collective-permute-done((bf16[2,2,4,128,128]{4,3,2,1,0:T(8,128)(2,1)}, bf16[2,2,4,128,128]{4,3,2,1,0:T(8,128)(2,1)S(1)}, u32[]{:S(2)}, u32[]{:S(2)}) %collective-permute-start.14) | collective-permute-done | bytes 524320 | tf_op jit(solution)/shard_map/ppermute | solution.py:24
  107.4 2.5 %copy-done.3 = bf16[2,8,4,320,128]{4,3,2,1,0:T(8,128)(2,1)S(1)} copy-done((bf16[2,8,4,320,128]{4,3,2,1,0:T(8,128)(2,1)S(1)}, bf16[2,8,4,320,128]{4,3,2,1,0:T(8,128)(2,1)}, u32[]{:S(2)}) %copy-start.3) | copy-done | bytes 5242904
  110.9 4.1 %shard_map.49 = (f32[2,2,2,2,128,128]{5,4,3,2,1,0:T(8,128)S(1)}, f32[2,2,2,2,128,128]{5,4,3,2,1,0:T(8,128)}) custom-call(s32[2]{0:T(128)S(1)} %pad_add_fusion.place, bf16[2,2,4,64,512]{4,3,2,1,0:T(8,128)(2,1)S(1)} %collective-permute-done.12.below, bf16[2,2,4,64,512]{4,3,2,1,0:T(8,128)(2,1)S(1)} %get-tuple-element.25.here, ...), custom_call_target="tpu_custom_call" | custom-call | flops 1610612736 | bytes 8388608 | tf_op jit(solution)/shard_map/pallas_call | solution.py:84
  116.1 2.7 %add.28 = f32[2,2,2,2,128,128]{5,4,3,2,1,0:T(8,128)} add(f32[2,2,2,2,128,128]{5,4,3,2,1,0:T(8,128)} %copy-done.5, f32[2,2,2,2,128,128]{5,4,3,2,1,0:T(8,128)} %collective-permute-done.11) | non-fusion elementwise | flops 262144 | bytes 3145728 | tf_op jit(solution)/shard_map/add | solution.py:132
  118.8 4.5 %all-to-all-start.2 = ((f32[4,2,2,128,128]{4,3,2,1,0:T(8,128)}), f32[4,2,2,128,128]{4,3,2,1,0:T(8,128)S(1)}, u32[]{:S(2)}, u32[]{:S(2)}) async-start(f32[4,2,2,128,128]{4,3,2,1,0:T(8,128)} %bitcast.7), calls=%async_computation.2 | async-start | bytes 2097152 | tf_op jit(solution)/shard_map/all_to_all | solution.py:134
  124.4 14.6 %all-to-all-done.2 = f32[4,2,2,128,128]{4,3,2,1,0:T(8,128)S(1)} async-done(((f32[4,2,2,128,128]{4,3,2,1,0:T(8,128)}), f32[4,2,2,128,128]{4,3,2,1,0:T(8,128)S(1)}, u32[]{:S(2)}, u32[]{:S(2)}) %all-to-all-start.2) | async-done | bytes 1048608 | tf_op jit(solution)/shard_map/all_to_all | solution.py:134
  139.0 3.5 %all-to-all-start.3 = ((f32[4,2,2,128,128]{4,3,2,1,0:T(8,128)}), f32[4,2,2,128,128]{4,3,2,1,0:T(8,128)S(1)}, u32[]{:S(2)}, u32[]{:S(2)}) async-start(f32[4,2,2,128,128]{4,3,2,1,0:T(8,128)} %bitcast.8), calls=%async_computation.3 | async-start | bytes 2097152 | tf_op jit(solution)/shard_map/all_to_all | solution.py:134
  145.2 12.2 %all-to-all-done.3 = f32[4,2,2,128,128]{4,3,2,1,0:T(8,128)S(1)} async-done(((f32[4,2,2,128,128]{4,3,2,1,0:T(8,128)}), f32[4,2,2,128,128]{4,3,2,1,0:T(8,128)S(1)}, u32[]{:S(2)}, u32[]{:S(2)}) %all-to-all-start.3) | async-done | bytes 1048608 | tf_op jit(solution)/shard_map/all_to_all | solution.py:134
  (52 shorter events, 18.1 us)
Async XLA Ops:
  0.8 13.5 %copy-start.10 = (s32[128,2]{0,1:T(2,128)S(1)}, s32[128,2]{0,1:T(2,128)}, u32[]{:S(2)}) copy-start(s32[128,2]{0,1:T(2,128)} %param.6) | copy-start | bytes 3076
  4.4 34.4 %collective-permute-start = (bf16[2,2,4,64,512]{4,3,2,1,0:T(8,128)(2,1)}, bf16[2,2,4,64,512]{4,3,2,1,0:T(8,128)(2,1)}, u32[]{:S(2)}, u32[]{:S(2)}) collective-permute-start(bf16[2,2,4,64,512]{4,3,2,1,0:T(8,128)(2,1)} %get-tuple-element.23.here), channel_id=1, source_target_pairs={{0,8},{8,16},{16,24},{24,32},{32,40},{40,48},{48,56},{56,64},{64,7... | collective-permute-start | bytes 3145736 | tf_op jit(solution)/shard_map/ppermute | solution.py:18
  8.2 30.5 %collective-permute-start.1 = (bf16[2,2,4,64,512]{4,3,2,1,0:T(8,128)(2,1)}, bf16[2,2,4,64,512]{4,3,2,1,0:T(8,128)(2,1)}, u32[]{:S(2)}, u32[]{:S(2)}) collective-permute-start(bf16[2,2,4,64,512]{4,3,2,1,0:T(8,128)(2,1)} %get-tuple-element.23.here), channel_id=1, source_target_pairs={{8,0},{16,8},{24,16},{32,24},{40,32},{48,40},{56,48},{64,56},{72,6... | collective-permute-start | bytes 3145736 | tf_op jit(solution)/shard_map/ppermute | solution.py:18
  17.3 3.0 %copy-start = (bf16[2,8,4,320,128]{4,3,2,1,0:T(8,128)(2,1)}, bf16[2,8,4,320,128]{4,3,2,1,0:T(8,128)(2,1)S(1)}, u32[]{:S(2)}) copy-start(bf16[2,8,4,320,128]{4,3,2,1,0:T(8,128)(2,1)S(1)} %bitcast_select_fusion.own) | copy-start | bytes 15728644
  20.3 15.2 %collective-permute-start.2 = (bf16[2,2,4,128,128]{4,3,2,1,0:T(8,128)(2,1)}, bf16[2,2,4,128,128]{4,3,2,1,0:T(8,128)(2,1)}, u32[]{:S(2)}, u32[]{:S(2)}) collective-permute-start(bf16[2,2,4,128,128]{4,3,2,1,0:T(8,128)(2,1)} %get-tuple-element.27), channel_id=1, source_target_pairs={{0,4},{4,0},{1,5},{5,1},{2,6},{6,2},{3,7},{7,3},{8,12},{12,8},{9,1... | collective-permute-start | bytes 1572872 | tf_op jit(solution)/shard_map/ppermute | solution.py:24
  23.5 35.6 %collective-permute-start.4 = (bf16[2,2,4,64,512]{4,3,2,1,0:T(8,128)(2,1)S(1)}, bf16[2,2,4,64,512]{4,3,2,1,0:T(8,128)(2,1)}, u32[]{:S(2)}, u32[]{:S(2)}) collective-permute-start(bf16[2,2,4,64,512]{4,3,2,1,0:T(8,128)(2,1)S(1)} %get-tuple-element.24.here), channel_id=1, source_target_pairs={{0,8},{8,16},{16,24},{24,32},{32,40},{40,48},{48,56},{56,64},{64,7... | collective-permute-start | bytes 3145736 | tf_op jit(solution)/shard_map/ppermute | solution.py:18
  25.4 36.9 %collective-permute-start.5 = (bf16[2,2,4,64,512]{4,3,2,1,0:T(8,128)(2,1)S(1)}, bf16[2,2,4,64,512]{4,3,2,1,0:T(8,128)(2,1)}, u32[]{:S(2)}, u32[]{:S(2)}) collective-permute-start(bf16[2,2,4,64,512]{4,3,2,1,0:T(8,128)(2,1)S(1)} %get-tuple-element.24.here), channel_id=1, source_target_pairs={{8,0},{16,8},{24,16},{32,24},{40,32},{48,40},{56,48},{64,56},{72,6... | collective-permute-start | bytes 3145736 | tf_op jit(solution)/shard_map/ppermute | solution.py:18
  35.5 14.2 %collective-permute-start.6 = (bf16[2,2,4,128,128]{4,3,2,1,0:T(8,128)(2,1)}, bf16[2,2,4,128,128]{4,3,2,1,0:T(8,128)(2,1)S(1)}, u32[]{:S(2)}, u32[]{:S(2)}) collective-permute-start(bf16[2,2,4,128,128]{4,3,2,1,0:T(8,128)(2,1)} %get-tuple-element.28), channel_id=1, source_target_pairs={{0,4},{4,0},{1,5},{5,1},{2,6},{6,2},{3,7},{7,3},{8,12},{12,8},{9,1... | collective-permute-start | bytes 1572872 | tf_op jit(solution)/shard_map/ppermute | solution.py:24
  38.7 2.5 %copy-start.1 = (bf16[2,8,4,320,128]{4,3,2,1,0:T(8,128)(2,1)S(1)}, bf16[2,8,4,320,128]{4,3,2,1,0:T(8,128)(2,1)}, u32[]{:S(2)}) copy-start(bf16[2,8,4,320,128]{4,3,2,1,0:T(8,128)(2,1)} %copy-done) | copy-start | bytes 15728644
  44.9 22.7 %collective-permute-start.3 = (f32[2,2,2,2,128,128]{5,4,3,2,1,0:T(8,128)S(1)}, f32[2,2,2,2,128,128]{5,4,3,2,1,0:T(8,128)S(1)}, u32[]{:S(2)}, u32[]{:S(2)}) collective-permute-start(f32[2,2,2,2,128,128]{5,4,3,2,1,0:T(8,128)S(1)} %get-tuple-element.14), channel_id=1, source_target_pairs={{0,1},{1,0},{2,3},{3,2},{4,5},{5,4},{6,7},{7,6},{8,9},{9,8},{10,11... | collective-permute-start | bytes 3145736 | tf_op jit(solution)/shard_map/ppermute | solution.py:24
  45.0 36.3 %collective-permute-start.8 = (bf16[2,2,4,64,512]{4,3,2,1,0:T(8,128)(2,1)S(1)}, bf16[2,2,4,64,512]{4,3,2,1,0:T(8,128)(2,1)}, u32[]{:S(2)}, u32[]{:S(2)}) collective-permute-start(bf16[2,2,4,64,512]{4,3,2,1,0:T(8,128)(2,1)S(1)} %get-tuple-element.26.here), channel_id=1, source_target_pairs={{0,8},{8,16},{16,24},{24,32},{32,40},{40,48},{48,56},{56,64},{64,7... | collective-permute-start | bytes 3145736 | tf_op jit(solution)/shard_map/ppermute | solution.py:18
  49.7 32.6 %collective-permute-start.9 = (bf16[2,2,4,64,512]{4,3,2,1,0:T(8,128)(2,1)S(1)}, bf16[2,2,4,64,512]{4,3,2,1,0:T(8,128)(2,1)}, u32[]{:S(2)}, u32[]{:S(2)}) collective-permute-start(bf16[2,2,4,64,512]{4,3,2,1,0:T(8,128)(2,1)S(1)} %get-tuple-element.26.here), channel_id=1, source_target_pairs={{8,0},{16,8},{24,16},{32,24},{40,32},{48,40},{56,48},{64,56},{72,6... | collective-permute-start | bytes 3145736 | tf_op jit(solution)/shard_map/ppermute | solution.py:18
  59.1 15.8 %collective-permute-start.10 = (bf16[2,2,4,128,128]{4,3,2,1,0:T(8,128)(2,1)}, bf16[2,2,4,128,128]{4,3,2,1,0:T(8,128)(2,1)}, u32[]{:S(2)}, u32[]{:S(2)}) collective-permute-start(bf16[2,2,4,128,128]{4,3,2,1,0:T(8,128)(2,1)} %get-tuple-element.30), channel_id=1, source_target_pairs={{0,4},{4,0},{1,5},{5,1},{2,6},{6,2},{3,7},{7,3},{8,12},{12,8},{9,1... | collective-permute-start | bytes 1572872 | tf_op jit(solution)/shard_map/ppermute | solution.py:24
  66.6 1.0 copy-start.4
  67.6 25.7 %collective-permute-start.7 = (f32[2,2,2,2,128,128]{5,4,3,2,1,0:T(8,128)}, f32[2,2,2,2,128,128]{5,4,3,2,1,0:T(8,128)}, u32[]{:S(2)}, u32[]{:S(2)}) collective-permute-start(f32[2,2,2,2,128,128]{5,4,3,2,1,0:T(8,128)} %get-tuple-element.16), channel_id=1, source_target_pairs={{0,1},{1,0},{2,3},{3,2},{4,5},{5,4},{6,7},{7,6},{8,9},{9,8},{10,11... | collective-permute-start | bytes 3145736 | tf_op jit(solution)/shard_map/ppermute | solution.py:24
  68.7 27.2 %all-to-all-start = ((f32[4,2,2,128,128]{4,3,2,1,0:T(8,128)}), f32[4,2,2,128,128]{4,3,2,1,0:T(8,128)}, u32[]{:S(2)}, u32[]{:S(2)}) async-start(f32[4,2,2,128,128]{4,3,2,1,0:T(8,128)} %bitcast.5), calls=%async_computation | async-start | bytes 2097152 | tf_op jit(solution)/shard_map/all_to_all | solution.py:134
  73.0 34.4 %collective-permute-start.12 = (bf16[2,2,4,64,512]{4,3,2,1,0:T(8,128)(2,1)S(1)}, bf16[2,2,4,64,512]{4,3,2,1,0:T(8,128)(2,1)S(1)}, u32[]{:S(2)}, u32[]{:S(2)}) collective-permute-start(bf16[2,2,4,64,512]{4,3,2,1,0:T(8,128)(2,1)S(1)} %get-tuple-element.25.here), channel_id=1, source_target_pairs={{0,8},{8,16},{16,24},{24,32},{32,40},{40,48},{48,56},{56,64},{64,7... | collective-permute-start | bytes 3145736 | tf_op jit(solution)/shard_map/ppermute | solution.py:18
  74.9 32.4 %collective-permute-start.13 = (bf16[2,2,4,64,512]{4,3,2,1,0:T(8,128)(2,1)S(1)}, bf16[2,2,4,64,512]{4,3,2,1,0:T(8,128)(2,1)}, u32[]{:S(2)}, u32[]{:S(2)}) collective-permute-start(bf16[2,2,4,64,512]{4,3,2,1,0:T(8,128)(2,1)S(1)} %get-tuple-element.25.here), channel_id=1, source_target_pairs={{8,0},{16,8},{24,16},{32,24},{40,32},{48,40},{56,48},{64,56},{72,6... | collective-permute-start | bytes 3145736 | tf_op jit(solution)/shard_map/ppermute | solution.py:18
  82.4 2.5 %copy-start.2 = (bf16[2,8,4,320,128]{4,3,2,1,0:T(8,128)(2,1)S(1)}, bf16[2,8,4,320,128]{4,3,2,1,0:T(8,128)(2,1)}, u32[]{:S(2)}) copy-start(bf16[2,8,4,320,128]{4,3,2,1,0:T(8,128)(2,1)} %copy-done) | copy-start | bytes 15728644
  89.1 1.0 copy-start.5
  90.1 25.9 %collective-permute-start.11 = (f32[2,2,2,2,128,128]{5,4,3,2,1,0:T(8,128)}, f32[2,2,2,2,128,128]{5,4,3,2,1,0:T(8,128)}, u32[]{:S(2)}, u32[]{:S(2)}) collective-permute-start(f32[2,2,2,2,128,128]{5,4,3,2,1,0:T(8,128)} %get-tuple-element.18), channel_id=1, source_target_pairs={{0,1},{1,0},{2,3},{3,2},{4,5},{5,4},{6,7},{7,6},{8,9},{9,8},{10,11... | collective-permute-start | bytes 3145736 | tf_op jit(solution)/shard_map/ppermute | solution.py:24
  90.1 16.4 %collective-permute-start.14 = (bf16[2,2,4,128,128]{4,3,2,1,0:T(8,128)(2,1)}, bf16[2,2,4,128,128]{4,3,2,1,0:T(8,128)(2,1)S(1)}, u32[]{:S(2)}, u32[]{:S(2)}) collective-permute-start(bf16[2,2,4,128,128]{4,3,2,1,0:T(8,128)(2,1)} %get-tuple-element.29), channel_id=1, source_target_pairs={{0,4},{4,0},{1,5},{5,1},{2,6},{6,2},{3,7},{7,3},{8,12},{12,8},{9,1... | collective-permute-start | bytes 1572872 | tf_op jit(solution)/shard_map/ppermute | solution.py:24
  96.0 22.8 %all-to-all-start.1 = ((f32[4,2,2,128,128]{4,3,2,1,0:T(8,128)}), f32[4,2,2,128,128]{4,3,2,1,0:T(8,128)}, u32[]{:S(2)}, u32[]{:S(2)}) async-start(f32[4,2,2,128,128]{4,3,2,1,0:T(8,128)} %bitcast.12), calls=%async_computation.1 | async-start | bytes 2097152 | tf_op jit(solution)/shard_map/all_to_all | solution.py:134
  106.6 0.8 copy-start.8
  107.4 2.5 %copy-start.3 = (bf16[2,8,4,320,128]{4,3,2,1,0:T(8,128)(2,1)S(1)}, bf16[2,8,4,320,128]{4,3,2,1,0:T(8,128)(2,1)}, u32[]{:S(2)}) copy-start(bf16[2,8,4,320,128]{4,3,2,1,0:T(8,128)(2,1)} %copy-done) | copy-start | bytes 15728644
  109.9 1.0 copy-start.9
  115.0 1.0 copy-start.6
  116.1 7.3 %copy-start.7 = (f32[2,2,2,2,128,128]{5,4,3,2,1,0:T(8,128)S(1)}, f32[2,2,2,2,128,128]{5,4,3,2,1,0:T(8,128)}, u32[]{:S(2)}) copy-start(f32[2,2,2,2,128,128]{5,4,3,2,1,0:T(8,128)} %copy-done.6) | copy-start | bytes 3145732
  116.1 7.3 %collective-permute-start.15 = (f32[2,2,2,2,128,128]{5,4,3,2,1,0:T(8,128)}, f32[2,2,2,2,128,128]{5,4,3,2,1,0:T(8,128)S(1)}, u32[]{:S(2)}, u32[]{:S(2)}) collective-permute-start(f32[2,2,2,2,128,128]{5,4,3,2,1,0:T(8,128)} %get-tuple-element.20), channel_id=1, source_target_pairs={{0,1},{1,0},{2,3},{3,2},{4,5},{5,4},{6,7},{7,6},{8,9},{9,8},{10,11... | collective-permute-start | bytes 3145736 | tf_op jit(solution)/shard_map/ppermute | solution.py:24
  118.8 20.2 %all-to-all-start.2 = ((f32[4,2,2,128,128]{4,3,2,1,0:T(8,128)}), f32[4,2,2,128,128]{4,3,2,1,0:T(8,128)S(1)}, u32[]{:S(2)}, u32[]{:S(2)}) async-start(f32[4,2,2,128,128]{4,3,2,1,0:T(8,128)} %bitcast.7), calls=%async_computation.2 | async-start | bytes 2097152 | tf_op jit(solution)/shard_map/all_to_all | solution.py:134
  139.0 18.3 %all-to-all-start.3 = ((f32[4,2,2,128,128]{4,3,2,1,0:T(8,128)}), f32[4,2,2,128,128]{4,3,2,1,0:T(8,128)S(1)}, u32[]{:S(2)}, u32[]{:S(2)}) async-start(f32[4,2,2,128,128]{4,3,2,1,0:T(8,128)} %bitcast.8), calls=%async_computation.3 | async-start | bytes 2097152 | tf_op jit(solution)/shard_map/all_to_all | solution.py:134

commit v2 on v1

--- a/solution.py
+++ b/solution.py
@@ -7,7 +7,7 @@
 from jax.experimental.pallas import tpu as pltpu
 from jax.sharding import Mesh, PartitionSpec as P
 
-CHUNKS = (2, 2, 2, 2)
+CHUNKS = (2, 2, 2, 1, 1)
 SHOT = ("sup", "half")
 XLINE = ("side", "core")
 RING = ("half", "side")
@@ -36,7 +36,7 @@
 
     lefts = []
     for part in range(2):
-        mine = [flat(own[part, 0, :, 2 * k * pts : (2 * k + 1) * pts, :]) for k in range(3)]
+        mine = [flat(own[part, 0, :, k * pts : (k + 1) * pts, :]) for k in range(3)]
         low, high = (flat(cross[part, 0, :, k * pts : (k + 1) * pts, :]) for k in range(2))
         none = jnp.zeros_like(low)
         theirs = [
@@ -70,12 +70,12 @@
                 send[to, side, part, 0] = leaves[first : first + shots]
 
 
-def products(place, below, here, above, own, cross, first):
+def products(place, below, here, above, own, cross):
     freqs, xs, pts, recv = here.shape[1:]
-    spread, shots = own.shape[3:]
+    shots = own.shape[4]
 
-    def of_freq(shape, offset=0):
-        return pl.BlockSpec((2, 1) + shape, lambda f: (0, f + offset, 0, 0, 0))
+    def of_freq(shape):
+        return pl.BlockSpec((2, 1) + shape, lambda f: (0, f, 0, 0, 0))
 
     window = of_freq((xs, pts, recv))
     out = jax.ShapeDtypeStruct((2, 2, 2, freqs, shots, recv // 4), jnp.float32)
@@ -89,7 +89,7 @@
             window,
             window,
             window,
-            of_freq((xs, spread, shots), first),
+            of_freq((xs, 3 * pts, shots)),
             of_freq((xs, 2 * pts, shots)),
         ],
         out_specs=[out_spec, out_spec],
@@ -107,33 +107,66 @@
     half, core = lax.axis_index("half"), lax.axis_index("core")
     place = jnp.stack([half, core]).astype(jnp.int32)
     heard = lax.broadcasted_iota(jnp.int32, surface_gathers.shape[2:], 2) < live[:, :, None]
-    chunks = [(sum(CHUNKS[:i]), size) for i, size in enumerate(CHUNKS)]
-
-    here, below, above = [], [], []
-    for first, size in chunks:
-        gathers = surface_gathers[:, first : first + size]
-        here.append(jnp.where(heard, gathers, jnp.zeros((), gathers.dtype)))
-        below.append(shifted(here[-1], 1))
-        above.append(shifted(here[-1], -1))
-
     first_point = (2 * lax.axis_index("sup") + half) * pts - (spread - pts) // 2
     inline = first_point + lax.broadcasted_iota(jnp.int32, (spread, aperture.shape[0]), 0)
     inside = (inline >= aperture[:, 0][None, :]) & (inline < aperture[:, 1][None, :])
+    chunks = [(sum(CHUNKS[:i]), sum(CHUNKS[: i + 1])) for i in range(len(CHUNKS))]
+
+    def muted(gathers, i):
+        gathers = gathers[:, slice(*chunks[i])]
+        return jnp.where(heard, gathers, jnp.zeros((), gathers.dtype))
+
+    def pieces(shots, i, which):
+        spans = [slice(k * pts, (k + 1) * pts) for k in which]
+        shots = shots[:, slice(*chunks[i])]
+        return jnp.concatenate(
+            [
+                jnp.where(inside[span], shots[:, :, :, span], jnp.zeros((), shots.dtype))
+                for span in spans
+            ],
+            axis=3,
+        )
+
     shots = source_gathers.transpose(0, 1, 3, 4, 2)
-    masked = jnp.where(inside, shots, jnp.zeros((), shots.dtype))
-    crossing = jnp.concatenate(
-        [masked[:, :, :, pts : 2 * pts], masked[:, :, :, 3 * pts : 4 * pts]], axis=3
+    count = len(chunks)
+    here, own, leaving = [None] * count, [None] * count, [None] * count
+    below, above, cross = [None] * count, [None] * count, [None] * count
+
+    def travel(i):
+        below[i], above[i] = shifted(here[i], 1), shifted(here[i], -1)
+        cross[i] = swapped(leaving[i], "half")
+
+    here[0] = muted(surface_gathers, 0)
+    here[0], shots, surface_gathers = lax.optimization_barrier(
+        (here[0], shots, surface_gathers)
     )
-    cross = [swapped(crossing[:, first : first + size], "half") for first, size in chunks]
+    leaving[0] = pieces(shots, 0, (1, 3))
+    travel(0)
+    leaving[0], shots, surface_gathers = lax.optimization_barrier(
+        (leaving[0], shots, surface_gathers)
+    )
+    for i in range(count):
+        own[i] = pieces(shots, i, (0, 2, 4))
+        if i:
+            here[i] = muted(surface_gathers, i)
+            leaving[i] = pieces(shots, i, (1, 3))
+    travel(1)
 
     predicted = []
-    for i, (first, size) in enumerate(chunks):
-        keep, send = products(place, below[i], here[i], above[i], masked, cross[i], first)
+    for i in range(count):
+        keep, send = products(place, below[i], here[i], above[i], own[i], cross[i])
         partial = keep + swapped(send, "core")
+        if i + 2 < count:
+            partial, own[i + 1], here[i + 2], leaving[i + 2] = lax.optimization_barrier(
+                (partial, own[i + 1], here[i + 2], leaving[i + 2])
+            )
+            travel(i + 2)
+        elif i + 1 < count:
+            partial, own[i + 1] = lax.optimization_barrier((partial, own[i + 1]))
         partial = partial.reshape((4,) + partial.shape[2:])
         terms = lax.all_to_all(partial, RING, 0, 0, tiled=True)
-        predicted.append(terms.sum(axis=0).astype(jnp.bfloat16))
-    return jnp.concatenate(predicted, axis=1)
+        predicted.append((terms[0] + terms[1]) + (terms[2] + terms[3]))
+    return jnp.concatenate([sums.astype(jnp.bfloat16) for sums in predicted], axis=1)
 
 
 def solution(mesh):

time: 160 us -> 191 us (1.19)
  starting transfers between devices: 60.5 us -> 84.9 us
  waiting for transfers between devices: 47.3 us -> 61.4 us
  local copies, waits for them, and re-layouts: 13.6 us -> 1.27 us
  other arithmetic: 20.3 us -> 26.7 us
    ppermute x8 -> x10, waiting for transfers between devices: 13.1 us -> 27.1 us  [swapped(): return lax.ppermute(block, axis, [(0, 1), (1, 0)])]
    unnamed x22 -> x34, local copies, waits for them, and re-layouts: 13.4 us -> 0.66 us
    ppermute x8 -> x10, starting transfers between devices: 31.1 us -> 43.8 us  [shifted(): lax.ppermute(block, 'sup', [(i, i + distance) for i in range(n) if 0 <= i...]
    ppermute x8 -> x10, waiting for transfers between devices: 7.47 us -> 19.2 us  [shifted(): lax.ppermute(block, 'sup', [(i, i + distance) for i in range(n) if 0 <= i...]
    all_to_all x4 -> x5, waiting for transfers between devices: 26.8 us -> 15.1 us  [on_device(): terms = lax.all_to_all(partial, RING, 0, 0, tiled=True)]
    all_to_all x4 -> x5, starting transfers between devices: 16.5 us -> 23.7 us  [on_device(): terms = lax.all_to_all(partial, RING, 0, 0, tiled=True)]
    ppermute x8 -> x10, starting transfers between devices: 12.9 us -> 17.4 us  [swapped(): return lax.ppermute(block, axis, [(0, 1), (1, 0)])]
    unnamed x0 -> x4, other arithmetic: none -> 3.78 us
  transfers between devices with their start and end apart: 20 -> 25, of which waited for: 8 -> 15; matrix products, arithmetic and copies ran while one was open for 10% -> 13% of each run, Pallas kernels for 10% -> 4%
where the time goes in v2:
time: 191 us; the launch traced here: 190 us
  starting transfers between devices  84.9 us (44%)
  waiting for transfers between devices  61.4 us (32%)
  other arithmetic  26.7 us (14%)
  Pallas kernels  15.1 us (8%)
    ppermute x10, starting transfers between devices, shifted(): lax.ppermute(block, 'sup', [(i, i + distance) for i in range(n) if 0 <= i...  43.8 us
    ppermute x10, waiting for transfers between devices, swapped(): return lax.ppermute(block, axis, [(0, 1), (1, 0)])  27.1 us
    all_to_all x5, starting transfers between devices, on_device(): terms = lax.all_to_all(partial, RING, 0, 0, tiled=True)  23.7 us
    ppermute x10, waiting for transfers between devices, shifted(): lax.ppermute(block, 'sup', [(i, i + distance) for i in range(n) if 0 <= i...  19.2 us
    ppermute x10, starting transfers between devices, swapped(): return lax.ppermute(block, axis, [(0, 1), (1, 0)])  17.4 us
    all_to_all x5, waiting for transfers between devices, on_device(): terms = lax.all_to_all(partial, RING, 0, 0, tiled=True)  15.1 us
    pallas_call x5, Pallas kernels, products(): pl.pallas_call(products_kernel, grid=(freqs,), in_specs=[pl.BlockSpec(mem...  15.1 us
    add x5, other arithmetic, on_device(): partial = keep + swapped(send, 'core')  7.57 us
  transfers between devices with their start and end apart: 25, of which 15 were waited for; matrix products, arithmetic and copies ran while one was open for 13% of the time, Pallas kernels for 4%

profile of v2, /device:TPU:6, one launch (start us, length us, event | category | flops | bytes accessed | tf_op | source)
XLA Modules:
  0.0 189.9 jit_solution(6581728237768699245)
XLA Ops:
  2.2 3.8 %collective-permute-start = (bf16[2,2,4,64,512]{4,3,2,1,0:T(8,128)(2,1)S(1)}, bf16[2,2,4,64,512]{4,3,2,1,0:T(8,128)(2,1)S(1)}, u32[]{:S(2)}, u32[]{:S(2)}) collective-permute-start(bf16[2,2,4,64,512]{4,3,2,1,0:T(8,128)(2,1)S(1)} %slice_select_fusion.2.here), channel_id=1, source_target_pairs={{0,8},{8,16},{16,24},{24,32},{32,40},{40,48},{48,56},{56,64},{64,7... | collective-permute-start | bytes 3145736 | tf_op jit(solution)/shard_map/ppermute | solution.py:18
  6.0 6.1 %collective-permute-start.1 = (bf16[2,2,4,64,512]{4,3,2,1,0:T(8,128)(2,1)S(1)}, bf16[2,2,4,64,512]{4,3,2,1,0:T(8,128)(2,1)S(1)}, u32[]{:S(2)}, u32[]{:S(2)}) collective-permute-start(bf16[2,2,4,64,512]{4,3,2,1,0:T(8,128)(2,1)S(1)} %slice_select_fusion.2.here), channel_id=1, source_target_pairs={{8,0},{16,8},{24,16},{32,24},{40,32},{48,40},{56,48},{64,56},{72,6... | collective-permute-start | bytes 3145736 | tf_op jit(solution)/shard_map/ppermute | solution.py:18
  15.4 3.2 %collective-permute-start.2 = (bf16[2,2,4,128,128]{4,3,2,1,0:T(8,128)(2,1)}, bf16[2,2,4,128,128]{4,3,2,1,0:T(8,128)(2,1)}, u32[]{:S(2)}, u32[]{:S(2)}) collective-permute-start(bf16[2,2,4,128,128]{4,3,2,1,0:T(8,128)(2,1)} %pad_maximum_fusion.3), channel_id=1, source_target_pairs={{0,4},{4,0},{1,5},{5,1},{2,6},{6,2},{3,7},{7,3},{8,12},{12,8},{9,1... | collective-permute-start | bytes 1572872 | tf_op jit(solution)/shard_map/ppermute | solution.py:24
  21.0 9.6 %collective-permute-done.2.cross = bf16[2,2,4,128,128]{4,3,2,1,0:T(8,128)(2,1)} collective-permute-done((bf16[2,2,4,128,128]{4,3,2,1,0:T(8,128)(2,1)}, bf16[2,2,4,128,128]{4,3,2,1,0:T(8,128)(2,1)}, u32[]{:S(2)}, u32[]{:S(2)}) %collective-permute-start.2) | collective-permute-done | bytes 524320 | tf_op jit(solution)/shard_map/ppermute | solution.py:24
  30.6 2.7 %collective-permute-done.below = bf16[2,2,4,64,512]{4,3,2,1,0:T(8,128)(2,1)S(1)} collective-permute-done((bf16[2,2,4,64,512]{4,3,2,1,0:T(8,128)(2,1)S(1)}, bf16[2,2,4,64,512]{4,3,2,1,0:T(8,128)(2,1)S(1)}, u32[]{:S(2)}, u32[]{:S(2)}) %collective-permute-start) | collective-permute-done | bytes 1048608 | tf_op jit(solution)/shard_map/ppermute | solution.py:18
  34.6 3.4 %shard_map.46 = (f32[2,2,2,2,128,128]{5,4,3,2,1,0:T(8,128)S(1)}, f32[2,2,2,2,128,128]{5,4,3,2,1,0:T(8,128)S(1)}) custom-call(s32[2]{0:T(128)S(1)} %pad_add_fusion.place, bf16[2,2,4,64,512]{4,3,2,1,0:T(8,128)(2,1)S(1)} %collective-permute-done.below, bf16[2,2,4,64,512]{4,3,2,1,0:T(8,128)(2,1)S(1)} %slice_select_fusion.2.here, ...), custom_call_target="tpu_custom_call" | custom-call | flops 1610612736 | bytes 8388608 | tf_op jit(solution)/shard_map/pallas_call | solution.py:84
  40.3 6.4 %collective-permute-start.5 = (bf16[2,2,4,64,512]{4,3,2,1,0:T(8,128)(2,1)S(1)}, bf16[2,2,4,64,512]{4,3,2,1,0:T(8,128)(2,1)S(1)}, u32[]{:S(2)}, u32[]{:S(2)}) collective-permute-start(bf16[2,2,4,64,512]{4,3,2,1,0:T(8,128)(2,1)S(1)} %get-tuple-element.108.here), channel_id=1, source_target_pairs={{8,0},{16,8},{24,16},{32,24},{40,32},{48,40},{56,48},{64,56},{72,6... | collective-permute-start | bytes 3145736 | tf_op jit(solution)/shard_map/ppermute | solution.py:18
  46.7 3.3 %collective-permute-start.6 = (bf16[2,2,4,128,128]{4,3,2,1,0:T(8,128)(2,1)S(1)}, bf16[2,2,4,128,128]{4,3,2,1,0:T(8,128)(2,1)S(1)}, u32[]{:S(2)}, u32[]{:S(2)}) collective-permute-start(bf16[2,2,4,128,128]{4,3,2,1,0:T(8,128)(2,1)S(1)} %pad_maximum_fusion.5), channel_id=1, source_target_pairs={{0,4},{4,0},{1,5},{5,1},{2,6},{6,2},{3,7},{7,3},{8,12},{12,8},{9,1... | collective-permute-start | bytes 1572872 | tf_op jit(solution)/shard_map/ppermute | solution.py:24
  52.0 10.3 %collective-permute-done.6.cross = bf16[2,2,4,128,128]{4,3,2,1,0:T(8,128)(2,1)S(1)} collective-permute-done((bf16[2,2,4,128,128]{4,3,2,1,0:T(8,128)(2,1)S(1)}, bf16[2,2,4,128,128]{4,3,2,1,0:T(8,128)(2,1)S(1)}, u32[]{:S(2)}, u32[]{:S(2)}) %collective-permute-start.6) | collective-permute-done | bytes 524320 | tf_op jit(solution)/shard_map/ppermute | solution.py:24
  62.4 6.2 %collective-permute-done.4.below = bf16[2,2,4,64,512]{4,3,2,1,0:T(8,128)(2,1)S(1)} collective-permute-done((bf16[2,2,4,64,512]{4,3,2,1,0:T(8,128)(2,1)S(1)}, bf16[2,2,4,64,512]{4,3,2,1,0:T(8,128)(2,1)S(1)}, u32[]{:S(2)}, u32[]{:S(2)}) %collective-permute-start.4) | collective-permute-done | bytes 1048608 | tf_op jit(solution)/shard_map/ppermute | solution.py:18
  69.7 3.7 %shard_map.47 = (f32[2,2,2,2,128,128]{5,4,3,2,1,0:T(8,128)S(1)}, f32[2,2,2,2,128,128]{5,4,3,2,1,0:T(8,128)}) custom-call(s32[2]{0:T(128)S(1)} %pad_add_fusion.place, bf16[2,2,4,64,512]{4,3,2,1,0:T(8,128)(2,1)S(1)} %collective-permute-done.4.below, bf16[2,2,4,64,512]{4,3,2,1,0:T(8,128)(2,1)S(1)} %get-tuple-element.108.here, ...), custom_call_target="tpu_custom_call" | custom-call | flops 1610612736 | bytes 8388608 | tf_op jit(solution)/shard_map/pallas_call | solution.py:84
  73.5 3.9 %collective-permute-start.8 = (bf16[2,2,4,64,512]{4,3,2,1,0:T(8,128)(2,1)S(1)}, bf16[2,2,4,64,512]{4,3,2,1,0:T(8,128)(2,1)}, u32[]{:S(2)}, u32[]{:S(2)}) collective-permute-start(bf16[2,2,4,64,512]{4,3,2,1,0:T(8,128)(2,1)S(1)} %get-tuple-element.46.here), channel_id=1, source_target_pairs={{0,8},{8,16},{16,24},{24,32},{32,40},{40,48},{48,56},{56,64},{64,7... | collective-permute-start | bytes 3145736 | tf_op jit(solution)/shard_map/ppermute | solution.py:18
  77.4 4.5 %collective-permute-start.9 = (bf16[2,2,4,64,512]{4,3,2,1,0:T(8,128)(2,1)S(1)}, bf16[2,2,4,64,512]{4,3,2,1,0:T(8,128)(2,1)}, u32[]{:S(2)}, u32[]{:S(2)}) collective-permute-start(bf16[2,2,4,64,512]{4,3,2,1,0:T(8,128)(2,1)S(1)} %get-tuple-element.46.here), channel_id=1, source_target_pairs={{8,0},{16,8},{24,16},{32,24},{40,32},{48,40},{56,48},{64,56},{72,6... | collective-permute-start | bytes 3145736 | tf_op jit(solution)/shard_map/ppermute | solution.py:18
  81.9 3.3 %collective-permute-start.10 = (bf16[2,2,4,128,128]{4,3,2,1,0:T(8,128)(2,1)}, bf16[2,2,4,128,128]{4,3,2,1,0:T(8,128)(2,1)}, u32[]{:S(2)}, u32[]{:S(2)}) collective-permute-start(bf16[2,2,4,128,128]{4,3,2,1,0:T(8,128)(2,1)} %pad_maximum_fusion.4), channel_id=1, source_target_pairs={{0,4},{4,0},{1,5},{5,1},{2,6},{6,2},{3,7},{7,3},{8,12},{12,8},{9,1... | collective-permute-start | bytes 1572872 | tf_op jit(solution)/shard_map/ppermute | solution.py:24
  85.2 2.4 %slice_select_fusion.22 = (bf16[2,1,4,64,128]{4,3,2,1,0:T(8,128)(2,1)}, bf16[2,1,4,64,128]{4,3,2,1,0:T(8,128)(2,1)}, bf16[2,1,4,64,128]{4,3,2,1,0:T(8,128)(2,1)}...) fusion(bf16[2,8,4,320,128]{4,3,2,1,0:T(8,128)(2,1)} %bitcast.38, ...), kind=kLoop, calls=%fused_computation.60 | loop fusion | flops 655360 | bytes 2662400 | tf_op jit(solution)/shard_map/jit(_where)/select_n | solution.py:124
  87.7 4.2 %all-to-all-start = ((f32[4,2,2,128,128]{4,3,2,1,0:T(8,128)}), f32[4,2,2,128,128]{4,3,2,1,0:T(8,128)}, u32[]{:S(2)}, u32[]{:S(2)}) async-start(f32[4,2,2,128,128]{4,3,2,1,0:T(8,128)} %bitcast.39), calls=%async_computation | async-start | bytes 2097152 | tf_op jit(solution)/shard_map/all_to_all | solution.py:167
  94.8 2.4 %add.141 = f32[2,2,2,2,128,128]{5,4,3,2,1,0:T(8,128)} add(f32[2,2,2,2,128,128]{5,4,3,2,1,0:T(8,128)S(1)} %get-tuple-element.43, f32[2,2,2,2,128,128]{5,4,3,2,1,0:T(8,128)} %collective-permute-done.7) | non-fusion elementwise | flops 262144 | bytes 3145728 | tf_op jit(solution)/shard_map/add | solution.py:158
  98.6 5.3 %collective-permute-done.8.below = bf16[2,2,4,64,512]{4,3,2,1,0:T(8,128)(2,1)} collective-permute-done((bf16[2,2,4,64,512]{4,3,2,1,0:T(8,128)(2,1)S(1)}, bf16[2,2,4,64,512]{4,3,2,1,0:T(8,128)(2,1)}, u32[]{:S(2)}, u32[]{:S(2)}) %collective-permute-start.8) | collective-permute-done | bytes 1048608 | tf_op jit(solution)/shard_map/ppermute | solution.py:18
  105.0 4.3 %shard_map.48 = (f32[2,2,2,2,128,128]{5,4,3,2,1,0:T(8,128)S(1)}, f32[2,2,2,2,128,128]{5,4,3,2,1,0:T(8,128)}) custom-call(s32[2]{0:T(128)S(1)} %pad_add_fusion.place, bf16[2,2,4,64,512]{4,3,2,1,0:T(8,128)(2,1)} %collective-permute-done.8.below, bf16[2,2,4,64,512]{4,3,2,1,0:T(8,128)(2,1)S(1)} %get-tuple-element.46.here, ...), custom_call_target="tpu_custom_call" | custom-call | flops 1610612736 | bytes 8388608 | tf_op jit(solution)/shard_map/pallas_call | solution.py:84
  109.4 4.6 %all-to-all-start.1 = ((f32[4,2,2,128,128]{4,3,2,1,0:T(8,128)}), f32[4,2,2,128,128]{4,3,2,1,0:T(8,128)}, u32[]{:S(2)}, u32[]{:S(2)}) async-start(f32[4,2,2,128,128]{4,3,2,1,0:T(8,128)} %bitcast.41), calls=%async_computation.1 | async-start | bytes 2097152 | tf_op jit(solution)/shard_map/all_to_all | solution.py:167
  114.0 3.4 %collective-permute-start.12 = (bf16[2,1,4,64,512]{4,3,2,1,0:T(8,128)(2,1)S(1)}, bf16[2,1,4,64,512]{4,3,2,1,0:T(8,128)(2,1)S(1)}, u32[]{:S(2)}, u32[]{:S(2)}) collective-permute-start(bf16[2,1,4,64,512]{4,3,2,1,0:T(8,128)(2,1)S(1)} %copy-done), channel_id=1, source_target_pairs={{0,8},{8,16},{16,24},{24,32},{32,40},{40,48},{48,56},{56,64},{64,7... | collective-permute-start | bytes 1572872 | tf_op jit(solution)/shard_map/ppermute | solution.py:18
  117.3 5.2 %collective-permute-start.13 = (bf16[2,1,4,64,512]{4,3,2,1,0:T(8,128)(2,1)S(1)}, bf16[2,1,4,64,512]{4,3,2,1,0:T(8,128)(2,1)}, u32[]{:S(2)}, u32[]{:S(2)}) collective-permute-start(bf16[2,1,4,64,512]{4,3,2,1,0:T(8,128)(2,1)S(1)} %copy-done), channel_id=1, source_target_pairs={{8,0},{16,8},{24,16},{32,24},{40,32},{48,40},{56,48},{64,56},{72,6... | collective-permute-start | bytes 1572872 | tf_op jit(solution)/shard_map/ppermute | solution.py:18
  122.5 3.6 %collective-permute-start.14 = (bf16[2,1,4,128,128]{4,3,2,1,0:T(8,128)(2,1)}, bf16[2,1,4,128,128]{4,3,2,1,0:T(8,128)(2,1)S(1)}, u32[]{:S(2)}, u32[]{:S(2)}) collective-permute-start(bf16[2,1,4,128,128]{4,3,2,1,0:T(8,128)(2,1)} %pad_maximum_fusion.8), channel_id=1, source_target_pairs={{0,4},{4,0},{1,5},{5,1},{2,6},{6,2},{3,7},{7,3},{8,12},{12,8},{9,1... | collective-permute-start | bytes 786440 | tf_op jit(solution)/shard_map/ppermute | solution.py:24
  130.6 6.6 %all-to-all-start.2 = ((f32[4,2,2,128,128]{4,3,2,1,0:T(8,128)}), f32[4,2,2,128,128]{4,3,2,1,0:T(8,128)}, u32[]{:S(2)}, u32[]{:S(2)}) async-start(f32[4,2,2,128,128]{4,3,2,1,0:T(8,128)} %bitcast.40), calls=%async_computation.2 | async-start | bytes 2097152 | tf_op jit(solution)/shard_map/all_to_all | solution.py:167
  139.5 3.4 %collective-permute-start.16 = (bf16[2,1,4,64,512]{4,3,2,1,0:T(8,128)(2,1)S(1)}, bf16[2,1,4,64,512]{4,3,2,1,0:T(8,128)(2,1)S(1)}, u32[]{:S(2)}, u32[]{:S(2)}) collective-permute-start(bf16[2,1,4,64,512]{4,3,2,1,0:T(8,128)(2,1)S(1)} %get-tuple-element.58.here), channel_id=1, source_target_pairs={{0,8},{8,16},{16,24},{24,32},{32,40},{40,48},{48,56},{56,64},{64,7... | collective-permute-start | bytes 1572872 | tf_op jit(solution)/shard_map/ppermute | solution.py:18
  142.9 5.2 %collective-permute-start.17 = (bf16[2,1,4,64,512]{4,3,2,1,0:T(8,128)(2,1)S(1)}, bf16[2,1,4,64,512]{4,3,2,1,0:T(8,128)(2,1)S(1)}, u32[]{:S(2)}, u32[]{:S(2)}) collective-permute-start(bf16[2,1,4,64,512]{4,3,2,1,0:T(8,128)(2,1)S(1)} %get-tuple-element.58.here), channel_id=1, source_target_pairs={{8,0},{16,8},{24,16},{32,24},{40,32},{48,40},{56,48},{64,56},{72,6... | collective-permute-start | bytes 1572872 | tf_op jit(solution)/shard_map/ppermute | solution.py:18
  148.0 3.6 %collective-permute-start.18 = (bf16[2,1,4,128,128]{4,3,2,1,0:T(8,128)(2,1)S(1)}, bf16[2,1,4,128,128]{4,3,2,1,0:T(8,128)(2,1)S(1)}, u32[]{:S(2)}, u32[]{:S(2)}) collective-permute-start(bf16[2,1,4,128,128]{4,3,2,1,0:T(8,128)(2,1)S(1)} %copy-done.9), channel_id=1, source_target_pairs={{0,4},{4,0},{1,5},{5,1},{2,6},{6,2},{3,7},{7,3},{8,12},{12,8},{9,1... | collective-permute-start | bytes 786440 | tf_op jit(solution)/shard_map/ppermute | solution.py:24
  152.5 5.8 %collective-permute-done.18.cross = bf16[2,1,4,128,128]{4,3,2,1,0:T(8,128)(2,1)S(1)} collective-permute-done((bf16[2,1,4,128,128]{4,3,2,1,0:T(8,128)(2,1)S(1)}, bf16[2,1,4,128,128]{4,3,2,1,0:T(8,128)(2,1)S(1)}, u32[]{:S(2)}, u32[]{:S(2)}) %collective-permute-start.18) | collective-permute-done | bytes 262176 | tf_op jit(solution)/shard_map/ppermute | solution.py:24
  161.5 4.8 %all-to-all-start.3 = ((f32[4,2,1,128,128]{4,3,1,2,0:T(8,128)}), f32[4,2,1,128,128]{4,3,1,2,0:T(8,128)S(1)}, u32[]{:S(2)}, u32[]{:S(2)}) async-start(f32[4,2,1,128,128]{4,3,1,2,0:T(8,128)} %bitcast.12), calls=%async_computation.3 | async-start | bytes 1048576 | tf_op jit(solution)/shard_map/all_to_all | solution.py:167
  169.7 6.8 %all-to-all-done.3 = f32[4,2,1,128,128]{4,3,1,2,0:T(8,128)S(1)} async-done(((f32[4,2,1,128,128]{4,3,1,2,0:T(8,128)}), f32[4,2,1,128,128]{4,3,1,2,0:T(8,128)S(1)}, u32[]{:S(2)}, u32[]{:S(2)}) %all-to-all-start.3) | async-done | bytes 524320 | tf_op jit(solution)/shard_map/all_to_all | solution.py:167
  176.5 3.5 %all-to-all-start.4 = ((f32[4,2,1,128,128]{4,3,1,2,0:T(8,128)}), f32[4,2,1,128,128]{4,3,1,2,0:T(8,128)S(1)}, u32[]{:S(2)}, u32[]{:S(2)}) async-start(f32[4,2,1,128,128]{4,3,1,2,0:T(8,128)} %bitcast.15), calls=%async_computation.4 | async-start | bytes 1048576 | tf_op jit(solution)/shard_map/all_to_all | solution.py:167
  181.2 8.0 %all-to-all-done.4 = f32[4,2,1,128,128]{4,3,1,2,0:T(8,128)S(1)} async-done(((f32[4,2,1,128,128]{4,3,1,2,0:T(8,128)}), f32[4,2,1,128,128]{4,3,1,2,0:T(8,128)S(1)}, u32[]{:S(2)}, u32[]{:S(2)}) %all-to-all-start.4) | async-done | bytes 524320 | tf_op jit(solution)/shard_map/all_to_all | solution.py:167
  (89 shorter events, 36.0 us)
Async XLA Ops:
  2.2 31.2 %collective-permute-start = (bf16[2,2,4,64,512]{4,3,2,1,0:T(8,128)(2,1)S(1)}, bf16[2,2,4,64,512]{4,3,2,1,0:T(8,128)(2,1)S(1)}, u32[]{:S(2)}, u32[]{:S(2)}) collective-permute-start(bf16[2,2,4,64,512]{4,3,2,1,0:T(8,128)(2,1)S(1)} %slice_select_fusion.2.here), channel_id=1, source_target_pairs={{0,8},{8,16},{16,24},{24,32},{32,40},{40,48},{48,56},{56,64},{64,7... | collective-permute-start | bytes 3145736 | tf_op jit(solution)/shard_map/ppermute | solution.py:18
  6.0 28.5 %collective-permute-start.1 = (bf16[2,2,4,64,512]{4,3,2,1,0:T(8,128)(2,1)S(1)}, bf16[2,2,4,64,512]{4,3,2,1,0:T(8,128)(2,1)S(1)}, u32[]{:S(2)}, u32[]{:S(2)}) collective-permute-start(bf16[2,2,4,64,512]{4,3,2,1,0:T(8,128)(2,1)S(1)} %slice_select_fusion.2.here), channel_id=1, source_target_pairs={{8,0},{16,8},{24,16},{32,24},{40,32},{48,40},{56,48},{64,56},{72,6... | collective-permute-start | bytes 3145736 | tf_op jit(solution)/shard_map/ppermute | solution.py:18
  15.4 15.2 %collective-permute-start.2 = (bf16[2,2,4,128,128]{4,3,2,1,0:T(8,128)(2,1)}, bf16[2,2,4,128,128]{4,3,2,1,0:T(8,128)(2,1)}, u32[]{:S(2)}, u32[]{:S(2)}) collective-permute-start(bf16[2,2,4,128,128]{4,3,2,1,0:T(8,128)(2,1)} %pad_maximum_fusion.3), channel_id=1, source_target_pairs={{0,4},{4,0},{1,5},{5,1},{2,6},{6,2},{3,7},{7,3},{8,12},{12,8},{9,1... | collective-permute-start | bytes 1572872 | tf_op jit(solution)/shard_map/ppermute | solution.py:24
  21.0 17.0 %copy-start.1 = (bf16[2,8,4,64,512]{4,3,2,1,0:T(8,128)(2,1)S(1)}, bf16[2,8,4,64,512]{4,3,2,1,0:T(8,128)(2,1)}, u32[]{:S(2)}) copy-start(bf16[2,8,4,64,512]{4,3,2,1,0:T(8,128)(2,1)} %param.4) | copy-start | bytes 12582916
  37.9 13.0 %collective-permute-start.3 = (f32[2,2,2,2,128,128]{5,4,3,2,1,0:T(8,128)S(1)}, f32[2,2,2,2,128,128]{5,4,3,2,1,0:T(8,128)S(1)}, u32[]{:S(2)}, u32[]{:S(2)}) collective-permute-start(f32[2,2,2,2,128,128]{5,4,3,2,1,0:T(8,128)S(1)} %get-tuple-element.39), channel_id=1, source_target_pairs={{0,1},{1,0},{2,3},{3,2},{4,5},{5,4},{6,7},{7,6},{8,9},{9,8},{10,11... | collective-permute-start | bytes 3145736 | tf_op jit(solution)/shard_map/ppermute | solution.py:24
  38.3 30.3 %collective-permute-start.4 = (bf16[2,2,4,64,512]{4,3,2,1,0:T(8,128)(2,1)S(1)}, bf16[2,2,4,64,512]{4,3,2,1,0:T(8,128)(2,1)S(1)}, u32[]{:S(2)}, u32[]{:S(2)}) collective-permute-start(bf16[2,2,4,64,512]{4,3,2,1,0:T(8,128)(2,1)S(1)} %get-tuple-element.108.here), channel_id=1, source_target_pairs={{0,8},{8,16},{16,24},{24,32},{32,40},{40,48},{48,56},{56,64},{64,7... | collective-permute-start | bytes 3145736 | tf_op jit(solution)/shard_map/ppermute | solution.py:18
  40.3 29.5 %collective-permute-start.5 = (bf16[2,2,4,64,512]{4,3,2,1,0:T(8,128)(2,1)S(1)}, bf16[2,2,4,64,512]{4,3,2,1,0:T(8,128)(2,1)S(1)}, u32[]{:S(2)}, u32[]{:S(2)}) collective-permute-start(bf16[2,2,4,64,512]{4,3,2,1,0:T(8,128)(2,1)S(1)} %get-tuple-element.108.here), channel_id=1, source_target_pairs={{8,0},{16,8},{24,16},{32,24},{40,32},{48,40},{56,48},{64,56},{72,6... | collective-permute-start | bytes 3145736 | tf_op jit(solution)/shard_map/ppermute | solution.py:18
  46.7 15.6 %collective-permute-start.6 = (bf16[2,2,4,128,128]{4,3,2,1,0:T(8,128)(2,1)S(1)}, bf16[2,2,4,128,128]{4,3,2,1,0:T(8,128)(2,1)S(1)}, u32[]{:S(2)}, u32[]{:S(2)}) collective-permute-start(bf16[2,2,4,128,128]{4,3,2,1,0:T(8,128)(2,1)S(1)} %pad_maximum_fusion.5), channel_id=1, source_target_pairs={{0,4},{4,0},{1,5},{5,1},{2,6},{6,2},{3,7},{7,3},{8,12},{12,8},{9,1... | collective-permute-start | bytes 1572872 | tf_op jit(solution)/shard_map/ppermute | solution.py:24
  52.0 33.2 %copy-start.11 = (pred[64,128]{1,0:T(8,128)(4,1)S(1)}, pred[64,128]{1,0:T(8,128)(4,1)}, u32[]{:S(2)}) copy-start(pred[64,128]{1,0:T(8,128)(4,1)} %copy-done.10) | copy-start | bytes 24580
  52.0 33.2 %copy-start.12 = (pred[64,128]{1,0:T(8,128)(4,1)S(1)}, pred[64,128]{1,0:T(8,128)(4,1)}, u32[]{:S(2)}) copy-start(pred[64,128]{1,0:T(8,128)(4,1)} %get-tuple-element.110) | copy-start | bytes 24580
  52.0 33.2 %copy-start.13 = (pred[64,128]{1,0:T(8,128)(4,1)S(1)}, pred[64,128]{1,0:T(8,128)(4,1)}, u32[]{:S(2)}) copy-start(pred[64,128]{1,0:T(8,128)(4,1)} %get-tuple-element.111) | copy-start | bytes 24580
  52.0 33.2 %copy-start.14 = (pred[64,128]{1,0:T(8,128)(4,1)S(1)}, pred[64,128]{1,0:T(8,128)(4,1)}, u32[]{:S(2)}) copy-start(pred[64,128]{1,0:T(8,128)(4,1)} %get-tuple-element.112) | copy-start | bytes 24580
  73.5 21.3 %collective-permute-start.7 = (f32[2,2,2,2,128,128]{5,4,3,2,1,0:T(8,128)}, f32[2,2,2,2,128,128]{5,4,3,2,1,0:T(8,128)}, u32[]{:S(2)}, u32[]{:S(2)}) collective-permute-start(f32[2,2,2,2,128,128]{5,4,3,2,1,0:T(8,128)} %get-tuple-element.44), channel_id=1, source_target_pairs={{0,1},{1,0},{2,3},{3,2},{4,5},{5,4},{6,7},{7,6},{8,9},{9,8},{10,11... | collective-permute-start | bytes 3145736 | tf_op jit(solution)/shard_map/ppermute | solution.py:24
  73.5 30.4 %collective-permute-start.8 = (bf16[2,2,4,64,512]{4,3,2,1,0:T(8,128)(2,1)S(1)}, bf16[2,2,4,64,512]{4,3,2,1,0:T(8,128)(2,1)}, u32[]{:S(2)}, u32[]{:S(2)}) collective-permute-start(bf16[2,2,4,64,512]{4,3,2,1,0:T(8,128)(2,1)S(1)} %get-tuple-element.46.here), channel_id=1, source_target_pairs={{0,8},{8,16},{16,24},{24,32},{32,40},{40,48},{48,56},{56,64},{64,7... | collective-permute-start | bytes 3145736 | tf_op jit(solution)/shard_map/ppermute | solution.py:18
  77.4 27.6 %collective-permute-start.9 = (bf16[2,2,4,64,512]{4,3,2,1,0:T(8,128)(2,1)S(1)}, bf16[2,2,4,64,512]{4,3,2,1,0:T(8,128)(2,1)}, u32[]{:S(2)}, u32[]{:S(2)}) collective-permute-start(bf16[2,2,4,64,512]{4,3,2,1,0:T(8,128)(2,1)S(1)} %get-tuple-element.46.here), channel_id=1, source_target_pairs={{8,0},{16,8},{24,16},{32,24},{40,32},{48,40},{56,48},{64,56},{72,6... | collective-permute-start | bytes 3145736 | tf_op jit(solution)/shard_map/ppermute | solution.py:18
  81.9 16.7 %collective-permute-start.10 = (bf16[2,2,4,128,128]{4,3,2,1,0:T(8,128)(2,1)}, bf16[2,2,4,128,128]{4,3,2,1,0:T(8,128)(2,1)}, u32[]{:S(2)}, u32[]{:S(2)}) collective-permute-start(bf16[2,2,4,128,128]{4,3,2,1,0:T(8,128)(2,1)} %pad_maximum_fusion.4), channel_id=1, source_target_pairs={{0,4},{4,0},{1,5},{5,1},{2,6},{6,2},{3,7},{7,3},{8,12},{12,8},{9,1... | collective-permute-start | bytes 1572872 | tf_op jit(solution)/shard_map/ppermute | solution.py:24
  87.7 21.7 %all-to-all-start = ((f32[4,2,2,128,128]{4,3,2,1,0:T(8,128)}), f32[4,2,2,128,128]{4,3,2,1,0:T(8,128)}, u32[]{:S(2)}, u32[]{:S(2)}) async-start(f32[4,2,2,128,128]{4,3,2,1,0:T(8,128)} %bitcast.39), calls=%async_computation | async-start | bytes 2097152 | tf_op jit(solution)/shard_map/all_to_all | solution.py:167
  109.2 17.6 %copy-start.5 = (bf16[2,1,4,64,128]{4,3,2,1,0:T(8,128)(2,1)S(1)}, bf16[2,1,4,64,128]{4,3,2,1,0:T(8,128)(2,1)}, u32[]{:S(2)}) copy-start(bf16[2,1,4,64,128]{4,3,2,1,0:T(8,128)(2,1)} %get-tuple-element.64) | copy-start | bytes 393220
  109.3 17.6 %copy-start.6 = (bf16[2,1,4,64,128]{4,3,2,1,0:T(8,128)(2,1)S(1)}, bf16[2,1,4,64,128]{4,3,2,1,0:T(8,128)(2,1)}, u32[]{:S(2)}) copy-start(bf16[2,1,4,64,128]{4,3,2,1,0:T(8,128)(2,1)} %get-tuple-element.86) | copy-start | bytes 393220
  109.3 18.5 %collective-permute-start.11 = (f32[2,2,2,2,128,128]{5,4,3,2,1,0:T(8,128)}, f32[2,2,2,2,128,128]{5,4,3,2,1,0:T(8,128)}, u32[]{:S(2)}, u32[]{:S(2)}) collective-permute-start(f32[2,2,2,2,128,128]{5,4,3,2,1,0:T(8,128)} %get-tuple-element.50), channel_id=1, source_target_pairs={{0,1},{1,0},{2,3},{3,2},{4,5},{5,4},{6,7},{7,6},{8,9},{9,8},{10,11... | collective-permute-start | bytes 3145736 | tf_op jit(solution)/shard_map/ppermute | solution.py:24
  109.4 21.2 %all-to-all-start.1 = ((f32[4,2,2,128,128]{4,3,2,1,0:T(8,128)}), f32[4,2,2,128,128]{4,3,2,1,0:T(8,128)}, u32[]{:S(2)}, u32[]{:S(2)}) async-start(f32[4,2,2,128,128]{4,3,2,1,0:T(8,128)} %bitcast.41), calls=%async_computation.1 | async-start | bytes 2097152 | tf_op jit(solution)/shard_map/all_to_all | solution.py:167
  114.0 23.2 %collective-permute-start.12 = (bf16[2,1,4,64,512]{4,3,2,1,0:T(8,128)(2,1)S(1)}, bf16[2,1,4,64,512]{4,3,2,1,0:T(8,128)(2,1)S(1)}, u32[]{:S(2)}, u32[]{:S(2)}) collective-permute-start(bf16[2,1,4,64,512]{4,3,2,1,0:T(8,128)(2,1)S(1)} %copy-done), channel_id=1, source_target_pairs={{0,8},{8,16},{16,24},{24,32},{32,40},{40,48},{48,56},{56,64},{64,7... | collective-permute-start | bytes 1572872 | tf_op jit(solution)/shard_map/ppermute | solution.py:18
  117.3 19.9 %collective-permute-start.13 = (bf16[2,1,4,64,512]{4,3,2,1,0:T(8,128)(2,1)S(1)}, bf16[2,1,4,64,512]{4,3,2,1,0:T(8,128)(2,1)}, u32[]{:S(2)}, u32[]{:S(2)}) collective-permute-start(bf16[2,1,4,64,512]{4,3,2,1,0:T(8,128)(2,1)S(1)} %copy-done), channel_id=1, source_target_pairs={{8,0},{16,8},{24,16},{32,24},{40,32},{48,40},{56,48},{64,56},{72,6... | collective-permute-start | bytes 1572872 | tf_op jit(solution)/shard_map/ppermute | solution.py:18
  122.5 14.7 %collective-permute-start.14 = (bf16[2,1,4,128,128]{4,3,2,1,0:T(8,128)(2,1)}, bf16[2,1,4,128,128]{4,3,2,1,0:T(8,128)(2,1)S(1)}, u32[]{:S(2)}, u32[]{:S(2)}) collective-permute-start(bf16[2,1,4,128,128]{4,3,2,1,0:T(8,128)(2,1)} %pad_maximum_fusion.8), channel_id=1, source_target_pairs={{0,4},{4,0},{1,5},{5,1},{2,6},{6,2},{3,7},{7,3},{8,12},{12,8},{9,1... | collective-permute-start | bytes 786440 | tf_op jit(solution)/shard_map/ppermute | solution.py:24
  130.6 30.9 %all-to-all-start.2 = ((f32[4,2,2,128,128]{4,3,2,1,0:T(8,128)}), f32[4,2,2,128,128]{4,3,2,1,0:T(8,128)}, u32[]{:S(2)}, u32[]{:S(2)}) async-start(f32[4,2,2,128,128]{4,3,2,1,0:T(8,128)} %bitcast.40), calls=%async_computation.2 | async-start | bytes 2097152 | tf_op jit(solution)/shard_map/all_to_all | solution.py:167
  139.4 12.3 %collective-permute-start.15 = (f32[2,2,2,1,128,128]{5,4,3,2,1,0:T(8,128)S(1)}, f32[2,2,2,1,128,128]{5,4,3,2,1,0:T(8,128)S(1)}, u32[]{:S(2)}, u32[]{:S(2)}) collective-permute-start(f32[2,2,2,1,128,128]{5,4,3,2,1,0:T(8,128)S(1)} %get-tuple-element.56), channel_id=1, source_target_pairs={{0,1},{1,0},{2,3},{3,2},{4,5},{5,4},{6,7},{7,6},{8,9},{9,8},{10,11... | collective-permute-start | bytes 1572872 | tf_op jit(solution)/shard_map/ppermute | solution.py:24
  139.5 19.2 %collective-permute-start.16 = (bf16[2,1,4,64,512]{4,3,2,1,0:T(8,128)(2,1)S(1)}, bf16[2,1,4,64,512]{4,3,2,1,0:T(8,128)(2,1)S(1)}, u32[]{:S(2)}, u32[]{:S(2)}) collective-permute-start(bf16[2,1,4,64,512]{4,3,2,1,0:T(8,128)(2,1)S(1)} %get-tuple-element.58.here), channel_id=1, source_target_pairs={{0,8},{8,16},{16,24},{24,32},{32,40},{40,48},{48,56},{56,64},{64,7... | collective-permute-start | bytes 1572872 | tf_op jit(solution)/shard_map/ppermute | solution.py:18
  142.9 17.0 %collective-permute-start.17 = (bf16[2,1,4,64,512]{4,3,2,1,0:T(8,128)(2,1)S(1)}, bf16[2,1,4,64,512]{4,3,2,1,0:T(8,128)(2,1)S(1)}, u32[]{:S(2)}, u32[]{:S(2)}) collective-permute-start(bf16[2,1,4,64,512]{4,3,2,1,0:T(8,128)(2,1)S(1)} %get-tuple-element.58.here), channel_id=1, source_target_pairs={{8,0},{16,8},{24,16},{32,24},{40,32},{48,40},{56,48},{64,56},{72,6... | collective-permute-start | bytes 1572872 | tf_op jit(solution)/shard_map/ppermute | solution.py:18
  148.0 10.3 %collective-permute-start.18 = (bf16[2,1,4,128,128]{4,3,2,1,0:T(8,128)(2,1)S(1)}, bf16[2,1,4,128,128]{4,3,2,1,0:T(8,128)(2,1)S(1)}, u32[]{:S(2)}, u32[]{:S(2)}) collective-permute-start(bf16[2,1,4,128,128]{4,3,2,1,0:T(8,128)(2,1)S(1)} %copy-done.9), channel_id=1, source_target_pairs={{0,4},{4,0},{1,5},{5,1},{2,6},{6,2},{3,7},{7,3},{8,12},{12,8},{9,1... | collective-permute-start | bytes 786440 | tf_op jit(solution)/shard_map/ppermute | solution.py:24
  161.4 7.4 %collective-permute-start.19 = (f32[2,2,2,1,128,128]{5,4,3,2,1,0:T(8,128)S(1)}, f32[2,2,2,1,128,128]{5,4,3,2,1,0:T(8,128)S(1)}, u32[]{:S(2)}, u32[]{:S(2)}) collective-permute-start(f32[2,2,2,1,128,128]{5,4,3,2,1,0:T(8,128)S(1)} %get-tuple-element.62), channel_id=1, source_target_pairs={{0,1},{1,0},{2,3},{3,2},{4,5},{5,4},{6,7},{7,6},{8,9},{9,8},{10,11... | collective-permute-start | bytes 1572872 | tf_op jit(solution)/shard_map/ppermute | solution.py:24
  161.5 14.9 %all-to-all-start.3 = ((f32[4,2,1,128,128]{4,3,1,2,0:T(8,128)}), f32[4,2,1,128,128]{4,3,1,2,0:T(8,128)S(1)}, u32[]{:S(2)}, u32[]{:S(2)}) async-start(f32[4,2,1,128,128]{4,3,1,2,0:T(8,128)} %bitcast.12), calls=%async_computation.3 | async-start | bytes 1048576 | tf_op jit(solution)/shard_map/all_to_all | solution.py:167
  176.5 12.7 %all-to-all-start.4 = ((f32[4,2,1,128,128]{4,3,1,2,0:T(8,128)}), f32[4,2,1,128,128]{4,3,1,2,0:T(8,128)S(1)}, u32[]{:S(2)}, u32[]{:S(2)}) async-start(f32[4,2,1,128,128]{4,3,1,2,0:T(8,128)} %bitcast.15), calls=%async_computation.4 | async-start | bytes 1048576 | tf_op jit(solution)/shard_map/all_to_all | solution.py:167
  (10 other events, 113.5 us)

commit v3 on v0

v3 whole, which is shorter than its diff:
```python
import functools

import jax
import jax.numpy as jnp
from jax import lax
from jax.experimental import pallas as pl
from jax.experimental.pallas import tpu as pltpu
from jax.sharding import Mesh, PartitionSpec as P

COST = 12
FIRST = 2
TOP = 32767.0
LOG = 256.0
LEAST = 2.0**-126
PAD = 16
SHOT = ("sup", "half")
XLINE = ("side", "core")
RING = ("half", "side", "core")


def shifted(block, distance):
    n = lax.axis_size("sup")
    return lax.ppermute(
        block, "sup", [(i, i + distance) for i in range(n) if 0 <= i + distance < n]
    )


def swapped(block, axes):
    n = lax.axis_size(axes)
    return lax.ppermute(block, axes, [(i, n - 1 - i) for i in range(n)])


def products_kernel(counts, place, *refs):
    out = refs[-1]
    groups, start = [], 0
    for count in counts:
        groups.append(refs[start : start + count])
        start += count
    windows, own, cross = groups[:3], groups[3], groups[4]
    half = place[0]
    upper = half == 1
    pts, recv = windows[0][0].shape[3:]
    shots = own[0].shape[4]

    def piece(blocks, part, k):
        return jnp.concatenate(
            [
                block[part, 0, :, k * pts : (k + 1) * pts, :].reshape(-1, shots)
                for block in blocks
            ],
            axis=0,
        )

    lefts, rights = [], []
    for k in range(3):
        both = []
        for part in range(2):
            low, high = piece(cross, part, 0), piece(cross, part, 1)
            none = jnp.zeros_like(low)
            theirs = (
                jnp.where(upper, low, none),
                jnp.where(upper, high, low),
                jnp.where(upper, none, high),
            )[k]
            both.append(jnp.concatenate([piece(own, part, k), theirs], axis=1))
        both = jnp.concatenate(both, axis=1).T
        real, imag = both[: 2 * shots], both[2 * shots :]
        lefts += [both, jnp.concatenate([-imag, real], axis=0)]
        rights += [
            [block[part, 0].reshape(-1, recv) for block in windows[k]] for part in range(2)
        ]
    left = jnp.concatenate(lefts, axis=1)
    right = jnp.concatenate([rows for side in rights for rows in side], axis=0)
    width = recv // 4
    total = jnp.dot(left, right, preferred_element_type=jnp.float32)
    for quarter in range(4):
        columns = total[:, quarter * width : (quarter + 1) * width]
        for block, to in enumerate((half, 1 - half)):
            values = [
                columns[(2 * part + block) * shots : (2 * part + block + 1) * shots]
                for part in range(2)
            ]
            peak = jnp.maximum(*(jnp.max(jnp.abs(v), axis=0, keepdims=True) for v in values))
            level = jnp.ceil(jnp.log2(jnp.maximum(peak, LEAST)) * LOG)
            unit = jnp.exp2(level * (-1.0 / LOG))
            for part in range(2):
                steps = jnp.clip(jnp.round(values[part] * unit * TOP), -TOP, TOP)
                out[4 * to + quarter, 0, part * shots : (part + 1) * shots] = steps.astype(
                    jnp.int32
                ).astype(jnp.int16)
            level = jnp.broadcast_to(level.astype(jnp.int32), (PAD, width))
            out[4 * to + quarter, 0, 2 * shots : 2 * shots + PAD] = level.astype(jnp.int16)


def products(place, freqs, *groups):
    arrays, starts = zip(*(block for group in groups for block in group))
    recv, shots = arrays[0].shape[4], arrays[-1].shape[4]
    rows = sum(array.shape[2] * array.shape[3] for array in arrays[: sum(map(len, groups[:3]))])
    first, count = freqs

    def spec(array, start):
        if array.shape[1] == count == 1:
            return pl.BlockSpec(memory_space=pltpu.VMEM)
        return pl.BlockSpec((2, 1) + array.shape[2:], lambda f: (0, f + first - start, 0, 0, 0))

    return pl.pallas_call(
        functools.partial(products_kernel, [len(group) for group in groups]),
        grid=(count,),
        in_specs=[pl.BlockSpec(memory_space=pltpu.SMEM)]
        + [spec(*block) for block in zip(arrays, starts)],
        out_specs=pl.BlockSpec((8, 1, 2 * shots + PAD, recv // 4), lambda f: (0, f, 0, 0)),
        out_shape=jax.ShapeDtypeStruct((8, count, 2 * shots + PAD, recv // 4), jnp.int16),
        compiler_params=pltpu.CompilerParams(vmem_limit_bytes=58 * 2**20),
        cost_estimate=pl.CostEstimate(
            flops=COST * count * 2 * (4 * shots) * (2 * rows) * recv,
            bytes_accessed=2**20,
            transcendentals=0,
        ),
        name="products",
    )(place, *arrays)


def finish_kernel(terms, *refs):
    out = refs[-1]
    shots = out.shape[3]

    def wide(values):
        return values.astype(jnp.int32).astype(jnp.float32)

    for core in range(2):
        sums = [jnp.zeros(out.shape[3:], jnp.float32) for _ in range(2)]
        for chip in range(4):
            source = 2 * chip + core
            level = wide(terms[source, 0, 2 * shots : 2 * shots + PAD])[:1]
            unit = jnp.exp2(level * (1.0 / LOG)) * (1.0 / TOP)
            for part in range(2):
                steps = wide(terms[source, 0, part * shots : (part + 1) * shots])
                sums[part] = sums[part] + steps * unit
        for part in range(2):
            out[part, core, 0] = sums[part].astype(out.dtype)


def finish(terms, freqs, count, before):
    first, size = freqs
    rows, width = terms.shape[2:]
    shots = (rows - PAD) // 2
    done = [] if before is None else [before]
    return pl.pallas_call(
        finish_kernel,
        grid=(size,),
        in_specs=[pl.BlockSpec((8, 1, rows, width), lambda f: (0, f, 0, 0))]
        + [pl.BlockSpec(memory_space=pl.ANY)] * len(done),
        out_specs=pl.BlockSpec((2, 2, 1, shots, width), lambda f: (0, 0, f + first, 0, 0)),
        out_shape=jax.ShapeDtypeStruct((2, 2, count, shots, width), jnp.bfloat16),
        input_output_aliases={1: 0} if done else {},
        compiler_params=pltpu.CompilerParams(vmem_limit_bytes=16 * 2**20),
        name="finish",
    )(terms, *done)


def on_device(surface_gathers, source_gathers, aperture, live):
    freqs_here, _, pts, recv = surface_gathers.shape[1:]
    spread = source_gathers.shape[4]
    half, core = lax.axis_index("half"), lax.axis_index("core")
    place = half.astype(jnp.int32).reshape(1)
    count = freqs_here // 2
    heard = lax.broadcasted_iota(jnp.int32, surface_gathers.shape[2:], 2) < live[:, :, None]
    first_point = (2 * lax.axis_index("sup") + half) * pts - (spread - pts) // 2
    inline = first_point + lax.broadcasted_iota(jnp.int32, (spread, aperture.shape[0]), 0)
    inside = (inline >= aperture[:, 0][None, :]) & (inline < aperture[:, 1][None, :])
    shots = source_gathers.transpose(0, 1, 3, 4, 2)

    def of_core(array, which, first, size):
        return lax.dynamic_slice_in_dim(array, which * count + first, size, 1)

    def muted(gathers, which, first, size):
        gathers = of_core(gathers, which, first, size)
        return jnp.where(heard, gathers, jnp.zeros((), gathers.dtype))

    def pieces(block, which):
        spans = [slice(k * pts, (k + 1) * pts) for k in which]
        return jnp.concatenate(
            [
                jnp.where(inside[span], block[:, :, :, span], jnp.zeros((), block.dtype))
                for span in spans
            ],
            axis=3,
        )

    early = muted(surface_gathers, core, 0, FIRST)
    early, surface_gathers, shots = lax.optimization_barrier((early, surface_gathers, shots))
    below_early, above_early = shifted(early, 1), shifted(early, -1)

    mine, others = of_core(shots, core, 0, count), of_core(shots, 1 - core, 0, count)
    cross = [
        (swapped(pieces(mine, (1, 3)), "half"), 0),
        (swapped(pieces(others, (1, 3)), ("half", "core")), 0),
    ]
    gathers = swapped(muted(surface_gathers, 1 - core, 0, count), "core")
    others = swapped(pieces(others, (0, 2, 4)), "core")
    gathers, others = lax.optimization_barrier((gathers, others))
    own = [(pieces(mine, (0, 2, 4)), 0), (others, 0)]
    early_too = gathers[:, :FIRST]
    below_too, above_too = shifted(early_too, 1), shifted(early_too, -1)
    arrived = [below_early, below_too]
    here, below, above = [], [], []
    for i in range(FIRST, count):
        block = muted(surface_gathers, core, i, 1)
        block = jnp.concatenate([block, gathers[:, i : i + 1]], axis=2)
        block, arrived[i - FIRST] = lax.optimization_barrier((block, arrived[i - FIRST]))
        here.append([(block, i)])
        below.append([(shifted(block, 1), i)])
        above.append([(shifted(block, -1), i)])
    here.insert(0, [(early, 0), (gathers, 0)])
    below.insert(0, [(block, 0) for block in arrived])
    above.insert(0, [(above_early, 0), (above_too, 0)])

    spans = [(0, FIRST)] + [(i, 1) for i in range(FIRST, count)]
    partial = [
        products(place, freqs, below[i], here[i], above[i], own, cross)
        for i, freqs in enumerate(spans)
    ]
    predicted = None
    for i, freqs in enumerate(spans):
        terms = lax.all_to_all(partial[i], RING, 0, 0, tiled=True)
        if i + 1 < len(spans):
            terms, partial[i + 1] = lax.optimization_barrier((terms, partial[i + 1]))
        predicted = finish(terms, freqs, count, predicted)
    return predicted.reshape((2, freqs_here) + predicted.shape[3:])


def solution(mesh):
    fine = Mesh(
        mesh.devices.reshape(mesh.shape["shot"] // 2, 2, mesh.shape["xline"] // 2, 2),
        SHOT + XLINE,
    )
    return jax.shard_map(
        on_device,
        mesh=fine,
        in_specs=(
            P(None, None, XLINE, SHOT, None),
            P(None, None, SHOT, XLINE, None),
            P(SHOT, None),
            P(XLINE, SHOT),
        ),
        out_specs=P(None, None, SHOT, XLINE),
        check_vma=False,
    )
```

time: 302 us -> 140 us (0.46)
  waiting for transfers between devices: 213 us -> 52.7 us
  starting transfers between devices: 18.4 us -> 47 us
  matrix products: 20.2 us -> 0 us
  Pallas kernels: 0 us -> 20.1 us
  local copies, waits for them, and re-layouts: 18.8 us -> 1.29 us
  between operations: 13.5 us -> 0.22 us
    ppermute x4 -> x12, waiting for transfers between devices: 165 us -> 35.6 us  [the longest x8 35.6 us: shifted(): lax.ppermute(block, 'sup', [(i, i + distance) for i in range(n) if 0 <= i...]
    reduce_scatter x1 -> x0, waiting for transfers between devices: 48 us -> none  [on_device(): lax.psum_scatter(partials, 'xline', scatter_dimension=3, tiled=True)]
    dot_general x4 -> x0, matrix products: 20.2 us -> none  [contract(): jnp.einsum('ginu,gnuw->giw', leading_operand, trailing_operand, preferred...]
    pallas_call x0 -> x6, Pallas kernels: none -> 20.1 us  [the longest x3 17.4 us: products(): pl.pallas_call(functools.partial(products_kernel, [len(group) for group i...]
    all_to_all x0 -> x3, waiting for transfers between devices: none -> 17.1 us  [on_device(): terms = lax.all_to_all(partial[i], RING, 0, 0, tiled=True)]
    ppermute x4 -> x12, starting transfers between devices: 18.4 us -> 35.5 us  [the longest x8 31.7 us: shifted(): lax.ppermute(block, 'sup', [(i, i + distance) for i in range(n) if 0 <= i...]
    unnamed x7 -> x8, local copies, waits for them, and re-layouts: 14.1 us -> 0.02 us
    all_to_all x0 -> x3, starting transfers between devices: none -> 11.6 us  [on_device(): terms = lax.all_to_all(partial[i], RING, 0, 0, tiled=True)]
  transfers between devices with their start and end apart: 5 -> 15, of which waited for: 3 -> 9; matrix products, arithmetic and copies ran while one was open for 7% -> 9% of each run, Pallas kernels for 0% -> 14%
where the time goes in v3:
time: 140 us
  waiting for transfers between devices  52.7 us (38%)
  starting transfers between devices  47 us (34%)
  Pallas kernels  20.1 us (14%)
  other arithmetic  18.3 us (13%)
    ppermute x8, waiting for transfers between devices, shifted(): lax.ppermute(block, 'sup', [(i, i + distance) for i in range(n) if 0 <= i...  35.6 us
    ppermute x8, starting transfers between devices, shifted(): lax.ppermute(block, 'sup', [(i, i + distance) for i in range(n) if 0 <= i...  31.7 us
    pallas_call x3, Pallas kernels, products(): pl.pallas_call(functools.partial(products_kernel, [len(group) for group i...  17.4 us
    all_to_all x3, waiting for transfers between devices, on_device(): terms = lax.all_to_all(partial[i], RING, 0, 0, tiled=True)  17.1 us
    all_to_all x3, starting transfers between devices, on_device(): terms = lax.all_to_all(partial[i], RING, 0, 0, tiled=True)  11.6 us
    select_n x3, other arithmetic, muted(): return jnp.where(heard, gathers, jnp.zeros((), gathers.dtype))  6.84 us
    select_n x1, other arithmetic, pieces(): jnp.where(inside[span], block[:, :, :, span], jnp.zeros((), block.dtype))  4.78 us
    concatenate x4, other arithmetic, pieces(): jnp.concatenate([jnp.where(inside[span], block[:, :, :, span], jnp.zeros(...  4.58 us
  transfers between devices with their start and end apart: 15, of which 9 were waited for; matrix products, arithmetic and copies ran while one was open for 9% of the time, Pallas kernels for 14%

profile of v3, /device:TPU:6, one launch (start us, length us, event | category | flops | bytes accessed | tf_op | source)
XLA Modules:
  0.0 139.7 jit_solution(9947682533072089069)
XLA Ops:
  0.8 2.3 %dynamic-slice_select_fusion.1.refs_2_ = bf16[2,2,4,64,512]{4,3,2,1,0:T(8,128)(2,1)} fusion(bf16[2,8,4,64,512]{4,3,2,1,0:T(8,128)(2,1)} %param.4, s32[]{:T(128)S(6)} %select_n.60, pred[4,64,512]{2,1,0:T(8,128)(4,1)S(1)} %iota_compare_fusion), kind=kLoop, calls=%fused_computation.7 | loop fusion | flops 524288 | bytes 2228228 | tf_op jit(solution)/shard_map/jit(_where)/select_n | solution.py:178
  3.2 3.2 %dynamic-slice_select_fusion = bf16[2,4,4,64,512]{4,3,2,1,0:T(8,128)(2,1)} fusion(bf16[2,8,4,64,512]{4,3,2,1,0:T(8,128)(2,1)} %param.4, s32[]{:T(128)S(6)} %select_n.64, pred[4,64,512]{2,1,0:T(8,128)(4,1)S(1)} %iota_compare_fusion), kind=kLoop, calls=%fused_computation | loop fusion | flops 1048576 | bytes 4325380 | tf_op jit(solution)/shard_map/jit(_where)/select_n | solution.py:178
  6.5 4.8 %dynamic-slice_select_fusion.3 = (bf16[2,4,4,64,128]{4,3,2,1,0:T(8,128)(2,1)S(1)}, bf16[2,4,4,64,128]{4,3,2,1,0:T(8,128)(2,1)S(1)}, bf16[2,4,4,64,128]{4,3,2,1,0...) fusion(bf16[2,8,4,320,128]{4,3,2,1,0:T(8,128)(2,1)} %bitcast.7,, ...), kind=kLoop, calls=%fused_computation.9 | loop fusion | flops 2621440 | bytes 10526744 | tf_op jit(solution)/shard_map/jit(_where)/select_n | solution.py:184
  12.0 3.8 %collective-permute-start.2 = (bf16[2,2,4,64,512]{4,3,2,1,0:T(8,128)(2,1)}, bf16[2,2,4,64,512]{4,3,2,1,0:T(8,128)(2,1)}, u32[]{:S(2)}, u32[]{:S(2)}) collective-permute-start(bf16[2,2,4,64,512]{4,3,2,1,0:T(8,128)(2,1)} %dynamic-slice_select_fusion.1.refs_2_), channel_id=1, source_target_pairs={{0,8},{8,16},{16,24},{24,32},{32,40},{40,48},{48,56},{56,64},{64,7... | collective-permute-start | bytes 3145736 | tf_op jit(solution)/shard_map/ppermute | solution.py:23
  15.9 6.1 %collective-permute-start.4 = (bf16[2,2,4,64,512]{4,3,2,1,0:T(8,128)(2,1)}, bf16[2,2,4,64,512]{4,3,2,1,0:T(8,128)(2,1)}, u32[]{:S(2)}, u32[]{:S(2)}) collective-permute-start(bf16[2,2,4,64,512]{4,3,2,1,0:T(8,128)(2,1)} %dynamic-slice_select_fusion.1.refs_2_), channel_id=1, source_target_pairs={{8,0},{16,8},{24,16},{32,24},{40,32},{48,40},{56,48},{64,56},{72,6... | collective-permute-start | bytes 3145736 | tf_op jit(solution)/shard_map/ppermute | solution.py:23
  22.0 1.1 pad_maximum_fusion.4
  23.1 3.2 %collective-permute-start.6 = (bf16[2,4,4,128,128]{4,3,2,1,0:T(8,128)(2,1)}, bf16[2,4,4,128,128]{4,3,2,1,0:T(8,128)(2,1)}, u32[]{:S(2)}, u32[]{:S(2)}) collective-permute-start(bf16[2,4,4,128,128]{4,3,2,1,0:T(8,128)(2,1)} %pad_maximum_fusion.4), channel_id=1, source_target_pairs={{0,4},{4,0},{1,5},{5,1},{2,6},{6,2},{3,7},{7,3},{8,12},{12,8},{9,1... | collective-permute-start | bytes 3145736 | tf_op jit(solution)/shard_map/ppermute | solution.py:30
  26.3 1.2 slice.75
  27.5 1.9 %collective-permute-start.3 = (bf16[2,2,4,64,512]{4,3,2,1,0:T(8,128)(2,1)}, bf16[2,2,4,64,512]{4,3,2,1,0:T(8,128)(2,1)}, u32[]{:S(2)}, u32[]{:S(2)}) collective-permute-start(bf16[2,2,4,64,512]{4,3,2,1,0:T(8,128)(2,1)} %slice.75), channel_id=1, source_target_pairs={{0,8},{8,16},{16,24},{24,32},{32,40},{40,48},{48,56},{56,64},{64,7... | collective-permute-start | bytes 3145736 | tf_op jit(solution)/shard_map/ppermute | solution.py:23
  30.4 13.9 %collective-permute-done.2.refs_0_ = bf16[2,2,4,64,512]{4,3,2,1,0:T(8,128)(2,1)} collective-permute-done((bf16[2,2,4,64,512]{4,3,2,1,0:T(8,128)(2,1)}, bf16[2,2,4,64,512]{4,3,2,1,0:T(8,128)(2,1)}, u32[]{:S(2)}, u32[]{:S(2)}) %collective-permute-start.2) | collective-permute-done | bytes 1048608 | tf_op jit(solution)/shard_map/ppermute | solution.py:23
  44.3 4.0 %collective-permute-start.5 = (bf16[2,2,4,64,512]{4,3,2,1,0:T(8,128)(2,1)}, bf16[2,2,4,64,512]{4,3,2,1,0:T(8,128)(2,1)}, u32[]{:S(2)}, u32[]{:S(2)}) collective-permute-start(bf16[2,2,4,64,512]{4,3,2,1,0:T(8,128)(2,1)} %slice.75), channel_id=1, source_target_pairs={{8,0},{16,8},{24,16},{32,24},{40,32},{48,40},{56,48},{64,56},{72,6... | collective-permute-start | bytes 3145736 | tf_op jit(solution)/shard_map/ppermute | solution.py:23
  48.3 2.3 %pad_maximum_fusion.1.refs_6_.refs_3_ = bf16[2,4,4,192,128]{4,3,2,1,0:T(8,128)(2,1)} fusion(bf16[2,4,4,64,128]{4,3,2,1,0:T(8,128)(2,1)S(1)} %get-tuple-element.42, bf16[2,4,4,64,128]{4,3,2,1,0:T(8,128)(2,1)S(1)} %get-tuple-element.44, bf16[2,4,4,64,128]{4,3,2,1,0:T(8,128)(2,1)} %get-tuple-element.46), kind=kLoop, calls=%fused_computation.2 | loop fusion | flops 4718592 | bytes 3145728 | tf_op jit(solution)/shard_map/concatenate | solution.py:182
  50.6 1.3 dynamic-slice_select_fusion.12
  52.0 1.1 pad_maximum_fusion.2.refs_1_
  53.2 13.0 %collective-permute-done.3.refs_1_ = bf16[2,2,4,64,512]{4,3,2,1,0:T(8,128)(2,1)} collective-permute-done((bf16[2,2,4,64,512]{4,3,2,1,0:T(8,128)(2,1)}, bf16[2,2,4,64,512]{4,3,2,1,0:T(8,128)(2,1)}, u32[]{:S(2)}, u32[]{:S(2)}) %collective-permute-start.3) | collective-permute-done | bytes 1048608 | tf_op jit(solution)/shard_map/ppermute | solution.py:23
  66.2 1.9 %collective-permute-start.8 = (bf16[2,1,8,64,512]{4,3,2,1,0:T(8,128)(2,1)}, bf16[2,1,8,64,512]{4,3,2,1,0:T(8,128)(2,1)}, u32[]{:S(2)}, u32[]{:S(2)}) collective-permute-start(bf16[2,1,8,64,512]{4,3,2,1,0:T(8,128)(2,1)} %pad_maximum_fusion.2.refs_1_), channel_id=1, source_target_pairs={{0,8},{8,16},{16,24},{24,32},{32,40},{40,48},{48,56},{56,64},{64,7... | collective-permute-start | bytes 3145736 | tf_op jit(solution)/shard_map/ppermute | solution.py:23
  68.1 6.0 %collective-permute-start.9 = (bf16[2,1,8,64,512]{4,3,2,1,0:T(8,128)(2,1)}, bf16[2,1,8,64,512]{4,3,2,1,0:T(8,128)(2,1)}, u32[]{:S(2)}, u32[]{:S(2)}) collective-permute-start(bf16[2,1,8,64,512]{4,3,2,1,0:T(8,128)(2,1)} %pad_maximum_fusion.2.refs_1_), channel_id=1, source_target_pairs={{8,0},{16,8},{24,16},{32,24},{40,32},{48,40},{56,48},{64,56},{72,6... | collective-permute-start | bytes 3145736 | tf_op jit(solution)/shard_map/ppermute | solution.py:23
  74.2 1.9 %collective-permute-start.10 = (bf16[2,1,8,64,512]{4,3,2,1,0:T(8,128)(2,1)S(1)}, bf16[2,1,8,64,512]{4,3,2,1,0:T(8,128)(2,1)}, u32[]{:S(2)}, u32[]{:S(2)}) collective-permute-start(bf16[2,1,8,64,512]{4,3,2,1,0:T(8,128)(2,1)S(1)} %pad_maximum_fusion.3.refs_1_), channel_id=1, source_target_pairs={{0,8},{8,16},{16,24},{24,32},{32,40},{40,48},{48,56},{56,64},{64,7... | collective-permute-start | bytes 3145736 | tf_op jit(solution)/shard_map/ppermute | solution.py:23
  76.1 6.0 %collective-permute-start.11 = (bf16[2,1,8,64,512]{4,3,2,1,0:T(8,128)(2,1)S(1)}, bf16[2,1,8,64,512]{4,3,2,1,0:T(8,128)(2,1)}, u32[]{:S(2)}, u32[]{:S(2)}) collective-permute-start(bf16[2,1,8,64,512]{4,3,2,1,0:T(8,128)(2,1)S(1)} %pad_maximum_fusion.3.refs_1_), channel_id=1, source_target_pairs={{8,0},{16,8},{24,16},{32,24},{40,32},{48,40},{56,48},{64,56},{72,6... | collective-permute-start | bytes 3145736 | tf_op jit(solution)/shard_map/ppermute | solution.py:23
  82.1 7.2 %products.3 = s16[8,2,272,128]{3,2,1,0:T(8,128)(2,1)} custom-call(s32[1]{0:T(128)} %bitcast.place, bf16[2,2,4,64,512]{4,3,2,1,0:T(8,128)(2,1)} %collective-permute-done.2.refs_0_, bf16[2,2,4,64,512]{4,3,2,1,0:T(8,128)(2,1)} %collective-permute-done.3.refs_1_, bf16[2,2,4,64,512]{4,3,2,1,0:T(8,128)(2,1)} %dynamic-slice_select_fusion.1.refs_2_, ...), custom_call_target="tpu_custom_call" | custom-call | flops 38654705664 | bytes 1048576 | tf_op jit(solution)/shard_map/products/pallas_call | solution.py:106
  89.4 4.5 %all-to-all-start = ((s16[8,2,272,128]{3,2,1,0:T(8,128)(2,1)}), s16[8,2,272,128]{3,2,1,0:T(8,128)(2,1)S(1)}, u32[]{:S(2)}, u32[]{:S(2)}) async-start(s16[8,2,272,128]{3,2,1,0:T(8,128)(2,1)} %products.3), calls=%async_computation | async-start | bytes 2228224 | tf_op jit(solution)/shard_map/all_to_all | solution.py:225
  93.8 2.7 %collective-permute-done.8.refs_0_ = bf16[2,1,8,64,512]{4,3,2,1,0:T(8,128)(2,1)} collective-permute-done((bf16[2,1,8,64,512]{4,3,2,1,0:T(8,128)(2,1)}, bf16[2,1,8,64,512]{4,3,2,1,0:T(8,128)(2,1)}, u32[]{:S(2)}, u32[]{:S(2)}) %collective-permute-start.8) | collective-permute-done | bytes 1048608 | tf_op jit(solution)/shard_map/ppermute | solution.py:23
  96.6 1.5 %collective-permute-done.9.refs_2_ = bf16[2,1,8,64,512]{4,3,2,1,0:T(8,128)(2,1)} collective-permute-done((bf16[2,1,8,64,512]{4,3,2,1,0:T(8,128)(2,1)}, bf16[2,1,8,64,512]{4,3,2,1,0:T(8,128)(2,1)}, u32[]{:S(2)}, u32[]{:S(2)}) %collective-permute-start.9) | collective-permute-done | bytes 1048608 | tf_op jit(solution)/shard_map/ppermute | solution.py:23
  98.1 5.1 %products.4 = s16[8,1,272,128]{3,2,1,0:T(8,128)(2,1)} custom-call(s32[1]{0:T(128)} %bitcast.place, bf16[2,1,8,64,512]{4,3,2,1,0:T(8,128)(2,1)} %collective-permute-done.8.refs_0_, bf16[2,1,8,64,512]{4,3,2,1,0:T(8,128)(2,1)} %pad_maximum_fusion.2.refs_1_, bf16[2,1,8,64,512]{4,3,2,1,0:T(8,128)(2,1)} %collective-permute-done.9.refs_2_, ...), custom_call_target="tpu_custom_call" | custom-call | flops 19327352832 | bytes 1048576 | tf_op jit(solution)/shard_map/products/pallas_call | solution.py:106
  103.2 7.3 %all-to-all-done.terms = s16[8,2,272,128]{3,2,1,0:T(8,128)(2,1)S(1)} async-done(((s16[8,2,272,128]{3,2,1,0:T(8,128)(2,1)}), s16[8,2,272,128]{3,2,1,0:T(8,128)(2,1)S(1)}, u32[]{:S(2)}, u32[]{:S(2)}) %all-to-all-start) | async-done | bytes 1114144 | tf_op jit(solution)/shard_map/all_to_all | solution.py:225
  110.5 3.5 %all-to-all-start.1 = ((s16[8,1,272,128]{3,2,1,0:T(8,128)(2,1)}), s16[8,1,272,128]{3,2,1,0:T(8,128)(2,1)S(1)}, u32[]{:S(2)}, u32[]{:S(2)}) async-start(s16[8,1,272,128]{3,2,1,0:T(8,128)(2,1)} %products.4), calls=%async_computation.1 | async-start | bytes 1114112 | tf_op jit(solution)/shard_map/all_to_all | solution.py:225
  114.1 3.5 %collective-permute-done.10.refs_0_ = bf16[2,1,8,64,512]{4,3,2,1,0:T(8,128)(2,1)} collective-permute-done((bf16[2,1,8,64,512]{4,3,2,1,0:T(8,128)(2,1)S(1)}, bf16[2,1,8,64,512]{4,3,2,1,0:T(8,128)(2,1)}, u32[]{:S(2)}, u32[]{:S(2)}) %collective-permute-start.10) | collective-permute-done | bytes 1048608 | tf_op jit(solution)/shard_map/ppermute | solution.py:23
  117.5 1.1 collective-permute-done.11.refs_2_
  118.6 5.1 %products.5 = s16[8,1,272,128]{3,2,1,0:T(8,128)(2,1)} custom-call(s32[1]{0:T(128)} %bitcast.place, bf16[2,1,8,64,512]{4,3,2,1,0:T(8,128)(2,1)} %collective-permute-done.10.refs_0_, bf16[2,1,8,64,512]{4,3,2,1,0:T(8,128)(2,1)} %copy-done.1, bf16[2,1,8,64,512]{4,3,2,1,0:T(8,128)(2,1)} %collective-permute-done.11.refs_2_, ...), custom_call_target="tpu_custom_call" | custom-call | flops 19327352832 | bytes 1048576 | tf_op jit(solution)/shard_map/products/pallas_call | solution.py:106
  124.7 3.5 %all-to-all-start.2 = ((s16[8,1,272,128]{3,2,1,0:T(8,128)(2,1)}), s16[8,1,272,128]{3,2,1,0:T(8,128)(2,1)S(1)}, u32[]{:S(2)}, u32[]{:S(2)}) async-start(s16[8,1,272,128]{3,2,1,0:T(8,128)(2,1)} %products.5), calls=%async_computation.2 | async-start | bytes 1114112 | tf_op jit(solution)/shard_map/all_to_all | solution.py:225
  128.2 1.1 finish.3.refs_0_
  130.1 8.8 %all-to-all-done.2.terms = s16[8,1,272,128]{3,2,1,0:T(8,128)(2,1)S(1)} async-done(((s16[8,1,272,128]{3,2,1,0:T(8,128)(2,1)}), s16[8,1,272,128]{3,2,1,0:T(8,128)(2,1)S(1)}, u32[]{:S(2)}, u32[]{:S(2)}) %all-to-all-start.2) | async-done | bytes 557088 | tf_op jit(solution)/shard_map/all_to_all | solution.py:225
  (29 shorter events, 5.4 us)
Async XLA Ops:
  3.2 3.2 %copy-start.2 = (s32[128,2]{0,1:T(2,128)S(1)}, s32[128,2]{0,1:T(2,128)}, u32[]{:S(2)}) copy-start(s32[128,2]{0,1:T(2,128)} %param.6) | copy-start | bytes 3076
  6.4 19.9 %collective-permute-start = (bf16[2,4,4,64,512]{4,3,2,1,0:T(8,128)(2,1)}, bf16[2,4,4,64,512]{4,3,2,1,0:T(8,128)(2,1)S(1)}, u32[]{:S(2)}, u32[]{:S(2)}) collective-permute-start(bf16[2,4,4,64,512]{4,3,2,1,0:T(8,128)(2,1)} %dynamic-slice_select_fusion), channel_id=1, source_target_pairs={{0,1},{1,0},{2,3},{3,2},{4,5},{5,4},{6,7},{7,6},{8,9},{9,8},{10,11... | collective-permute-start | bytes 6291464 | tf_op jit(solution)/shard_map/ppermute | solution.py:30
  11.5 14.8 %collective-permute-start.1 = (bf16[2,4,4,192,128]{4,3,2,1,0:T(8,128)(2,1)S(1)}, bf16[2,4,4,192,128]{4,3,2,1,0:T(8,128)(2,1)S(1)}, u32[]{:S(2)}, u32[]{:S(2)}) collective-permute-start(bf16[2,4,4,192,128]{4,3,2,1,0:T(8,128)(2,1)S(1)} %pad_maximum_fusion), channel_id=1, source_target_pairs={{0,1},{1,0},{2,3},{3,2},{4,5},{5,4},{6,7},{7,6},{8,9},{9,8},{10,11... | collective-permute-start | bytes 4718600 | tf_op jit(solution)/shard_map/ppermute | solution.py:30
  12.0 32.3 %collective-permute-start.2 = (bf16[2,2,4,64,512]{4,3,2,1,0:T(8,128)(2,1)}, bf16[2,2,4,64,512]{4,3,2,1,0:T(8,128)(2,1)}, u32[]{:S(2)}, u32[]{:S(2)}) collective-permute-start(bf16[2,2,4,64,512]{4,3,2,1,0:T(8,128)(2,1)} %dynamic-slice_select_fusion.1.refs_2_), channel_id=1, source_target_pairs={{0,8},{8,16},{16,24},{24,32},{32,40},{40,48},{48,56},{56,64},{64,7... | collective-permute-start | bytes 3145736 | tf_op jit(solution)/shard_map/ppermute | solution.py:23
  15.9 52.2 %collective-permute-start.4 = (bf16[2,2,4,64,512]{4,3,2,1,0:T(8,128)(2,1)}, bf16[2,2,4,64,512]{4,3,2,1,0:T(8,128)(2,1)}, u32[]{:S(2)}, u32[]{:S(2)}) collective-permute-start(bf16[2,2,4,64,512]{4,3,2,1,0:T(8,128)(2,1)} %dynamic-slice_select_fusion.1.refs_2_), channel_id=1, source_target_pairs={{8,0},{16,8},{24,16},{32,24},{40,32},{48,40},{56,48},{64,56},{72,6... | collective-permute-start | bytes 3145736 | tf_op jit(solution)/shard_map/ppermute | solution.py:23
  23.1 51.1 %collective-permute-start.6 = (bf16[2,4,4,128,128]{4,3,2,1,0:T(8,128)(2,1)}, bf16[2,4,4,128,128]{4,3,2,1,0:T(8,128)(2,1)}, u32[]{:S(2)}, u32[]{:S(2)}) collective-permute-start(bf16[2,4,4,128,128]{4,3,2,1,0:T(8,128)(2,1)} %pad_maximum_fusion.4), channel_id=1, source_target_pairs={{0,4},{4,0},{1,5},{5,1},{2,6},{6,2},{3,7},{7,3},{8,12},{12,8},{9,1... | collective-permute-start | bytes 3145736 | tf_op jit(solution)/shard_map/ppermute | solution.py:30
  26.3 4.2 %copy-start.3 = (bf16[2,4,4,192,128]{4,3,2,1,0:T(8,128)(2,1)}, bf16[2,4,4,192,128]{4,3,2,1,0:T(8,128)(2,1)S(1)}, u32[]{:S(2)}) copy-start(bf16[2,4,4,192,128]{4,3,2,1,0:T(8,128)(2,1)S(1)} %collective-permute-done.1.refs_7_.refs_4_) | copy-start | bytes 4718596
  26.3 25.7 %copy-start = (bf16[2,4,4,64,512]{4,3,2,1,0:T(8,128)(2,1)}, bf16[2,4,4,64,512]{4,3,2,1,0:T(8,128)(2,1)S(1)}, u32[]{:S(2)}) copy-start(bf16[2,4,4,64,512]{4,3,2,1,0:T(8,128)(2,1)S(1)} %collective-permute-done.refs_3_) | copy-start | bytes 6291460
  27.5 38.7 %collective-permute-start.3 = (bf16[2,2,4,64,512]{4,3,2,1,0:T(8,128)(2,1)}, bf16[2,2,4,64,512]{4,3,2,1,0:T(8,128)(2,1)}, u32[]{:S(2)}, u32[]{:S(2)}) collective-permute-start(bf16[2,2,4,64,512]{4,3,2,1,0:T(8,128)(2,1)} %slice.75), channel_id=1, source_target_pairs={{0,8},{8,16},{16,24},{24,32},{32,40},{40,48},{48,56},{56,64},{64,7... | collective-permute-start | bytes 3145736 | tf_op jit(solution)/shard_map/ppermute | solution.py:23
  30.4 45.6 %collective-permute-start.7 = (bf16[2,4,4,128,128]{4,3,2,1,0:T(8,128)(2,1)}, bf16[2,4,4,128,128]{4,3,2,1,0:T(8,128)(2,1)}, u32[]{:S(2)}, u32[]{:S(2)}) collective-permute-start(bf16[2,4,4,128,128]{4,3,2,1,0:T(8,128)(2,1)} %pad_maximum_fusion.5), channel_id=1, source_target_pairs={{0,5},{1,4},{4,1},{5,0},{2,7},{3,6},{6,3},{7,2},{8,13},{9,12},{12,... | collective-permute-start | bytes 3145736 | tf_op jit(solution)/shard_map/ppermute | solution.py:30
  44.3 37.8 %collective-permute-start.5 = (bf16[2,2,4,64,512]{4,3,2,1,0:T(8,128)(2,1)}, bf16[2,2,4,64,512]{4,3,2,1,0:T(8,128)(2,1)}, u32[]{:S(2)}, u32[]{:S(2)}) collective-permute-start(bf16[2,2,4,64,512]{4,3,2,1,0:T(8,128)(2,1)} %slice.75), channel_id=1, source_target_pairs={{8,0},{16,8},{24,16},{32,24},{40,32},{48,40},{56,48},{64,56},{72,6... | collective-permute-start | bytes 3145736 | tf_op jit(solution)/shard_map/ppermute | solution.py:23
  53.2 36.1 %copy-start.1 = (bf16[2,1,8,64,512]{4,3,2,1,0:T(8,128)(2,1)}, bf16[2,1,8,64,512]{4,3,2,1,0:T(8,128)(2,1)S(1)}, u32[]{:S(2)}) copy-start(bf16[2,1,8,64,512]{4,3,2,1,0:T(8,128)(2,1)S(1)} %pad_maximum_fusion.3.refs_1_) | copy-start | bytes 3145732
  66.2 30.4 %collective-permute-start.8 = (bf16[2,1,8,64,512]{4,3,2,1,0:T(8,128)(2,1)}, bf16[2,1,8,64,512]{4,3,2,1,0:T(8,128)(2,1)}, u32[]{:S(2)}, u32[]{:S(2)}) collective-permute-start(bf16[2,1,8,64,512]{4,3,2,1,0:T(8,128)(2,1)} %pad_maximum_fusion.2.refs_1_), channel_id=1, source_target_pairs={{0,8},{8,16},{16,24},{24,32},{32,40},{40,48},{48,56},{56,64},{64,7... | collective-permute-start | bytes 3145736 | tf_op jit(solution)/shard_map/ppermute | solution.py:23
  68.1 29.9 %collective-permute-start.9 = (bf16[2,1,8,64,512]{4,3,2,1,0:T(8,128)(2,1)}, bf16[2,1,8,64,512]{4,3,2,1,0:T(8,128)(2,1)}, u32[]{:S(2)}, u32[]{:S(2)}) collective-permute-start(bf16[2,1,8,64,512]{4,3,2,1,0:T(8,128)(2,1)} %pad_maximum_fusion.2.refs_1_), channel_id=1, source_target_pairs={{8,0},{16,8},{24,16},{32,24},{40,32},{48,40},{56,48},{64,56},{72,6... | collective-permute-start | bytes 3145736 | tf_op jit(solution)/shard_map/ppermute | solution.py:23
  74.2 43.4 %collective-permute-start.10 = (bf16[2,1,8,64,512]{4,3,2,1,0:T(8,128)(2,1)S(1)}, bf16[2,1,8,64,512]{4,3,2,1,0:T(8,128)(2,1)}, u32[]{:S(2)}, u32[]{:S(2)}) collective-permute-start(bf16[2,1,8,64,512]{4,3,2,1,0:T(8,128)(2,1)S(1)} %pad_maximum_fusion.3.refs_1_), channel_id=1, source_target_pairs={{0,8},{8,16},{16,24},{24,32},{32,40},{40,48},{48,56},{56,64},{64,7... | collective-permute-start | bytes 3145736 | tf_op jit(solution)/shard_map/ppermute | solution.py:23
  76.1 42.5 %collective-permute-start.11 = (bf16[2,1,8,64,512]{4,3,2,1,0:T(8,128)(2,1)S(1)}, bf16[2,1,8,64,512]{4,3,2,1,0:T(8,128)(2,1)}, u32[]{:S(2)}, u32[]{:S(2)}) collective-permute-start(bf16[2,1,8,64,512]{4,3,2,1,0:T(8,128)(2,1)S(1)} %pad_maximum_fusion.3.refs_1_), channel_id=1, source_target_pairs={{8,0},{16,8},{24,16},{32,24},{40,32},{48,40},{56,48},{64,56},{72,6... | collective-permute-start | bytes 3145736 | tf_op jit(solution)/shard_map/ppermute | solution.py:23
  89.4 21.2 %all-to-all-start = ((s16[8,2,272,128]{3,2,1,0:T(8,128)(2,1)}), s16[8,2,272,128]{3,2,1,0:T(8,128)(2,1)S(1)}, u32[]{:S(2)}, u32[]{:S(2)}) async-start(s16[8,2,272,128]{3,2,1,0:T(8,128)(2,1)} %products.3), calls=%async_computation | async-start | bytes 2228224 | tf_op jit(solution)/shard_map/all_to_all | solution.py:225
  110.5 14.2 %all-to-all-start.1 = ((s16[8,1,272,128]{3,2,1,0:T(8,128)(2,1)}), s16[8,1,272,128]{3,2,1,0:T(8,128)(2,1)S(1)}, u32[]{:S(2)}, u32[]{:S(2)}) async-start(s16[8,1,272,128]{3,2,1,0:T(8,128)(2,1)} %products.4), calls=%async_computation.1 | async-start | bytes 1114112 | tf_op jit(solution)/shard_map/all_to_all | solution.py:225
  124.7 14.2 %all-to-all-start.2 = ((s16[8,1,272,128]{3,2,1,0:T(8,128)(2,1)}), s16[8,1,272,128]{3,2,1,0:T(8,128)(2,1)S(1)}, u32[]{:S(2)}, u32[]{:S(2)}) async-start(s16[8,1,272,128]{3,2,1,0:T(8,128)(2,1)} %products.5), calls=%async_computation.2 | async-start | bytes 1114112 | tf_op jit(solution)/shard_map/all_to_all | solution.py:225

commit v4 on v3

--- a/solution.py
+++ b/solution.py
@@ -13,6 +13,7 @@
 LOG = 256.0
 LEAST = 2.0**-126
 PAD = 16
+STEPS = 2
 SHOT = ("sup", "half")
 XLINE = ("side", "core")
 RING = ("half", "side", "core")
@@ -30,13 +31,9 @@
     return lax.ppermute(block, axes, [(i, n - 1 - i) for i in range(n)])
 
 
-def products_kernel(counts, place, *refs):
-    out = refs[-1]
-    groups, start = [], 0
-    for count in counts:
-        groups.append(refs[start : start + count])
-        start += count
-    windows, own, cross = groups[:3], groups[3], groups[4]
+def products_kernel(place, *refs):
+    out, total = refs[-2:]
+    windows, own, cross = (refs[0:2], refs[2:4], refs[4:6]), refs[6:8], refs[8:10]
     half = place[0]
     upper = half == 1
     pts, recv = windows[0][0].shape[3:]
@@ -66,13 +63,27 @@
         both = jnp.concatenate(both, axis=1).T
         real, imag = both[: 2 * shots], both[2 * shots :]
         lefts += [both, jnp.concatenate([-imag, real], axis=0)]
-        rights += [
-            [block[part, 0].reshape(-1, recv) for block in windows[k]] for part in range(2)
-        ]
+        rights += [block[part, 0].reshape(-1, recv) for part in range(2) for block in windows[k]]
     left = jnp.concatenate(lefts, axis=1)
-    right = jnp.concatenate([rows for side in rights for rows in side], axis=0)
-    width = recv // 4
-    total = jnp.dot(left, right, preferred_element_type=jnp.float32)
+    right = jnp.concatenate(rights, axis=0)
+    term = jnp.dot(left, right, preferred_element_type=jnp.float32)
+    step, last = pl.program_id(1), pl.num_programs(1) - 1
+
+    @pl.when(step == 0)
+    def _():
+        total[...] = term
+
+    @pl.when((step > 0) & (step < last))
+    def _():
+        total[...] += term
+
+    @pl.when(step == last)
+    def _():
+        encode(half, total[...] + term, out)
+
+
+def encode(half, total, out):
+    shots, width = total.shape[0] // 4, total.shape[1] // 4
     for quarter in range(4):
         columns = total[:, quarter * width : (quarter + 1) * width]
         for block, to in enumerate((half, 1 - half)):
@@ -93,23 +104,28 @@
 
 
 def products(place, freqs, *groups):
+    groups = [group if len(group) == 2 else group * 2 for group in groups]
     arrays, starts = zip(*(block for group in groups for block in group))
     recv, shots = arrays[0].shape[4], arrays[-1].shape[4]
-    rows = sum(array.shape[2] * array.shape[3] for array in arrays[: sum(map(len, groups[:3]))])
+    xs = arrays[-1].shape[2]
+    rows = 6 * xs * arrays[0].shape[3]
     first, count = freqs
-
-    def spec(array, start):
-        if array.shape[1] == count == 1:
-            return pl.BlockSpec(memory_space=pltpu.VMEM)
-        return pl.BlockSpec((2, 1) + array.shape[2:], lambda f: (0, f + first - start, 0, 0, 0))
+    step = xs // STEPS
+
+    def spec(array, start, which):
+        skip = which * STEPS if array.shape[2] > xs else 0
+        return pl.BlockSpec(
+            (2, 1, step) + array.shape[3:], lambda f, x: (0, f + first - start, x + skip, 0, 0)
+        )
 
     return pl.pallas_call(
-        functools.partial(products_kernel, [len(group) for group in groups]),
-        grid=(count,),
+        products_kernel,
+        grid=(count, STEPS),
         in_specs=[pl.BlockSpec(memory_space=pltpu.SMEM)]
-        + [spec(*block) for block in zip(arrays, starts)],
-        out_specs=pl.BlockSpec((8, 1, 2 * shots + PAD, recv // 4), lambda f: (0, f, 0, 0)),
+        + [spec(*block, i % 2) for i, block in enumerate(zip(arrays, starts))],
+        out_specs=pl.BlockSpec((8, 1, 2 * shots + PAD, recv // 4), lambda f, x: (0, f, 0, 0)),
         out_shape=jax.ShapeDtypeStruct((8, count, 2 * shots + PAD, recv // 4), jnp.int16),
+        scratch_shapes=[pltpu.VMEM((4 * shots, recv), jnp.float32)],
         compiler_params=pltpu.CompilerParams(vmem_limit_bytes=58 * 2**20),
         cost_estimate=pl.CostEstimate(
             flops=COST * count * 2 * (4 * shots) * (2 * rows) * recv,
@@ -158,68 +174,176 @@
     )(terms, *done)
 
 
+def mute_kernel(place, live, mine, others, early, leaving, kept):
+    step = pl.program_id(0)
+    xs, pts, recv = kept.shape
+
+    @pl.when(step == 0)
+    def _():
+        rows = lax.broadcasted_iota(jnp.int32, (pts, pts), 0)
+        diagonal = rows == lax.broadcasted_iota(jnp.int32, (pts, pts), 1)
+        receiver = lax.broadcasted_iota(jnp.int32, (pts, recv), 1).astype(jnp.float32)
+        for x in range(xs):
+            row = jnp.broadcast_to(live[x : x + 1, :].astype(jnp.float32), (pts, pts))
+            column = jnp.sum(jnp.where(diagonal, row, 0.0), axis=1, keepdims=True)
+            kept[x] = (receiver < column).astype(jnp.float32).astype(kept.dtype)
+        for part in range(2):
+            for freq in range(early.shape[1]):
+                early[part, freq] = mine[part, freq] * kept[...]
+
+    for part in range(2):
+        for freq in range(leaving.shape[1]):
+            leaving[part, freq] = others[part, freq] * kept[...]
+
+
+def mute(place, gathers, live):
+    freqs, xs, pts, recv = gathers.shape[1:]
+    count = freqs // 2
+    block = (2, FIRST, xs, pts, recv)
+
+    def array(size):
+        return jax.ShapeDtypeStruct((2, size, xs, pts, recv), gathers.dtype)
+
+    return pl.pallas_call(
+        mute_kernel,
+        grid_spec=pltpu.PrefetchScalarGridSpec(
+            num_scalar_prefetch=1,
+            grid=(count // FIRST,),
+            in_specs=[
+                pl.BlockSpec((xs, pts), lambda i, place: (0, 0)),
+                pl.BlockSpec(block, lambda i, place: (0, place[1] * (count // FIRST), 0, 0, 0)),
+                pl.BlockSpec(
+                    block, lambda i, place: (0, (1 - place[1]) * (count // FIRST) + i, 0, 0, 0)
+                ),
+            ],
+            out_specs=[
+                pl.BlockSpec(block, lambda i, place: (0, 0, 0, 0, 0)),
+                pl.BlockSpec(block, lambda i, place: (0, i, 0, 0, 0)),
+            ],
+            scratch_shapes=[pltpu.VMEM((xs, pts, recv), gathers.dtype)],
+        ),
+        out_shape=[array(FIRST), array(count)],
+        compiler_params=pltpu.CompilerParams(vmem_limit_bytes=58 * 2**20),
+        cost_estimate=pl.CostEstimate(flops=0, bytes_accessed=6 * 2**20, transcendentals=0),
+        name="mute",
+    )(place, live, gathers, gathers)
+
+
+def mask_kernel(plan, place, aperture, *refs):
+    inside = refs[-1]
+    spread, shots = inside.shape
+    pts = spread // 5
+
+    @pl.when(pl.program_id(0) == 0)
+    def _():
+        inline = place[2] + lax.broadcasted_iota(jnp.int32, (spread, shots), 0)
+        within = (inline >= aperture[0:1, :]) & (inline < aperture[1:2, :])
+        inside[...] = within.astype(jnp.float32).astype(inside.dtype)
+
+    for source, piece, to, at, offset in plan:
+        kept = inside[offset * pts : (offset + 1) * pts, :]
+        for part in range(2):
+            for freq in range(refs[source].shape[1]):
+                refs[to][part, freq, :, at * pts : (at + 1) * pts, :] = (
+                    refs[source][part, freq, :, piece * pts : (piece + 1) * pts, :] * kept
+                )
+
+
+def mask(place, shots, aperture, plan, sources, outputs):
+    freqs, xs, spread, width = shots.shape[1:]
+    count, pts = freqs // 2, spread // 5
+    steps, size = count // FIRST, FIRST
+
+    def source(other, at, pieces):
+        def index(i, place):
+            return (0, (place[1] ^ other) * steps + i, 0, at, 0)
+
+        return pl.BlockSpec((2, size, xs, pieces * pts, width), index)
+
+    moved = (sum(pieces for _, _, pieces in sources) + sum(outputs)) * 2**19
+    return pl.pallas_call(
+        functools.partial(mask_kernel, plan),
+        grid_spec=pltpu.PrefetchScalarGridSpec(
+            num_scalar_prefetch=1,
+            grid=(steps,),
+            in_specs=[pl.BlockSpec((2, width), lambda i, place: (0, 0))]
+            + [source(*block) for block in sources],
+            out_specs=[
+                pl.BlockSpec((2, size, xs, pieces * pts, width), lambda i, place: (0, i, 0, 0, 0))
+                for pieces in outputs
+            ],
+            scratch_shapes=[pltpu.VMEM((spread, width), shots.dtype)],
+        ),
+        out_shape=[
+            jax.ShapeDtypeStruct((2, count, xs, pieces * pts, width), shots.dtype)
+            for pieces in outputs
+        ],
+        compiler_params=pltpu.CompilerParams(vmem_limit_bytes=58 * 2**20),
+        cost_estimate=pl.CostEstimate(flops=0, bytes_accessed=moved, transcendentals=0),
+        name="mask",
+    )(place, aperture, *[shots] * len(sources))
+
+
 def on_device(surface_gathers, source_gathers, aperture, live):
-    freqs_here, _, pts, recv = surface_gathers.shape[1:]
+    freqs_here, _, pts, _ = surface_gathers.shape[1:]
     spread = source_gathers.shape[4]
     half, core = lax.axis_index("half"), lax.axis_index("core")
-    place = half.astype(jnp.int32).reshape(1)
     count = freqs_here // 2
+    first_point = (2 * lax.axis_index("sup") + half) * pts - (spread - pts) // 2
+    place = jnp.stack([half, core, first_point]).astype(jnp.int32)
+
+    early, leaving = mute(place, surface_gathers, live)
+    below_early, above_early = shifted(early, 1), shifted(early, -1)
+    shots = source_gathers.transpose(0, 1, 3, 4, 2)
+    crossing, cross_leaving, shots_leaving = mask(
+        place,
+        shots,
+        aperture.T,
+        ((0, 0, 3, 0, 1), (1, 0, 3, 1, 3), (2, 1, 4, 0, 1), (2, 3, 4, 1, 3))
+        + tuple((2, 2 * k, 5, k, 2 * k) for k in range(3)),
+        ((0, 1, 1), (0, 3, 1), (1, 0, 5)),
+        (2, 2, 3),
+    )
+    cross = [(swapped(crossing, "half"), 0), (swapped(cross_leaving, ("half", "core")), 0)]
+    gathers = swapped(leaving, "core")
+    others = swapped(shots_leaving, "core")
+    gathers, others, surface_gathers, shots = lax.optimization_barrier(
+        (gathers, others, surface_gathers, shots)
+    )
+    (staying,) = mask(
+        place,
+        shots,
+        aperture.T,
+        tuple((k, 0, 3, k, 2 * k) for k in range(3)),
+        ((0, 0, 1), (0, 2, 1), (0, 4, 1)),
+        (3,),
+    )
     heard = lax.broadcasted_iota(jnp.int32, surface_gathers.shape[2:], 2) < live[:, :, None]
-    first_point = (2 * lax.axis_index("sup") + half) * pts - (spread - pts) // 2
-    inline = first_point + lax.broadcasted_iota(jnp.int32, (spread, aperture.shape[0]), 0)
-    inside = (inline >= aperture[:, 0][None, :]) & (inline < aperture[:, 1][None, :])
-    shots = source_gathers.transpose(0, 1, 3, 4, 2)
-
-    def of_core(array, which, first, size):
-        return lax.dynamic_slice_in_dim(array, which * count + first, size, 1)
-
-    def muted(gathers, which, first, size):
-        gathers = of_core(gathers, which, first, size)
-        return jnp.where(heard, gathers, jnp.zeros((), gathers.dtype))
-
-    def pieces(block, which):
-        spans = [slice(k * pts, (k + 1) * pts) for k in which]
-        return jnp.concatenate(
-            [
-                jnp.where(inside[span], block[:, :, :, span], jnp.zeros((), block.dtype))
-                for span in spans
-            ],
-            axis=3,
-        )
-
-    early = muted(surface_gathers, core, 0, FIRST)
-    early, surface_gathers, shots = lax.optimization_barrier((early, surface_gathers, shots))
-    below_early, above_early = shifted(early, 1), shifted(early, -1)
-
-    mine, others = of_core(shots, core, 0, count), of_core(shots, 1 - core, 0, count)
-    cross = [
-        (swapped(pieces(mine, (1, 3)), "half"), 0),
-        (swapped(pieces(others, (1, 3)), ("half", "core")), 0),
-    ]
-    gathers = swapped(muted(surface_gathers, 1 - core, 0, count), "core")
-    others = swapped(pieces(others, (0, 2, 4)), "core")
-    gathers, others = lax.optimization_barrier((gathers, others))
-    own = [(pieces(mine, (0, 2, 4)), 0), (others, 0)]
+    late = lax.dynamic_slice_in_dim(surface_gathers, core * count + FIRST, count - FIRST, 1)
+    late = jnp.where(heard, late, jnp.zeros((), late.dtype))
     early_too = gathers[:, :FIRST]
     below_too, above_too = shifted(early_too, 1), shifted(early_too, -1)
-    arrived = [below_early, below_too]
-    here, below, above = [], [], []
-    for i in range(FIRST, count):
-        block = muted(surface_gathers, core, i, 1)
-        block = jnp.concatenate([block, gathers[:, i : i + 1]], axis=2)
-        block, arrived[i - FIRST] = lax.optimization_barrier((block, arrived[i - FIRST]))
-        here.append([(block, i)])
-        below.append([(shifted(block, 1), i)])
-        above.append([(shifted(block, -1), i)])
-    here.insert(0, [(early, 0), (gathers, 0)])
-    below.insert(0, [(block, 0) for block in arrived])
-    above.insert(0, [(above_early, 0), (above_too, 0)])
-
+    own = [(staying, 0), (others, 0)]
+    here, below, above = [[(early, 0), (gathers, 0)]], [], []
+    arrived = [below_early, above_early]
     spans = [(0, FIRST)] + [(i, 1) for i in range(FIRST, count)]
-    partial = [
-        products(place, freqs, below[i], here[i], above[i], own, cross)
-        for i, freqs in enumerate(spans)
-    ]
+    partial = []
+    for i, (first, size) in enumerate(spans):
+        if i:
+            block = jnp.concatenate(
+                [late[:, first - FIRST : first - FIRST + 1], gathers[:, first : first + 1]], axis=2
+            )
+            if i == 1:
+                block, arrived = lax.optimization_barrier((block, arrived))
+                below.append([(arrived[0], 0), (below_too, 0)])
+                above.append([(arrived[1], 0), (above_too, 0)])
+                partial.append(products(place, spans[0], below[0], here[0], above[0], own, cross))
+            else:
+                block, partial[i - 2] = lax.optimization_barrier((block, partial[i - 2]))
+            here.append([(block, first)])
+            below.append([(shifted(block, 1), first)])
+            above.append([(shifted(block, -1), first)])
+            partial.append(products(place, spans[i], below[i], here[i], above[i], own, cross))
     predicted = None
     for i, freqs in enumerate(spans):
         terms = lax.all_to_all(partial[i], RING, 0, 0, tiled=True)

time: 140 us -> 138 us (0.986)
  other arithmetic: 18.3 us -> 3.35 us
  Pallas kernels: 20.1 us -> 32.3 us
    ppermute x8, waiting for transfers between devices: 35.6 us -> 21.9 us  [shifted(): lax.ppermute(block, 'sup', [(i, i + distance) for i in range(n) if 0 <= i...]
    pallas_call x3 -> x6, Pallas kernels: 17.4 us -> 29.6 us  [the longest x3 17.8 us: products(): pl.pallas_call(products_kernel, grid=(count, STEPS), in_specs=[pl.BlockSp...]
    select_n x4 -> x1, other arithmetic: 11.6 us -> 1.36 us  [on_device(): late = jnp.where(heard, late, jnp.zeros((), late.dtype))]
    ppermute x4, waiting for transfers between devices: 0.01 us -> 8.24 us  [swapped(): return lax.ppermute(block, axes, [(i, n - 1 - i) for i in range(n)])]
    all_to_all x3, waiting for transfers between devices: 17.1 us -> 22.4 us  [on_device(): terms = lax.all_to_all(partial[i], RING, 0, 0, tiled=True)]
    concatenate x6 -> x2, other arithmetic: 5.78 us -> 1.2 us  [on_device(): jnp.concatenate([late[:, first - FIRST:first - FIRST + 1], gathers[:, fir...]
  transfers between devices with their start and end apart: 15 -> 15, of which waited for: 9 -> 8; matrix products, arithmetic and copies ran while one was open for 9% -> 3% of each run, Pallas kernels for 14% -> 20%
where the time goes in v4:
time: 138 us; the launch traced here: 137 us
  waiting for transfers between devices  52.5 us (38%)
  starting transfers between devices  47.2 us (34%)
  Pallas kernels  32.3 us (23%)
  other arithmetic  3.35 us (2%)
    ppermute x8, starting transfers between devices, shifted(): lax.ppermute(block, 'sup', [(i, i + distance) for i in range(n) if 0 <= i...  31.7 us
    all_to_all x3, waiting for transfers between devices, on_device(): terms = lax.all_to_all(partial[i], RING, 0, 0, tiled=True)  22.4 us
    ppermute x8, waiting for transfers between devices, shifted(): lax.ppermute(block, 'sup', [(i, i + distance) for i in range(n) if 0 <= i...  21.9 us
    pallas_call x3, Pallas kernels, products(): pl.pallas_call(products_kernel, grid=(count, STEPS), in_specs=[pl.BlockSp...  17.8 us
    all_to_all x3, starting transfers between devices, on_device(): terms = lax.all_to_all(partial[i], RING, 0, 0, tiled=True)  11.6 us
    ppermute x4, waiting for transfers between devices, swapped(): return lax.ppermute(block, axes, [(i, n - 1 - i) for i in range(n)])  8.24 us
    pallas_call x2, Pallas kernels, mask(): pl.pallas_call(functools.partial(mask_kernel, plan), grid_spec=pltpu.Pref...  7.55 us
    pallas_call x1, Pallas kernels, mute(): pl.pallas_call(mute_kernel, grid_spec=pltpu.PrefetchScalarGridSpec(num_sc...  4.25 us
  transfers between devices with their start and end apart: 15, of which 8 were waited for; matrix products, arithmetic and copies ran while one was open for 3% of the time, Pallas kernels for 20%

profile of v4, /device:TPU:6, one launch (start us, length us, event | category | flops | bytes accessed | tf_op | source)
XLA Modules:
  0.0 136.8 jit_solution(12918483041389536967)
XLA Ops:
  0.7 4.2 %mute.1 = (bf16[2,2,4,64,512]{4,3,2,1,0:T(8,128)(2,1)}, bf16[2,4,4,64,512]{4,3,2,1,0:T(8,128)(2,1)}) custom-call(s32[3]{0:T(128)} %pad_add_fusion.place, s32[4,64]{1,0:T(4,128)} %live.1, bf16[2,8,4,64,512]{4,3,2,1,0:T(8,128)(2,1)} %others.1, bf16[2,8,4,64,512]{4,3,2,1,0:T(8,128)(2,1)} %others.1), custom_call_target="tpu_custom_call" | custom-call | bytes 6291456 | tf_op jit(solution)/shard_map/mute/pallas_call | solution.py:207
  4.9 4.4 %mask.2 = (bf16[2,4,4,128,128]{4,3,2,1,0:T(8,128)(2,1)}, bf16[2,4,4,128,128]{4,3,2,1,0:T(8,128)(2,1)}, bf16[2,4,4,192,128]{4,3,2,1,0:T(8,128)(2,1)}) custom-call(s32[3]{0:T(128)} %pad_add_fusion.place, s32[2,128]{1,0:T(2,128)} %bitcast.12, bf16[2,8,4,320,128]{4,3,2,1,0:T(8,128)(2,1)} %bitcast.6, bf16[2,8,4,320,128]{4,3,2,1,0:T(8,128)(2,1)} %bitcast.7, ...), custom_call_target="tpu_custom_call" | custom-call | bytes 7340032 | tf_op jit(solution)/shard_map/mask/pallas_call | solution.py:264
  9.9 3.8 %collective-permute-start.2 = (bf16[2,2,4,64,512]{4,3,2,1,0:T(8,128)(2,1)}, bf16[2,2,4,64,512]{4,3,2,1,0:T(8,128)(2,1)}, u32[]{:S(2)}, u32[]{:S(2)}) collective-permute-start(bf16[2,2,4,64,512]{4,3,2,1,0:T(8,128)(2,1)} %get-tuple-element.27.refs_2_), channel_id=1, source_target_pairs={{0,8},{8,16},{16,24},{24,32},{32,40},{40,48},{48,56},{56,64},{64,7... | collective-permute-start | bytes 3145736 | tf_op jit(solution)/shard_map/ppermute | solution.py:24
  13.7 6.1 %collective-permute-start.3 = (bf16[2,2,4,64,512]{4,3,2,1,0:T(8,128)(2,1)}, bf16[2,2,4,64,512]{4,3,2,1,0:T(8,128)(2,1)}, u32[]{:S(2)}, u32[]{:S(2)}) collective-permute-start(bf16[2,2,4,64,512]{4,3,2,1,0:T(8,128)(2,1)} %get-tuple-element.27.refs_2_), channel_id=1, source_target_pairs={{8,0},{16,8},{24,16},{32,24},{40,32},{48,40},{56,48},{64,56},{72,6... | collective-permute-start | bytes 3145736 | tf_op jit(solution)/shard_map/ppermute | solution.py:24
  19.8 3.3 %collective-permute-start.6 = (bf16[2,4,4,128,128]{4,3,2,1,0:T(8,128)(2,1)}, bf16[2,4,4,128,128]{4,3,2,1,0:T(8,128)(2,1)S(1)}, u32[]{:S(2)}, u32[]{:S(2)}) collective-permute-start(bf16[2,4,4,128,128]{4,3,2,1,0:T(8,128)(2,1)} %get-tuple-element.32), channel_id=1, source_target_pairs={{0,4},{4,0},{1,5},{5,1},{2,6},{6,2},{3,7},{7,3},{8,12},{12,8},{9,1... | collective-permute-start | bytes 3145736 | tf_op jit(solution)/shard_map/ppermute | solution.py:31
  23.4 1.1 slice.19
  24.5 1.9 %collective-permute-start.4 = (bf16[2,2,4,64,512]{4,3,2,1,0:T(8,128)(2,1)}, bf16[2,2,4,64,512]{4,3,2,1,0:T(8,128)(2,1)}, u32[]{:S(2)}, u32[]{:S(2)}) collective-permute-start(bf16[2,2,4,64,512]{4,3,2,1,0:T(8,128)(2,1)} %slice.19), channel_id=1, source_target_pairs={{0,8},{8,16},{16,24},{24,32},{32,40},{40,48},{48,56},{56,64},{64,7... | collective-permute-start | bytes 3145736 | tf_op jit(solution)/shard_map/ppermute | solution.py:24
  26.4 15.7 %collective-permute-done.2.refs_0_ = bf16[2,2,4,64,512]{4,3,2,1,0:T(8,128)(2,1)} collective-permute-done((bf16[2,2,4,64,512]{4,3,2,1,0:T(8,128)(2,1)}, bf16[2,2,4,64,512]{4,3,2,1,0:T(8,128)(2,1)}, u32[]{:S(2)}, u32[]{:S(2)}) %collective-permute-start.2) | collective-permute-done | bytes 1048608 | tf_op jit(solution)/shard_map/ppermute | solution.py:24
  42.1 4.0 %collective-permute-start.5 = (bf16[2,2,4,64,512]{4,3,2,1,0:T(8,128)(2,1)}, bf16[2,2,4,64,512]{4,3,2,1,0:T(8,128)(2,1)}, u32[]{:S(2)}, u32[]{:S(2)}) collective-permute-start(bf16[2,2,4,64,512]{4,3,2,1,0:T(8,128)(2,1)} %slice.19), channel_id=1, source_target_pairs={{8,0},{16,8},{24,16},{32,24},{40,32},{48,40},{56,48},{64,56},{72,6... | collective-permute-start | bytes 3145736 | tf_op jit(solution)/shard_map/ppermute | solution.py:24
  46.1 1.4 dynamic-slice_select_fusion
  47.7 1.1 pad_maximum_fusion.1.refs_2_.refs_3_
  48.8 3.1 %mask.3.refs_6_ = bf16[2,4,4,192,128]{4,3,2,1,0:T(8,128)(2,1)} custom-call(s32[3]{0:T(128)} %pad_add_fusion.place, s32[2,128]{1,0:T(2,128)} %bitcast.13, bf16[2,8,4,320,128]{4,3,2,1,0:T(8,128)(2,1)} %bitcast.9, bf16[2,8,4,320,128]{4,3,2,1,0:T(8,128)(2,1)} %bitcast.10, bf16[2,8,4,320,128]{4,3,2,1,0:T(8,128)(2,1)} %bitcast.11), custom_call_target="tpu_custom_call" | custom-call | bytes 3145728 | tf_op jit(solution)/shard_map/mask/pallas_call | solution.py:264
  51.9 1.9 %collective-permute-start.8 = (bf16[2,1,8,64,512]{4,3,2,1,0:T(8,128)(2,1)}, bf16[2,1,8,64,512]{4,3,2,1,0:T(8,128)(2,1)}, u32[]{:S(2)}, u32[]{:S(2)}) collective-permute-start(bf16[2,1,8,64,512]{4,3,2,1,0:T(8,128)(2,1)} %pad_maximum_fusion.1.refs_2_.refs_3_), channel_id=1, source_target_pairs={{0,8},{8,16},{16,24},{24,32},{32,40},{40,48},{48,56},{56,64},{64,7... | collective-permute-start | bytes 3145736 | tf_op jit(solution)/shard_map/ppermute | solution.py:24
  53.9 6.0 %collective-permute-start.9 = (bf16[2,1,8,64,512]{4,3,2,1,0:T(8,128)(2,1)}, bf16[2,1,8,64,512]{4,3,2,1,0:T(8,128)(2,1)}, u32[]{:S(2)}, u32[]{:S(2)}) collective-permute-start(bf16[2,1,8,64,512]{4,3,2,1,0:T(8,128)(2,1)} %pad_maximum_fusion.1.refs_2_.refs_3_), channel_id=1, source_target_pairs={{8,0},{16,8},{24,16},{32,24},{40,32},{48,40},{56,48},{64,56},{72,6... | collective-permute-start | bytes 3145736 | tf_op jit(solution)/shard_map/ppermute | solution.py:24
  60.0 8.2 %collective-permute-done.7.refs_9_ = bf16[2,4,4,128,128]{4,3,2,1,0:T(8,128)(2,1)} collective-permute-done((bf16[2,4,4,128,128]{4,3,2,1,0:T(8,128)(2,1)}, bf16[2,4,4,128,128]{4,3,2,1,0:T(8,128)(2,1)}, u32[]{:S(2)}, u32[]{:S(2)}) %collective-permute-start.7) | collective-permute-done | bytes 1048608 | tf_op jit(solution)/shard_map/ppermute | solution.py:31
  68.2 2.2 %collective-permute-done.5.refs_5_ = bf16[2,2,4,64,512]{4,3,2,1,0:T(8,128)(2,1)} collective-permute-done((bf16[2,2,4,64,512]{4,3,2,1,0:T(8,128)(2,1)}, bf16[2,2,4,64,512]{4,3,2,1,0:T(8,128)(2,1)}, u32[]{:S(2)}, u32[]{:S(2)}) %collective-permute-start.5) | collective-permute-done | bytes 1048608 | tf_op jit(solution)/shard_map/ppermute | solution.py:24
  70.4 8.1 %products.3 = s16[8,2,272,128]{3,2,1,0:T(8,128)(2,1)} custom-call(s32[3]{0:T(128)} %pad_add_fusion.place, bf16[2,2,4,64,512]{4,3,2,1,0:T(8,128)(2,1)} %collective-permute-done.2.refs_0_, bf16[2,2,4,64,512]{4,3,2,1,0:T(8,128)(2,1)} %collective-permute-done.4.refs_1_, bf16[2,2,4,64,512]{4,3,2,1,0:T(8,128)(2,1)} %get-tuple-element.27.refs_2_, ...), custom_call_target="tpu_custom_call" | custom-call | flops 38654705664 | bytes 1048576 | tf_op jit(solution)/shard_map/products/pallas_call | solution.py:121
  78.5 1.9 %collective-permute-start.10 = (bf16[2,1,8,64,512]{4,3,2,1,0:T(8,128)(2,1)S(1)}, bf16[2,1,8,64,512]{4,3,2,1,0:T(8,128)(2,1)}, u32[]{:S(2)}, u32[]{:S(2)}) collective-permute-start(bf16[2,1,8,64,512]{4,3,2,1,0:T(8,128)(2,1)S(1)} %pad_maximum_fusion.refs_2_.refs_3_), channel_id=1, source_target_pairs={{0,8},{8,16},{16,24},{24,32},{32,40},{40,48},{48,56},{56,64},{64,7... | collective-permute-start | bytes 3145736 | tf_op jit(solution)/shard_map/ppermute | solution.py:24
  80.4 6.1 %collective-permute-start.11 = (bf16[2,1,8,64,512]{4,3,2,1,0:T(8,128)(2,1)S(1)}, bf16[2,1,8,64,512]{4,3,2,1,0:T(8,128)(2,1)}, u32[]{:S(2)}, u32[]{:S(2)}) collective-permute-start(bf16[2,1,8,64,512]{4,3,2,1,0:T(8,128)(2,1)S(1)} %pad_maximum_fusion.refs_2_.refs_3_), channel_id=1, source_target_pairs={{8,0},{16,8},{24,16},{32,24},{40,32},{48,40},{56,48},{64,56},{72,6... | collective-permute-start | bytes 3145736 | tf_op jit(solution)/shard_map/ppermute | solution.py:24
  86.5 4.5 %all-to-all-start = ((s16[8,2,272,128]{3,2,1,0:T(8,128)(2,1)}), s16[8,2,272,128]{3,2,1,0:T(8,128)(2,1)S(1)}, u32[]{:S(2)}, u32[]{:S(2)}) async-start(s16[8,2,272,128]{3,2,1,0:T(8,128)(2,1)} %products.3), calls=%async_computation | async-start | bytes 2228224 | tf_op jit(solution)/shard_map/all_to_all | solution.py:349
  91.0 1.9 %collective-permute-done.9.refs_4_.refs_5_ = bf16[2,1,8,64,512]{4,3,2,1,0:T(8,128)(2,1)} collective-permute-done((bf16[2,1,8,64,512]{4,3,2,1,0:T(8,128)(2,1)}, bf16[2,1,8,64,512]{4,3,2,1,0:T(8,128)(2,1)}, u32[]{:S(2)}, u32[]{:S(2)}) %collective-permute-start.9) | collective-permute-done | bytes 1048608 | tf_op jit(solution)/shard_map/ppermute | solution.py:24
  92.9 4.9 %products.4 = s16[8,1,272,128]{3,2,1,0:T(8,128)(2,1)} custom-call(s32[3]{0:T(128)} %pad_add_fusion.place, bf16[2,1,8,64,512]{4,3,2,1,0:T(8,128)(2,1)} %collective-permute-done.8.refs_0_.refs_1_, bf16[2,1,8,64,512]{4,3,2,1,0:T(8,128)(2,1)} %collective-permute-done.8.refs_0_.refs_1_, bf16[2,1,8,64,512]{4,3,2,1,0:T(8,128)(2,1)} %pad_maximum_fusion.1.refs_2_.refs_3_, ...), custom_call_target="tpu_custom_call" | custom-call | flops 19327352832 | bytes 1048576 | tf_op jit(solution)/shard_map/products/pallas_call | solution.py:121
  97.8 9.9 %all-to-all-done.terms = s16[8,2,272,128]{3,2,1,0:T(8,128)(2,1)S(1)} async-done(((s16[8,2,272,128]{3,2,1,0:T(8,128)(2,1)}), s16[8,2,272,128]{3,2,1,0:T(8,128)(2,1)S(1)}, u32[]{:S(2)}, u32[]{:S(2)}) %all-to-all-start) | async-done | bytes 1114144 | tf_op jit(solution)/shard_map/all_to_all | solution.py:349
  107.7 3.5 %all-to-all-start.1 = ((s16[8,1,272,128]{3,2,1,0:T(8,128)(2,1)}), s16[8,1,272,128]{3,2,1,0:T(8,128)(2,1)S(1)}, u32[]{:S(2)}, u32[]{:S(2)}) async-start(s16[8,1,272,128]{3,2,1,0:T(8,128)(2,1)} %products.4), calls=%async_computation.1 | async-start | bytes 1114112 | tf_op jit(solution)/shard_map/all_to_all | solution.py:349
  111.2 2.0 %collective-permute-done.11.refs_4_.refs_5_ = bf16[2,1,8,64,512]{4,3,2,1,0:T(8,128)(2,1)} collective-permute-done((bf16[2,1,8,64,512]{4,3,2,1,0:T(8,128)(2,1)S(1)}, bf16[2,1,8,64,512]{4,3,2,1,0:T(8,128)(2,1)}, u32[]{:S(2)}, u32[]{:S(2)}) %collective-permute-start.11) | collective-permute-done | bytes 1048608 | tf_op jit(solution)/shard_map/ppermute | solution.py:24
  113.2 4.9 %products.5 = s16[8,1,272,128]{3,2,1,0:T(8,128)(2,1)} custom-call(s32[3]{0:T(128)} %pad_add_fusion.place, bf16[2,1,8,64,512]{4,3,2,1,0:T(8,128)(2,1)} %collective-permute-done.10.refs_0_.refs_1_, bf16[2,1,8,64,512]{4,3,2,1,0:T(8,128)(2,1)} %collective-permute-done.10.refs_0_.refs_1_, bf16[2,1,8,64,512]{4,3,2,1,0:T(8,128)(2,1)} %copy-done.1, ...), custom_call_target="tpu_custom_call" | custom-call | flops 19327352832 | bytes 1048576 | tf_op jit(solution)/shard_map/products/pallas_call | solution.py:121
  118.1 3.7 %all-to-all-done.1.terms = s16[8,1,272,128]{3,2,1,0:T(8,128)(2,1)S(1)} async-done(((s16[8,1,272,128]{3,2,1,0:T(8,128)(2,1)}), s16[8,1,272,128]{3,2,1,0:T(8,128)(2,1)S(1)}, u32[]{:S(2)}, u32[]{:S(2)}) %all-to-all-start.1) | async-done | bytes 557088 | tf_op jit(solution)/shard_map/all_to_all | solution.py:349
  121.8 3.5 %all-to-all-start.2 = ((s16[8,1,272,128]{3,2,1,0:T(8,128)(2,1)}), s16[8,1,272,128]{3,2,1,0:T(8,128)(2,1)S(1)}, u32[]{:S(2)}, u32[]{:S(2)}) async-start(s16[8,1,272,128]{3,2,1,0:T(8,128)(2,1)} %products.5), calls=%async_computation.2 | async-start | bytes 1114112 | tf_op jit(solution)/shard_map/all_to_all | solution.py:349
  125.4 1.1 finish.3.refs_0_
  126.4 0.8 finish.4.refs_0_
  127.2 8.8 %all-to-all-done.2.terms = s16[8,1,272,128]{3,2,1,0:T(8,128)(2,1)S(1)} async-done(((s16[8,1,272,128]{3,2,1,0:T(8,128)(2,1)}), s16[8,1,272,128]{3,2,1,0:T(8,128)(2,1)S(1)}, u32[]{:S(2)}, u32[]{:S(2)}) %all-to-all-start.2) | async-done | bytes 557088 | tf_op jit(solution)/shard_map/all_to_all | solution.py:349
  136.0 0.8 finish.5
  (23 shorter events, 1.7 us)
Async XLA Ops:
  4.9 18.4 %collective-permute-start = (bf16[2,4,4,64,512]{4,3,2,1,0:T(8,128)(2,1)}, bf16[2,4,4,64,512]{4,3,2,1,0:T(8,128)(2,1)S(1)}, u32[]{:S(2)}, u32[]{:S(2)}) collective-permute-start(bf16[2,4,4,64,512]{4,3,2,1,0:T(8,128)(2,1)} %get-tuple-element.23), channel_id=1, source_target_pairs={{0,1},{1,0},{2,3},{3,2},{4,5},{5,4},{6,7},{7,6},{8,9},{9,8},{10,11... | collective-permute-start | bytes 6291464 | tf_op jit(solution)/shard_map/ppermute | solution.py:31
  4.9 18.2 %copy-start.2 = (s32[4,64]{1,0:T(4,128)S(1)}, s32[4,64]{1,0:T(4,128)}, u32[]{:S(2)}) copy-start(s32[4,64]{1,0:T(4,128)} %live.1) | copy-start | bytes 3076
  9.4 13.9 %collective-permute-start.1 = (bf16[2,4,4,192,128]{4,3,2,1,0:T(8,128)(2,1)}, bf16[2,4,4,192,128]{4,3,2,1,0:T(8,128)(2,1)}, u32[]{:S(2)}, u32[]{:S(2)}) collective-permute-start(bf16[2,4,4,192,128]{4,3,2,1,0:T(8,128)(2,1)} %get-tuple-element.24), channel_id=1, source_target_pairs={{0,1},{1,0},{2,3},{3,2},{4,5},{5,4},{6,7},{7,6},{8,9},{9,8},{10,11... | collective-permute-start | bytes 4718600 | tf_op jit(solution)/shard_map/ppermute | solution.py:31
  9.9 32.3 %collective-permute-start.2 = (bf16[2,2,4,64,512]{4,3,2,1,0:T(8,128)(2,1)}, bf16[2,2,4,64,512]{4,3,2,1,0:T(8,128)(2,1)}, u32[]{:S(2)}, u32[]{:S(2)}) collective-permute-start(bf16[2,2,4,64,512]{4,3,2,1,0:T(8,128)(2,1)} %get-tuple-element.27.refs_2_), channel_id=1, source_target_pairs={{0,8},{8,16},{16,24},{24,32},{32,40},{40,48},{48,56},{56,64},{64,7... | collective-permute-start | bytes 3145736 | tf_op jit(solution)/shard_map/ppermute | solution.py:24
  13.7 35.1 %collective-permute-start.3 = (bf16[2,2,4,64,512]{4,3,2,1,0:T(8,128)(2,1)}, bf16[2,2,4,64,512]{4,3,2,1,0:T(8,128)(2,1)}, u32[]{:S(2)}, u32[]{:S(2)}) collective-permute-start(bf16[2,2,4,64,512]{4,3,2,1,0:T(8,128)(2,1)} %get-tuple-element.27.refs_2_), channel_id=1, source_target_pairs={{8,0},{16,8},{24,16},{32,24},{40,32},{48,40},{56,48},{64,56},{72,6... | collective-permute-start | bytes 3145736 | tf_op jit(solution)/shard_map/ppermute | solution.py:24
  19.8 34.1 %collective-permute-start.6 = (bf16[2,4,4,128,128]{4,3,2,1,0:T(8,128)(2,1)}, bf16[2,4,4,128,128]{4,3,2,1,0:T(8,128)(2,1)S(1)}, u32[]{:S(2)}, u32[]{:S(2)}) collective-permute-start(bf16[2,4,4,128,128]{4,3,2,1,0:T(8,128)(2,1)} %get-tuple-element.32), channel_id=1, source_target_pairs={{0,4},{4,0},{1,5},{5,1},{2,6},{6,2},{3,7},{7,3},{8,12},{12,8},{9,1... | collective-permute-start | bytes 3145736 | tf_op jit(solution)/shard_map/ppermute | solution.py:31
  23.3 44.9 %collective-permute-start.7 = (bf16[2,4,4,128,128]{4,3,2,1,0:T(8,128)(2,1)}, bf16[2,4,4,128,128]{4,3,2,1,0:T(8,128)(2,1)}, u32[]{:S(2)}, u32[]{:S(2)}) collective-permute-start(bf16[2,4,4,128,128]{4,3,2,1,0:T(8,128)(2,1)} %get-tuple-element.33), channel_id=1, source_target_pairs={{0,5},{1,4},{4,1},{5,0},{2,7},{3,6},{6,3},{7,2},{8,13},{9,12},{12,... | collective-permute-start | bytes 3145736 | tf_op jit(solution)/shard_map/ppermute | solution.py:31
  23.4 24.1 %copy-start = (bf16[2,4,4,64,512]{4,3,2,1,0:T(8,128)(2,1)}, bf16[2,4,4,64,512]{4,3,2,1,0:T(8,128)(2,1)S(1)}, u32[]{:S(2)}) copy-start(bf16[2,4,4,64,512]{4,3,2,1,0:T(8,128)(2,1)S(1)} %collective-permute-done.refs_3_) | copy-start | bytes 6291460
  24.5 43.7 %collective-permute-start.4 = (bf16[2,2,4,64,512]{4,3,2,1,0:T(8,128)(2,1)}, bf16[2,2,4,64,512]{4,3,2,1,0:T(8,128)(2,1)}, u32[]{:S(2)}, u32[]{:S(2)}) collective-permute-start(bf16[2,2,4,64,512]{4,3,2,1,0:T(8,128)(2,1)} %slice.19), channel_id=1, source_target_pairs={{0,8},{8,16},{16,24},{24,32},{32,40},{40,48},{48,56},{56,64},{64,7... | collective-permute-start | bytes 3145736 | tf_op jit(solution)/shard_map/ppermute | solution.py:24
  42.1 28.3 %collective-permute-start.5 = (bf16[2,2,4,64,512]{4,3,2,1,0:T(8,128)(2,1)}, bf16[2,2,4,64,512]{4,3,2,1,0:T(8,128)(2,1)}, u32[]{:S(2)}, u32[]{:S(2)}) collective-permute-start(bf16[2,2,4,64,512]{4,3,2,1,0:T(8,128)(2,1)} %slice.19), channel_id=1, source_target_pairs={{8,0},{16,8},{24,16},{32,24},{40,32},{48,40},{56,48},{64,56},{72,6... | collective-permute-start | bytes 3145736 | tf_op jit(solution)/shard_map/ppermute | solution.py:24
  51.9 39.1 %collective-permute-start.8 = (bf16[2,1,8,64,512]{4,3,2,1,0:T(8,128)(2,1)}, bf16[2,1,8,64,512]{4,3,2,1,0:T(8,128)(2,1)}, u32[]{:S(2)}, u32[]{:S(2)}) collective-permute-start(bf16[2,1,8,64,512]{4,3,2,1,0:T(8,128)(2,1)} %pad_maximum_fusion.1.refs_2_.refs_3_), channel_id=1, source_target_pairs={{0,8},{8,16},{16,24},{24,32},{32,40},{40,48},{48,56},{56,64},{64,7... | collective-permute-start | bytes 3145736 | tf_op jit(solution)/shard_map/ppermute | solution.py:24
  53.9 26.5 %copy-start.1 = (bf16[2,1,8,64,512]{4,3,2,1,0:T(8,128)(2,1)}, bf16[2,1,8,64,512]{4,3,2,1,0:T(8,128)(2,1)S(1)}, u32[]{:S(2)}) copy-start(bf16[2,1,8,64,512]{4,3,2,1,0:T(8,128)(2,1)S(1)} %pad_maximum_fusion.refs_2_.refs_3_) | copy-start | bytes 3145732
  53.9 16.5 %copy-start.3 = (bf16[2,4,4,128,128]{4,3,2,1,0:T(8,128)(2,1)}, bf16[2,4,4,128,128]{4,3,2,1,0:T(8,128)(2,1)S(1)}, u32[]{:S(2)}) copy-start(bf16[2,4,4,128,128]{4,3,2,1,0:T(8,128)(2,1)S(1)} %collective-permute-done.6.refs_8_) | copy-start | bytes 3145732
  53.9 39.0 %collective-permute-start.9 = (bf16[2,1,8,64,512]{4,3,2,1,0:T(8,128)(2,1)}, bf16[2,1,8,64,512]{4,3,2,1,0:T(8,128)(2,1)}, u32[]{:S(2)}, u32[]{:S(2)}) collective-permute-start(bf16[2,1,8,64,512]{4,3,2,1,0:T(8,128)(2,1)} %pad_maximum_fusion.1.refs_2_.refs_3_), channel_id=1, source_target_pairs={{8,0},{16,8},{24,16},{32,24},{40,32},{48,40},{56,48},{64,56},{72,6... | collective-permute-start | bytes 3145736 | tf_op jit(solution)/shard_map/ppermute | solution.py:24
  78.5 32.7 %collective-permute-start.10 = (bf16[2,1,8,64,512]{4,3,2,1,0:T(8,128)(2,1)S(1)}, bf16[2,1,8,64,512]{4,3,2,1,0:T(8,128)(2,1)}, u32[]{:S(2)}, u32[]{:S(2)}) collective-permute-start(bf16[2,1,8,64,512]{4,3,2,1,0:T(8,128)(2,1)S(1)} %pad_maximum_fusion.refs_2_.refs_3_), channel_id=1, source_target_pairs={{0,8},{8,16},{16,24},{24,32},{32,40},{40,48},{48,56},{56,64},{64,7... | collective-permute-start | bytes 3145736 | tf_op jit(solution)/shard_map/ppermute | solution.py:24
  80.4 32.8 %collective-permute-start.11 = (bf16[2,1,8,64,512]{4,3,2,1,0:T(8,128)(2,1)S(1)}, bf16[2,1,8,64,512]{4,3,2,1,0:T(8,128)(2,1)}, u32[]{:S(2)}, u32[]{:S(2)}) collective-permute-start(bf16[2,1,8,64,512]{4,3,2,1,0:T(8,128)(2,1)S(1)} %pad_maximum_fusion.refs_2_.refs_3_), channel_id=1, source_target_pairs={{8,0},{16,8},{24,16},{32,24},{40,32},{48,40},{56,48},{64,56},{72,6... | collective-permute-start | bytes 3145736 | tf_op jit(solution)/shard_map/ppermute | solution.py:24
  86.5 21.1 %all-to-all-start = ((s16[8,2,272,128]{3,2,1,0:T(8,128)(2,1)}), s16[8,2,272,128]{3,2,1,0:T(8,128)(2,1)S(1)}, u32[]{:S(2)}, u32[]{:S(2)}) async-start(s16[8,2,272,128]{3,2,1,0:T(8,128)(2,1)} %products.3), calls=%async_computation | async-start | bytes 2228224 | tf_op jit(solution)/shard_map/all_to_all | solution.py:349
  107.7 14.2 %all-to-all-start.1 = ((s16[8,1,272,128]{3,2,1,0:T(8,128)(2,1)}), s16[8,1,272,128]{3,2,1,0:T(8,128)(2,1)S(1)}, u32[]{:S(2)}, u32[]{:S(2)}) async-start(s16[8,1,272,128]{3,2,1,0:T(8,128)(2,1)} %products.4), calls=%async_computation.1 | async-start | bytes 1114112 | tf_op jit(solution)/shard_map/all_to_all | solution.py:349
  121.8 14.2 %all-to-all-start.2 = ((s16[8,1,272,128]{3,2,1,0:T(8,128)(2,1)}), s16[8,1,272,128]{3,2,1,0:T(8,128)(2,1)S(1)}, u32[]{:S(2)}, u32[]{:S(2)}) async-start(s16[8,1,272,128]{3,2,1,0:T(8,128)(2,1)} %products.5), calls=%async_computation.2 | async-start | bytes 1114112 | tf_op jit(solution)/shard_map/all_to_all | solution.py:349

commit v5 on v4

--- a/solution.py
+++ b/solution.py
@@ -174,19 +174,41 @@
     )(terms, *done)
 
 
-def mute_kernel(place, live, mine, others, early, leaving, kept):
-    step = pl.program_id(0)
+def keep_live(live, kept):
     xs, pts, recv = kept.shape
-
-    @pl.when(step == 0)
-    def _():
-        rows = lax.broadcasted_iota(jnp.int32, (pts, pts), 0)
-        diagonal = rows == lax.broadcasted_iota(jnp.int32, (pts, pts), 1)
-        receiver = lax.broadcasted_iota(jnp.int32, (pts, recv), 1).astype(jnp.float32)
-        for x in range(xs):
-            row = jnp.broadcast_to(live[x : x + 1, :].astype(jnp.float32), (pts, pts))
-            column = jnp.sum(jnp.where(diagonal, row, 0.0), axis=1, keepdims=True)
-            kept[x] = (receiver < column).astype(jnp.float32).astype(kept.dtype)
+    rows = lax.broadcasted_iota(jnp.int32, (pts, pts), 0)
+    diagonal = rows == lax.broadcasted_iota(jnp.int32, (pts, pts), 1)
+    receiver = lax.broadcasted_iota(jnp.int32, (pts, recv), 1).astype(jnp.float32)
+    for x in range(xs):
+        row = jnp.broadcast_to(live[x : x + 1, :].astype(jnp.float32), (pts, pts))
+        column = jnp.sum(jnp.where(diagonal, row, 0.0), axis=1, keepdims=True)
+        kept[x] = (receiver < column).astype(jnp.float32).astype(kept.dtype)
+
+
+def keep_inside(first_point, aperture, inside):
+    inline = first_point + lax.broadcasted_iota(jnp.int32, inside.shape, 0)
+    within = (inline >= aperture[0:1, :]) & (inline < aperture[1:2, :])
+    inside[...] = within.astype(jnp.float32).astype(inside.dtype)
+
+
+def put_masked(source, piece, to, at, offset, inside):
+    pts = inside.shape[0] // 5
+    kept = inside[offset * pts : (offset + 1) * pts, :]
+    for part in range(2):
+        for freq in range(source.shape[1]):
+            to[part, freq, :, at * pts : (at + 1) * pts, :] = (
+                source[part, freq, :, piece * pts : (piece + 1) * pts, :] * kept
+            )
+
+
+def first_kernel(place, live, aperture, *refs):
+    mine, others, low, high, other_shots = refs[:5]
+    early, leaving, crossing, cross_leaving, shots_leaving, kept, inside = refs[5:]
+
+    @pl.when(pl.program_id(0) == 0)
+    def _():
+        keep_live(live, kept)
+        keep_inside(place[2], aperture, inside)
         for part in range(2):
             for freq in range(early.shape[1]):
                 early[part, freq] = mine[part, freq] * kept[...]
@@ -194,94 +216,104 @@
     for part in range(2):
         for freq in range(leaving.shape[1]):
             leaving[part, freq] = others[part, freq] * kept[...]
-
-
-def mute(place, gathers, live):
+    put_masked(low, 0, crossing, 0, 1, inside)
+    put_masked(high, 0, crossing, 1, 3, inside)
+    for k in range(5):
+        put_masked(other_shots, k, cross_leaving if k % 2 else shots_leaving, k // 2, k, inside)
+
+
+def second_kernel(place, aperture, below, here, above, staying, inside):
+    @pl.when(pl.program_id(0) == 0)
+    def _():
+        keep_inside(place[2], aperture, inside)
+
+    for k, source in enumerate((below, here, above)):
+        put_masked(source, 0, staying, k, 2 * k, inside)
+
+
+def prepare(place, gathers, live, shots, aperture):
     freqs, xs, pts, recv = gathers.shape[1:]
+    spread, width = shots.shape[3:]
     count = freqs // 2
-    block = (2, FIRST, xs, pts, recv)
-
-    def array(size):
-        return jax.ShapeDtypeStruct((2, size, xs, pts, recv), gathers.dtype)
-
+    steps = count // FIRST
+
+    def block(rows, columns):
+        return (2, FIRST, xs, rows, columns)
+
+    def source(other, at, rows):
+        def index(i, place):
+            return (0, (place[1] ^ other) * steps + i, 0, at, 0)
+
+        return pl.BlockSpec(block(rows, width), index)
+
+    def result(rows, columns):
+        return pl.BlockSpec(block(rows, columns), lambda i, place: (0, i, 0, 0, 0))
+
+    sizes = (2 * pts, 2 * pts, 3 * pts)
     return pl.pallas_call(
-        mute_kernel,
+        first_kernel,
         grid_spec=pltpu.PrefetchScalarGridSpec(
             num_scalar_prefetch=1,
-            grid=(count // FIRST,),
+            grid=(steps,),
             in_specs=[
                 pl.BlockSpec((xs, pts), lambda i, place: (0, 0)),
-                pl.BlockSpec(block, lambda i, place: (0, place[1] * (count // FIRST), 0, 0, 0)),
+                pl.BlockSpec((2, width), lambda i, place: (0, 0)),
+                pl.BlockSpec(block(pts, recv), lambda i, place: (0, place[1] * steps, 0, 0, 0)),
                 pl.BlockSpec(
-                    block, lambda i, place: (0, (1 - place[1]) * (count // FIRST) + i, 0, 0, 0)
+                    block(pts, recv), lambda i, place: (0, (1 - place[1]) * steps + i, 0, 0, 0)
                 ),
+                source(0, 1, pts),
+                source(0, 3, pts),
+                source(1, 0, spread),
             ],
             out_specs=[
-                pl.BlockSpec(block, lambda i, place: (0, 0, 0, 0, 0)),
-                pl.BlockSpec(block, lambda i, place: (0, i, 0, 0, 0)),
+                pl.BlockSpec(block(pts, recv), lambda i, place: (0, 0, 0, 0, 0)),
+                result(pts, recv),
+            ]
+            + [result(rows, width) for rows in sizes],
+            scratch_shapes=[
+                pltpu.VMEM((xs, pts, recv), gathers.dtype),
+                pltpu.VMEM((spread, width), shots.dtype),
             ],
-            scratch_shapes=[pltpu.VMEM((xs, pts, recv), gathers.dtype)],
         ),
-        out_shape=[array(FIRST), array(count)],
+        out_shape=[
+            jax.ShapeDtypeStruct((2, FIRST, xs, pts, recv), gathers.dtype),
+            jax.ShapeDtypeStruct((2, count, xs, pts, recv), gathers.dtype),
+        ]
+        + [jax.ShapeDtypeStruct((2, count, xs, rows, width), shots.dtype) for rows in sizes],
         compiler_params=pltpu.CompilerParams(vmem_limit_bytes=58 * 2**20),
-        cost_estimate=pl.CostEstimate(flops=0, bytes_accessed=6 * 2**20, transcendentals=0),
-        name="mute",
-    )(place, live, gathers, gathers)
-
-
-def mask_kernel(plan, place, aperture, *refs):
-    inside = refs[-1]
-    spread, shots = inside.shape
-    pts = spread // 5
-
-    @pl.when(pl.program_id(0) == 0)
-    def _():
-        inline = place[2] + lax.broadcasted_iota(jnp.int32, (spread, shots), 0)
-        within = (inline >= aperture[0:1, :]) & (inline < aperture[1:2, :])
-        inside[...] = within.astype(jnp.float32).astype(inside.dtype)
-
-    for source, piece, to, at, offset in plan:
-        kept = inside[offset * pts : (offset + 1) * pts, :]
-        for part in range(2):
-            for freq in range(refs[source].shape[1]):
-                refs[to][part, freq, :, at * pts : (at + 1) * pts, :] = (
-                    refs[source][part, freq, :, piece * pts : (piece + 1) * pts, :] * kept
-                )
-
-
-def mask(place, shots, aperture, plan, sources, outputs):
+        cost_estimate=pl.CostEstimate(flops=0, bytes_accessed=13 * 2**20, transcendentals=0),
+        name="prepare",
+    )(place, live, aperture, gathers, gathers, shots, shots, shots)
+
+
+def stay(place, shots, aperture):
     freqs, xs, spread, width = shots.shape[1:]
     count, pts = freqs // 2, spread // 5
-    steps, size = count // FIRST, FIRST
-
-    def source(other, at, pieces):
-        def index(i, place):
-            return (0, (place[1] ^ other) * steps + i, 0, at, 0)
-
-        return pl.BlockSpec((2, size, xs, pieces * pts, width), index)
-
-    moved = (sum(pieces for _, _, pieces in sources) + sum(outputs)) * 2**19
+    steps = count // FIRST
+
+    def source(at):
+        return pl.BlockSpec(
+            (2, FIRST, xs, pts, width), lambda i, place: (0, place[1] * steps + i, 0, at, 0)
+        )
+
     return pl.pallas_call(
-        functools.partial(mask_kernel, plan),
+        second_kernel,
         grid_spec=pltpu.PrefetchScalarGridSpec(
             num_scalar_prefetch=1,
             grid=(steps,),
             in_specs=[pl.BlockSpec((2, width), lambda i, place: (0, 0))]
-            + [source(*block) for block in sources],
-            out_specs=[
-                pl.BlockSpec((2, size, xs, pieces * pts, width), lambda i, place: (0, i, 0, 0, 0))
-                for pieces in outputs
-            ],
+            + [source(at) for at in (0, 2, 4)],
+            out_specs=pl.BlockSpec(
+                (2, FIRST, xs, 3 * pts, width), lambda i, place: (0, i, 0, 0, 0)
+            ),
             scratch_shapes=[pltpu.VMEM((spread, width), shots.dtype)],
         ),
-        out_shape=[
-            jax.ShapeDtypeStruct((2, count, xs, pieces * pts, width), shots.dtype)
-            for pieces in outputs
-        ],
+        out_shape=jax.ShapeDtypeStruct((2, count, xs, 3 * pts, width), shots.dtype),
         compiler_params=pltpu.CompilerParams(vmem_limit_bytes=58 * 2**20),
-        cost_estimate=pl.CostEstimate(flops=0, bytes_accessed=moved, transcendentals=0),
-        name="mask",
-    )(place, aperture, *[shots] * len(sources))
+        cost_estimate=pl.CostEstimate(flops=0, bytes_accessed=3 * 2**20, transcendentals=0),
+        name="stay",
+    )(place, aperture, shots, shots, shots)
 
 
 def on_device(surface_gathers, source_gathers, aperture, live):
@@ -292,32 +324,17 @@
     first_point = (2 * lax.axis_index("sup") + half) * pts - (spread - pts) // 2
     place = jnp.stack([half, core, first_point]).astype(jnp.int32)
 
-    early, leaving = mute(place, surface_gathers, live)
+    shots = source_gathers.transpose(0, 1, 3, 4, 2)
+    early, leaving, crossing, cross_leaving, shots_leaving = prepare(
+        place, surface_gathers, live, shots, aperture.T
+    )
     below_early, above_early = shifted(early, 1), shifted(early, -1)
-    shots = source_gathers.transpose(0, 1, 3, 4, 2)
-    crossing, cross_leaving, shots_leaving = mask(
-        place,
-        shots,
-        aperture.T,
-        ((0, 0, 3, 0, 1), (1, 0, 3, 1, 3), (2, 1, 4, 0, 1), (2, 3, 4, 1, 3))
-        + tuple((2, 2 * k, 5, k, 2 * k) for k in range(3)),
-        ((0, 1, 1), (0, 3, 1), (1, 0, 5)),
-        (2, 2, 3),
-    )
-    cross = [(swapped(crossing, "half"), 0), (swapped(cross_leaving, ("half", "core")), 0)]
     gathers = swapped(leaving, "core")
     others = swapped(shots_leaving, "core")
-    gathers, others, surface_gathers, shots = lax.optimization_barrier(
-        (gathers, others, surface_gathers, shots)
-    )
-    (staying,) = mask(
-        place,
-        shots,
-        aperture.T,
-        tuple((k, 0, 3, k, 2 * k) for k in range(3)),
-        ((0, 0, 1), (0, 2, 1), (0, 4, 1)),
-        (3,),
-    )
+    cross = [(swapped(crossing, "half"), 0), (swapped(cross_leaving, ("half", "core")), 0)]
+    gathers, surface_gathers = lax.optimization_barrier((gathers, surface_gathers))
+    others, shots = lax.optimization_barrier((others, shots))
+    staying = stay(place, shots, aperture.T)
     heard = lax.broadcasted_iota(jnp.int32, surface_gathers.shape[2:], 2) < live[:, :, None]
     late = lax.dynamic_slice_in_dim(surface_gathers, core * count + FIRST, count - FIRST, 1)
     late = jnp.where(heard, late, jnp.zeros((), late.dtype))
@@ -327,7 +344,6 @@
     here, below, above = [[(early, 0), (gathers, 0)]], [], []
     arrived = [below_early, above_early]
     spans = [(0, FIRST)] + [(i, 1) for i in range(FIRST, count)]
-    partial = []
     for i, (first, size) in enumerate(spans):
         if i:
             block = jnp.concatenate(
@@ -335,15 +351,18 @@
             )
             if i == 1:
                 block, arrived = lax.optimization_barrier((block, arrived))
-                below.append([(arrived[0], 0), (below_too, 0)])
-                above.append([(arrived[1], 0), (above_too, 0)])
-                partial.append(products(place, spans[0], below[0], here[0], above[0], own, cross))
+                block_after = [below_too, above_too]
             else:
-                block, partial[i - 2] = lax.optimization_barrier((block, partial[i - 2]))
+                block, block_after = lax.optimization_barrier((block, block_after))
+                below.insert(0, [(arrived[0], 0), (block_after[0], 0)])
+                above.insert(0, [(arrived[1], 0), (block_after[1], 0)])
             here.append([(block, first)])
             below.append([(shifted(block, 1), first)])
             above.append([(shifted(block, -1), first)])
-            partial.append(products(place, spans[i], below[i], here[i], above[i], own, cross))
+    partial = [
+        products(place, spans[i], below[i], here[i], above[i], own, cross)
+        for i in range(len(spans))
+    ]
     predicted = None
     for i, freqs in enumerate(spans):
         terms = lax.all_to_all(partial[i], RING, 0, 0, tiled=True)

time: 138 us -> 134 us (0.971)
  Pallas kernels: 32.3 us -> 30 us
  starting transfers between devices: 47.2 us -> 45.1 us
    ppermute x8, waiting for transfers between devices: 21.9 us -> 33 us  [shifted(): lax.ppermute(block, 'sup', [(i, i + distance) for i in range(n) if 0 <= i...]
    ppermute x4, waiting for transfers between devices: 8.24 us -> 0.01 us  [swapped(): return lax.ppermute(block, axes, [(i, n - 1 - i) for i in range(n)])]
    pallas_call x3 -> x2, Pallas kernels: 11.8 us -> 9.38 us  [the longest x1 6.28 us: prepare(): pl.pallas_call(first_kernel, grid_spec=pltpu.PrefetchScalarGridSpec(num_s...]
    ppermute x8, starting transfers between devices: 31.7 us -> 29.6 us  [shifted(): lax.ppermute(block, 'sup', [(i, i + distance) for i in range(n) if 0 <= i...]
    all_to_all x3, waiting for transfers between devices: 22.4 us -> 20.6 us  [on_device(): terms = lax.all_to_all(partial[i], RING, 0, 0, tiled=True)]
  transfers between devices with their start and end apart: 15 -> 15, of which waited for: 8 -> 7; matrix products, arithmetic and copies ran while one was open for 3% -> 2% of each run, Pallas kernels for 20% -> 17%
where the time goes in v5:
time: 134 us
  waiting for transfers between devices  53.6 us (40%)
  starting transfers between devices  45.1 us (34%)
  Pallas kernels  30 us (22%)
  other arithmetic  3.36 us (3%)
    ppermute x8, waiting for transfers between devices, shifted(): lax.ppermute(block, 'sup', [(i, i + distance) for i in range(n) if 0 <= i...  33 us
    ppermute x8, starting transfers between devices, shifted(): lax.ppermute(block, 'sup', [(i, i + distance) for i in range(n) if 0 <= i...  29.6 us
    all_to_all x3, waiting for transfers between devices, on_device(): terms = lax.all_to_all(partial[i], RING, 0, 0, tiled=True)  20.6 us
    pallas_call x3, Pallas kernels, products(): pl.pallas_call(products_kernel, grid=(count, STEPS), in_specs=[pl.BlockSp...  17.9 us
    all_to_all x3, starting transfers between devices, on_device(): terms = lax.all_to_all(partial[i], RING, 0, 0, tiled=True)  11.6 us
    pallas_call x1, Pallas kernels, prepare(): pl.pallas_call(first_kernel, grid_spec=pltpu.PrefetchScalarGridSpec(num_s...  6.28 us
    ppermute x4, starting transfers between devices, swapped(): return lax.ppermute(block, axes, [(i, n - 1 - i) for i in range(n)])  3.9 us
    pallas_call x1, Pallas kernels, stay(): pl.pallas_call(second_kernel, grid_spec=pltpu.PrefetchScalarGridSpec(num_...  3.1 us
  transfers between devices with their start and end apart: 15, of which 7 were waited for; matrix products, arithmetic and copies ran while one was open for 2% of the time, Pallas kernels for 17%

profile of v5, /device:TPU:6, one launch (start us, length us, event | category | flops | bytes accessed | tf_op | source)
XLA Modules:
  0.0 133.5 jit_solution(17270958061656780350)
XLA Ops:
  0.0 0.7 pad_add_fusion.place
  0.7 6.3 %prepare.1 = (bf16[2,2,4,64,512]{4,3,2,1,0:T(8,128)(2,1)}, bf16[2,4,4,64,512]{4,3,2,1,0:T(8,128)(2,1)}, bf16[2,4,4,128,128]{4,3,2,1,0:T(8,128)(2,1)}, bf16[2,4,4...) custom-call(s32[3]{0:T(128)} %pad_add_fusion.place, s32[4,64]{1,0:T(4,128)} %live.1, s32[2,128]{1,0:T(2,128)} %bitcast.12, ...), custom_call_target="tpu_custom_call" | custom-call | bytes 13631488 | tf_op jit(solution)/shard_map/prepare/pallas_call | solution.py:253
  7.0 0.5 collective-permute-start.5
  7.5 3.8 %collective-permute-start.1 = (bf16[2,2,4,64,512]{4,3,2,1,0:T(8,128)(2,1)}, bf16[2,2,4,64,512]{4,3,2,1,0:T(8,128)(2,1)}, u32[]{:S(2)}, u32[]{:S(2)}) collective-permute-start(bf16[2,2,4,64,512]{4,3,2,1,0:T(8,128)(2,1)} %get-tuple-element.27.refs_2_), channel_id=1, source_target_pairs={{0,8},{8,16},{16,24},{24,32},{32,40},{40,48},{48,56},{56,64},{64,7... | collective-permute-start | bytes 3145736 | tf_op jit(solution)/shard_map/ppermute | solution.py:24
  11.3 6.1 %collective-permute-start.2 = (bf16[2,2,4,64,512]{4,3,2,1,0:T(8,128)(2,1)}, bf16[2,2,4,64,512]{4,3,2,1,0:T(8,128)(2,1)}, u32[]{:S(2)}, u32[]{:S(2)}) collective-permute-start(bf16[2,2,4,64,512]{4,3,2,1,0:T(8,128)(2,1)} %get-tuple-element.27.refs_2_), channel_id=1, source_target_pairs={{8,0},{16,8},{24,16},{32,24},{40,32},{48,40},{56,48},{64,56},{72,6... | collective-permute-start | bytes 3145736 | tf_op jit(solution)/shard_map/ppermute | solution.py:24
  17.4 3.3 %collective-permute-start.6 = (bf16[2,4,4,128,128]{4,3,2,1,0:T(8,128)(2,1)}, bf16[2,4,4,128,128]{4,3,2,1,0:T(8,128)(2,1)S(1)}, u32[]{:S(2)}, u32[]{:S(2)}) collective-permute-start(bf16[2,4,4,128,128]{4,3,2,1,0:T(8,128)(2,1)} %get-tuple-element.35), channel_id=1, source_target_pairs={{0,4},{4,0},{1,5},{5,1},{2,6},{6,2},{3,7},{7,3},{8,12},{12,8},{9,1... | collective-permute-start | bytes 3145736 | tf_op jit(solution)/shard_map/ppermute | solution.py:31
  21.0 3.1 %stay.1.refs_6_ = bf16[2,4,4,192,128]{4,3,2,1,0:T(8,128)(2,1)} custom-call(s32[3]{0:T(128)} %pad_add_fusion.place, s32[2,128]{1,0:T(2,128)} %bitcast.13, bf16[2,8,4,320,128]{4,3,2,1,0:T(8,128)(2,1)} %bitcast.9, bf16[2,8,4,320,128]{4,3,2,1,0:T(8,128)(2,1)} %bitcast.10, bf16[2,8,4,320,128]{4,3,2,1,0:T(8,128)(2,1)} %bitcast.11), custom_call_target="tpu_custom_call" | custom-call | bytes 3145728 | tf_op jit(solution)/shard_map/stay/pallas_call | solution.py:300
  24.2 1.9 %collective-permute-start.3 = (bf16[2,2,4,64,512]{4,3,2,1,0:T(8,128)(2,1)S(1)}, bf16[2,2,4,64,512]{4,3,2,1,0:T(8,128)(2,1)S(1)}, u32[]{:S(2)}, u32[]{:S(2)}) collective-permute-start(bf16[2,2,4,64,512]{4,3,2,1,0:T(8,128)(2,1)S(1)} %slice.19), channel_id=1, source_target_pairs={{0,8},{8,16},{16,24},{24,32},{32,40},{40,48},{48,56},{56,64},{64,7... | collective-permute-start | bytes 3145736 | tf_op jit(solution)/shard_map/ppermute | solution.py:24
  26.1 13.6 %collective-permute-done.1.refs_0_ = bf16[2,2,4,64,512]{4,3,2,1,0:T(8,128)(2,1)} collective-permute-done((bf16[2,2,4,64,512]{4,3,2,1,0:T(8,128)(2,1)}, bf16[2,2,4,64,512]{4,3,2,1,0:T(8,128)(2,1)}, u32[]{:S(2)}, u32[]{:S(2)}) %collective-permute-start.1) | collective-permute-done | bytes 1048608 | tf_op jit(solution)/shard_map/ppermute | solution.py:24
  39.8 3.9 %collective-permute-start.4 = (bf16[2,2,4,64,512]{4,3,2,1,0:T(8,128)(2,1)S(1)}, bf16[2,2,4,64,512]{4,3,2,1,0:T(8,128)(2,1)S(1)}, u32[]{:S(2)}, u32[]{:S(2)}) collective-permute-start(bf16[2,2,4,64,512]{4,3,2,1,0:T(8,128)(2,1)S(1)} %slice.19), channel_id=1, source_target_pairs={{8,0},{16,8},{24,16},{32,24},{40,32},{48,40},{56,48},{64,56},{72,6... | collective-permute-start | bytes 3145736 | tf_op jit(solution)/shard_map/ppermute | solution.py:24
  43.7 1.4 %dynamic-slice_select_fusion = bf16[2,2,4,64,512]{4,3,2,1,0:T(8,128)(2,1)S(1)} fusion(bf16[2,8,4,64,512]{4,3,2,1,0:T(8,128)(2,1)} %refs_1_.1, s32[]{:T(128)S(6)} %select_n.7, pred[4,64,512]{2,1,0:T(8,128)(4,1)S(1)} %iota_compare_fusion), kind=kLoop, calls=%fused_computation.2 | loop fusion | flops 524288 | bytes 2228228 | tf_op jit(solution)/shard_map/jit(_where)/select_n | solution.py:340
  45.3 1.1 pad_maximum_fusion.refs_2_.refs_3_
  46.4 1.9 %collective-permute-start.8 = (bf16[2,1,8,64,512]{4,3,2,1,0:T(8,128)(2,1)}, bf16[2,1,8,64,512]{4,3,2,1,0:T(8,128)(2,1)}, u32[]{:S(2)}, u32[]{:S(2)}) collective-permute-start(bf16[2,1,8,64,512]{4,3,2,1,0:T(8,128)(2,1)} %pad_maximum_fusion.refs_2_.refs_3_), channel_id=1, source_target_pairs={{0,8},{8,16},{16,24},{24,32},{32,40},{40,48},{48,56},{56,64},{64,7... | collective-permute-start | bytes 3145736 | tf_op jit(solution)/shard_map/ppermute | solution.py:24
  48.4 13.7 %collective-permute-done.3.refs_1_ = bf16[2,2,4,64,512]{4,3,2,1,0:T(8,128)(2,1)S(1)} collective-permute-done((bf16[2,2,4,64,512]{4,3,2,1,0:T(8,128)(2,1)S(1)}, bf16[2,2,4,64,512]{4,3,2,1,0:T(8,128)(2,1)S(1)}, u32[]{:S(2)}, u32[]{:S(2)}) %collective-permute-start.3) | collective-permute-done | bytes 1048608 | tf_op jit(solution)/shard_map/ppermute | solution.py:24
  62.1 4.0 %collective-permute-start.9 = (bf16[2,1,8,64,512]{4,3,2,1,0:T(8,128)(2,1)}, bf16[2,1,8,64,512]{4,3,2,1,0:T(8,128)(2,1)}, u32[]{:S(2)}, u32[]{:S(2)}) collective-permute-start(bf16[2,1,8,64,512]{4,3,2,1,0:T(8,128)(2,1)} %pad_maximum_fusion.refs_2_.refs_3_), channel_id=1, source_target_pairs={{8,0},{16,8},{24,16},{32,24},{40,32},{48,40},{56,48},{64,56},{72,6... | collective-permute-start | bytes 3145736 | tf_op jit(solution)/shard_map/ppermute | solution.py:24
  66.1 1.9 %collective-permute-start.10 = (bf16[2,1,8,64,512]{4,3,2,1,0:T(8,128)(2,1)S(1)}, bf16[2,1,8,64,512]{4,3,2,1,0:T(8,128)(2,1)}, u32[]{:S(2)}, u32[]{:S(2)}) collective-permute-start(bf16[2,1,8,64,512]{4,3,2,1,0:T(8,128)(2,1)S(1)} %pad_maximum_fusion.1.refs_2_.refs_3_), channel_id=1, source_target_pairs={{0,8},{8,16},{16,24},{24,32},{32,40},{40,48},{48,56},{56,64},{64,7... | collective-permute-start | bytes 3145736 | tf_op jit(solution)/shard_map/ppermute | solution.py:24
  68.1 6.0 %collective-permute-start.11 = (bf16[2,1,8,64,512]{4,3,2,1,0:T(8,128)(2,1)S(1)}, bf16[2,1,8,64,512]{4,3,2,1,0:T(8,128)(2,1)}, u32[]{:S(2)}, u32[]{:S(2)}) collective-permute-start(bf16[2,1,8,64,512]{4,3,2,1,0:T(8,128)(2,1)S(1)} %pad_maximum_fusion.1.refs_2_.refs_3_), channel_id=1, source_target_pairs={{8,0},{16,8},{24,16},{32,24},{40,32},{48,40},{56,48},{64,56},{72,6... | collective-permute-start | bytes 3145736 | tf_op jit(solution)/shard_map/ppermute | solution.py:24
  74.1 1.0 copy-done.4
  75.1 8.1 %products.3 = s16[8,2,272,128]{3,2,1,0:T(8,128)(2,1)} custom-call(s32[3]{0:T(128)} %pad_add_fusion.place, bf16[2,2,4,64,512]{4,3,2,1,0:T(8,128)(2,1)} %collective-permute-done.1.refs_0_, bf16[2,2,4,64,512]{4,3,2,1,0:T(8,128)(2,1)} %copy-done.5, bf16[2,2,4,64,512]{4,3,2,1,0:T(8,128)(2,1)} %get-tuple-element.27.refs_2_, bf16[2,4,4,64,512]{4,3,2,1,0:T(8,128)(2,1)} %copy-done, ...), custom_call_target="tpu_custom_call" | custom-call | flops 38654705664 | bytes 1048576 | tf_op jit(solution)/shard_map/products/pallas_call | solution.py:121
  83.3 4.5 %all-to-all-start = ((s16[8,2,272,128]{3,2,1,0:T(8,128)(2,1)}), s16[8,2,272,128]{3,2,1,0:T(8,128)(2,1)S(1)}, u32[]{:S(2)}, u32[]{:S(2)}) async-start(s16[8,2,272,128]{3,2,1,0:T(8,128)(2,1)} %products.3), calls=%async_computation | async-start | bytes 2228224 | tf_op jit(solution)/shard_map/all_to_all | solution.py:368
  87.7 2.7 %collective-permute-done.9.refs_4_.refs_5_ = bf16[2,1,8,64,512]{4,3,2,1,0:T(8,128)(2,1)} collective-permute-done((bf16[2,1,8,64,512]{4,3,2,1,0:T(8,128)(2,1)}, bf16[2,1,8,64,512]{4,3,2,1,0:T(8,128)(2,1)}, u32[]{:S(2)}, u32[]{:S(2)}) %collective-permute-start.9) | collective-permute-done | bytes 1048608 | tf_op jit(solution)/shard_map/ppermute | solution.py:24
  90.4 4.9 %products.4 = s16[8,1,272,128]{3,2,1,0:T(8,128)(2,1)} custom-call(s32[3]{0:T(128)} %pad_add_fusion.place, bf16[2,1,8,64,512]{4,3,2,1,0:T(8,128)(2,1)} %collective-permute-done.8.refs_0_.refs_1_, bf16[2,1,8,64,512]{4,3,2,1,0:T(8,128)(2,1)} %collective-permute-done.8.refs_0_.refs_1_, bf16[2,1,8,64,512]{4,3,2,1,0:T(8,128)(2,1)} %pad_maximum_fusion.refs_2_.refs_3_, ...), custom_call_target="tpu_custom_call" | custom-call | flops 19327352832 | bytes 1048576 | tf_op jit(solution)/shard_map/products/pallas_call | solution.py:121
  95.3 9.1 %all-to-all-done.terms = s16[8,2,272,128]{3,2,1,0:T(8,128)(2,1)S(1)} async-done(((s16[8,2,272,128]{3,2,1,0:T(8,128)(2,1)}), s16[8,2,272,128]{3,2,1,0:T(8,128)(2,1)S(1)}, u32[]{:S(2)}, u32[]{:S(2)}) %all-to-all-start) | async-done | bytes 1114144 | tf_op jit(solution)/shard_map/all_to_all | solution.py:368
  104.4 3.5 %all-to-all-start.1 = ((s16[8,1,272,128]{3,2,1,0:T(8,128)(2,1)}), s16[8,1,272,128]{3,2,1,0:T(8,128)(2,1)S(1)}, u32[]{:S(2)}, u32[]{:S(2)}) async-start(s16[8,1,272,128]{3,2,1,0:T(8,128)(2,1)} %products.4), calls=%async_computation.1 | async-start | bytes 1114112 | tf_op jit(solution)/shard_map/all_to_all | solution.py:368
  108.0 3.0 %collective-permute-done.11.refs_4_.refs_5_ = bf16[2,1,8,64,512]{4,3,2,1,0:T(8,128)(2,1)} collective-permute-done((bf16[2,1,8,64,512]{4,3,2,1,0:T(8,128)(2,1)S(1)}, bf16[2,1,8,64,512]{4,3,2,1,0:T(8,128)(2,1)}, u32[]{:S(2)}, u32[]{:S(2)}) %collective-permute-start.11) | collective-permute-done | bytes 1048608 | tf_op jit(solution)/shard_map/ppermute | solution.py:24
  110.9 4.9 %products.5 = s16[8,1,272,128]{3,2,1,0:T(8,128)(2,1)} custom-call(s32[3]{0:T(128)} %pad_add_fusion.place, bf16[2,1,8,64,512]{4,3,2,1,0:T(8,128)(2,1)} %collective-permute-done.10.refs_0_.refs_1_, bf16[2,1,8,64,512]{4,3,2,1,0:T(8,128)(2,1)} %collective-permute-done.10.refs_0_.refs_1_, bf16[2,1,8,64,512]{4,3,2,1,0:T(8,128)(2,1)} %copy-done.1, ...), custom_call_target="tpu_custom_call" | custom-call | flops 19327352832 | bytes 1048576 | tf_op jit(solution)/shard_map/products/pallas_call | solution.py:121
  115.8 2.8 %all-to-all-done.1.terms = s16[8,1,272,128]{3,2,1,0:T(8,128)(2,1)S(1)} async-done(((s16[8,1,272,128]{3,2,1,0:T(8,128)(2,1)}), s16[8,1,272,128]{3,2,1,0:T(8,128)(2,1)S(1)}, u32[]{:S(2)}, u32[]{:S(2)}) %all-to-all-start.1) | async-done | bytes 557088 | tf_op jit(solution)/shard_map/all_to_all | solution.py:368
  118.6 3.5 %all-to-all-start.2 = ((s16[8,1,272,128]{3,2,1,0:T(8,128)(2,1)}), s16[8,1,272,128]{3,2,1,0:T(8,128)(2,1)S(1)}, u32[]{:S(2)}, u32[]{:S(2)}) async-start(s16[8,1,272,128]{3,2,1,0:T(8,128)(2,1)} %products.5), calls=%async_computation.2 | async-start | bytes 1114112 | tf_op jit(solution)/shard_map/all_to_all | solution.py:368
  122.1 1.1 finish.3.refs_0_
  123.2 0.8 finish.4.refs_0_
  124.0 8.8 %all-to-all-done.2.terms = s16[8,1,272,128]{3,2,1,0:T(8,128)(2,1)S(1)} async-done(((s16[8,1,272,128]{3,2,1,0:T(8,128)(2,1)}), s16[8,1,272,128]{3,2,1,0:T(8,128)(2,1)S(1)}, u32[]{:S(2)}, u32[]{:S(2)}) %all-to-all-start.2) | async-done | bytes 557088 | tf_op jit(solution)/shard_map/all_to_all | solution.py:368
  132.7 0.8 finish.5
  (28 shorter events, 0.7 us)
Async XLA Ops:
  0.7 20.1 %copy-start.2 = (s32[4,64]{1,0:T(4,128)S(1)}, s32[4,64]{1,0:T(4,128)}, u32[]{:S(2)}) copy-start(s32[4,64]{1,0:T(4,128)} %live.1) | copy-start | bytes 3076
  7.0 17.1 %collective-permute-start = (bf16[2,4,4,64,512]{4,3,2,1,0:T(8,128)(2,1)}, bf16[2,4,4,64,512]{4,3,2,1,0:T(8,128)(2,1)S(1)}, u32[]{:S(2)}, u32[]{:S(2)}) collective-permute-start(bf16[2,4,4,64,512]{4,3,2,1,0:T(8,128)(2,1)} %get-tuple-element.24), channel_id=1, source_target_pairs={{0,1},{1,0},{2,3},{3,2},{4,5},{5,4},{6,7},{7,6},{8,9},{9,8},{10,11... | collective-permute-start | bytes 6291464 | tf_op jit(solution)/shard_map/ppermute | solution.py:31
  7.0 13.9 %collective-permute-start.5 = (bf16[2,4,4,192,128]{4,3,2,1,0:T(8,128)(2,1)}, bf16[2,4,4,192,128]{4,3,2,1,0:T(8,128)(2,1)}, u32[]{:S(2)}, u32[]{:S(2)}) collective-permute-start(bf16[2,4,4,192,128]{4,3,2,1,0:T(8,128)(2,1)} %get-tuple-element.32), channel_id=1, source_target_pairs={{0,1},{1,0},{2,3},{3,2},{4,5},{5,4},{6,7},{7,6},{8,9},{9,8},{10,11... | collective-permute-start | bytes 4718600 | tf_op jit(solution)/shard_map/ppermute | solution.py:31
  7.5 32.3 %collective-permute-start.1 = (bf16[2,2,4,64,512]{4,3,2,1,0:T(8,128)(2,1)}, bf16[2,2,4,64,512]{4,3,2,1,0:T(8,128)(2,1)}, u32[]{:S(2)}, u32[]{:S(2)}) collective-permute-start(bf16[2,2,4,64,512]{4,3,2,1,0:T(8,128)(2,1)} %get-tuple-element.27.refs_2_), channel_id=1, source_target_pairs={{0,8},{8,16},{16,24},{24,32},{32,40},{40,48},{48,56},{56,64},{64,7... | collective-permute-start | bytes 3145736 | tf_op jit(solution)/shard_map/ppermute | solution.py:24
  11.3 35.1 %collective-permute-start.2 = (bf16[2,2,4,64,512]{4,3,2,1,0:T(8,128)(2,1)}, bf16[2,2,4,64,512]{4,3,2,1,0:T(8,128)(2,1)}, u32[]{:S(2)}, u32[]{:S(2)}) collective-permute-start(bf16[2,2,4,64,512]{4,3,2,1,0:T(8,128)(2,1)} %get-tuple-element.27.refs_2_), channel_id=1, source_target_pairs={{8,0},{16,8},{24,16},{32,24},{40,32},{48,40},{56,48},{64,56},{72,6... | collective-permute-start | bytes 3145736 | tf_op jit(solution)/shard_map/ppermute | solution.py:24
  17.4 50.6 %collective-permute-start.6 = (bf16[2,4,4,128,128]{4,3,2,1,0:T(8,128)(2,1)}, bf16[2,4,4,128,128]{4,3,2,1,0:T(8,128)(2,1)S(1)}, u32[]{:S(2)}, u32[]{:S(2)}) collective-permute-start(bf16[2,4,4,128,128]{4,3,2,1,0:T(8,128)(2,1)} %get-tuple-element.35), channel_id=1, source_target_pairs={{0,4},{4,0},{1,5},{5,1},{2,6},{6,2},{3,7},{7,3},{8,12},{12,8},{9,1... | collective-permute-start | bytes 3145736 | tf_op jit(solution)/shard_map/ppermute | solution.py:31
  20.9 53.2 %collective-permute-start.7 = (bf16[2,4,4,128,128]{4,3,2,1,0:T(8,128)(2,1)}, bf16[2,4,4,128,128]{4,3,2,1,0:T(8,128)(2,1)S(1)}, u32[]{:S(2)}, u32[]{:S(2)}) collective-permute-start(bf16[2,4,4,128,128]{4,3,2,1,0:T(8,128)(2,1)} %get-tuple-element.36), channel_id=1, source_target_pairs={{0,5},{1,4},{4,1},{5,0},{2,7},{3,6},{6,3},{7,2},{8,13},{9,12},{12,... | collective-permute-start | bytes 3145736 | tf_op jit(solution)/shard_map/ppermute | solution.py:31
  24.1 21.0 %copy-start = (bf16[2,4,4,64,512]{4,3,2,1,0:T(8,128)(2,1)}, bf16[2,4,4,64,512]{4,3,2,1,0:T(8,128)(2,1)S(1)}, u32[]{:S(2)}) copy-start(bf16[2,4,4,64,512]{4,3,2,1,0:T(8,128)(2,1)S(1)} %collective-permute-done.refs_3_) | copy-start | bytes 6291460
  24.2 37.9 %collective-permute-start.3 = (bf16[2,2,4,64,512]{4,3,2,1,0:T(8,128)(2,1)S(1)}, bf16[2,2,4,64,512]{4,3,2,1,0:T(8,128)(2,1)S(1)}, u32[]{:S(2)}, u32[]{:S(2)}) collective-permute-start(bf16[2,2,4,64,512]{4,3,2,1,0:T(8,128)(2,1)S(1)} %slice.19), channel_id=1, source_target_pairs={{0,8},{8,16},{16,24},{24,32},{32,40},{40,48},{48,56},{56,64},{64,7... | collective-permute-start | bytes 3145736 | tf_op jit(solution)/shard_map/ppermute | solution.py:24
  39.8 26.3 %collective-permute-start.4 = (bf16[2,2,4,64,512]{4,3,2,1,0:T(8,128)(2,1)S(1)}, bf16[2,2,4,64,512]{4,3,2,1,0:T(8,128)(2,1)S(1)}, u32[]{:S(2)}, u32[]{:S(2)}) collective-permute-start(bf16[2,2,4,64,512]{4,3,2,1,0:T(8,128)(2,1)S(1)} %slice.19), channel_id=1, source_target_pairs={{8,0},{16,8},{24,16},{32,24},{40,32},{48,40},{56,48},{64,56},{72,6... | collective-permute-start | bytes 3145736 | tf_op jit(solution)/shard_map/ppermute | solution.py:24
  46.4 41.4 %collective-permute-start.8 = (bf16[2,1,8,64,512]{4,3,2,1,0:T(8,128)(2,1)}, bf16[2,1,8,64,512]{4,3,2,1,0:T(8,128)(2,1)}, u32[]{:S(2)}, u32[]{:S(2)}) collective-permute-start(bf16[2,1,8,64,512]{4,3,2,1,0:T(8,128)(2,1)} %pad_maximum_fusion.refs_2_.refs_3_), channel_id=1, source_target_pairs={{0,8},{8,16},{16,24},{24,32},{32,40},{40,48},{48,56},{56,64},{64,7... | collective-permute-start | bytes 3145736 | tf_op jit(solution)/shard_map/ppermute | solution.py:24
  48.4 34.9 %copy-start.1 = (bf16[2,1,8,64,512]{4,3,2,1,0:T(8,128)(2,1)}, bf16[2,1,8,64,512]{4,3,2,1,0:T(8,128)(2,1)S(1)}, u32[]{:S(2)}) copy-start(bf16[2,1,8,64,512]{4,3,2,1,0:T(8,128)(2,1)S(1)} %pad_maximum_fusion.1.refs_2_.refs_3_) | copy-start | bytes 3145732
  62.1 5.9 %copy-start.5 = (bf16[2,2,4,64,512]{4,3,2,1,0:T(8,128)(2,1)}, bf16[2,2,4,64,512]{4,3,2,1,0:T(8,128)(2,1)S(1)}, u32[]{:S(2)}) copy-start(bf16[2,2,4,64,512]{4,3,2,1,0:T(8,128)(2,1)S(1)} %collective-permute-done.3.refs_1_) | copy-start | bytes 3145732
  62.1 28.3 %collective-permute-start.9 = (bf16[2,1,8,64,512]{4,3,2,1,0:T(8,128)(2,1)}, bf16[2,1,8,64,512]{4,3,2,1,0:T(8,128)(2,1)}, u32[]{:S(2)}, u32[]{:S(2)}) collective-permute-start(bf16[2,1,8,64,512]{4,3,2,1,0:T(8,128)(2,1)} %pad_maximum_fusion.refs_2_.refs_3_), channel_id=1, source_target_pairs={{8,0},{16,8},{24,16},{32,24},{40,32},{48,40},{56,48},{64,56},{72,6... | collective-permute-start | bytes 3145736 | tf_op jit(solution)/shard_map/ppermute | solution.py:24
  66.1 8.0 %copy-start.6 = (bf16[2,2,4,64,512]{4,3,2,1,0:T(8,128)(2,1)}, bf16[2,2,4,64,512]{4,3,2,1,0:T(8,128)(2,1)S(1)}, u32[]{:S(2)}) copy-start(bf16[2,2,4,64,512]{4,3,2,1,0:T(8,128)(2,1)S(1)} %collective-permute-done.4.refs_5_) | copy-start | bytes 3145732
  66.1 41.8 %collective-permute-start.10 = (bf16[2,1,8,64,512]{4,3,2,1,0:T(8,128)(2,1)S(1)}, bf16[2,1,8,64,512]{4,3,2,1,0:T(8,128)(2,1)}, u32[]{:S(2)}, u32[]{:S(2)}) collective-permute-start(bf16[2,1,8,64,512]{4,3,2,1,0:T(8,128)(2,1)S(1)} %pad_maximum_fusion.1.refs_2_.refs_3_), channel_id=1, source_target_pairs={{0,8},{8,16},{16,24},{24,32},{32,40},{40,48},{48,56},{56,64},{64,7... | collective-permute-start | bytes 3145736 | tf_op jit(solution)/shard_map/ppermute | solution.py:24
  68.1 6.1 %copy-start.3 = (bf16[2,4,4,128,128]{4,3,2,1,0:T(8,128)(2,1)}, bf16[2,4,4,128,128]{4,3,2,1,0:T(8,128)(2,1)S(1)}, u32[]{:S(2)}) copy-start(bf16[2,4,4,128,128]{4,3,2,1,0:T(8,128)(2,1)S(1)} %collective-permute-done.6.refs_8_) | copy-start | bytes 3145732
  68.1 42.9 %collective-permute-start.11 = (bf16[2,1,8,64,512]{4,3,2,1,0:T(8,128)(2,1)S(1)}, bf16[2,1,8,64,512]{4,3,2,1,0:T(8,128)(2,1)}, u32[]{:S(2)}, u32[]{:S(2)}) collective-permute-start(bf16[2,1,8,64,512]{4,3,2,1,0:T(8,128)(2,1)S(1)} %pad_maximum_fusion.1.refs_2_.refs_3_), channel_id=1, source_target_pairs={{8,0},{16,8},{24,16},{32,24},{40,32},{48,40},{56,48},{64,56},{72,6... | collective-permute-start | bytes 3145736 | tf_op jit(solution)/shard_map/ppermute | solution.py:24
  74.1 1.0 copy-start.4
  83.3 21.1 %all-to-all-start = ((s16[8,2,272,128]{3,2,1,0:T(8,128)(2,1)}), s16[8,2,272,128]{3,2,1,0:T(8,128)(2,1)S(1)}, u32[]{:S(2)}, u32[]{:S(2)}) async-start(s16[8,2,272,128]{3,2,1,0:T(8,128)(2,1)} %products.3), calls=%async_computation | async-start | bytes 2228224 | tf_op jit(solution)/shard_map/all_to_all | solution.py:368
  104.4 14.2 %all-to-all-start.1 = ((s16[8,1,272,128]{3,2,1,0:T(8,128)(2,1)}), s16[8,1,272,128]{3,2,1,0:T(8,128)(2,1)S(1)}, u32[]{:S(2)}, u32[]{:S(2)}) async-start(s16[8,1,272,128]{3,2,1,0:T(8,128)(2,1)} %products.4), calls=%async_computation.1 | async-start | bytes 1114112 | tf_op jit(solution)/shard_map/all_to_all | solution.py:368
  118.6 14.2 %all-to-all-start.2 = ((s16[8,1,272,128]{3,2,1,0:T(8,128)(2,1)}), s16[8,1,272,128]{3,2,1,0:T(8,128)(2,1)S(1)}, u32[]{:S(2)}, u32[]{:S(2)}) async-start(s16[8,1,272,128]{3,2,1,0:T(8,128)(2,1)} %products.5), calls=%async_computation.2 | async-start | bytes 1114112 | tf_op jit(solution)/shard_map/all_to_all | solution.py:368

commit v6 on v5

--- a/solution.py
+++ b/solution.py
@@ -353,7 +353,7 @@
                 block, arrived = lax.optimization_barrier((block, arrived))
                 block_after = [below_too, above_too]
             else:
-                block, block_after = lax.optimization_barrier((block, block_after))
+                block, block_after[0] = lax.optimization_barrier((block, block_after[0]))
                 below.insert(0, [(arrived[0], 0), (block_after[0], 0)])
                 above.insert(0, [(arrived[1], 0), (block_after[1], 0)])
             here.append([(block, first)])

time: 134 us -> 133 us (level)
    ppermute x8, waiting for transfers between devices: 33 us -> 35 us  [shifted(): lax.ppermute(block, 'sup', [(i, i + distance) for i in range(n) if 0 <= i...]
    all_to_all x3, waiting for transfers between devices: 20.6 us -> 18.6 us  [on_device(): terms = lax.all_to_all(partial[i], RING, 0, 0, tiled=True)]
where the time goes in v6:
time: 133 us; the launch traced here: 132 us
  waiting for transfers between devices  53.6 us (40%)
  starting transfers between devices  45.1 us (34%)
  Pallas kernels  29.9 us (22%)
  other arithmetic  3.29 us (2%)
    ppermute x8, waiting for transfers between devices, shifted(): lax.ppermute(block, 'sup', [(i, i + distance) for i in range(n) if 0 <= i...  35 us
    ppermute x8, starting transfers between devices, shifted(): lax.ppermute(block, 'sup', [(i, i + distance) for i in range(n) if 0 <= i...  29.6 us
    all_to_all x3, waiting for transfers between devices, on_device(): terms = lax.all_to_all(partial[i], RING, 0, 0, tiled=True)  18.6 us
    pallas_call x3, Pallas kernels, products(): pl.pallas_call(products_kernel, grid=(count, STEPS), in_specs=[pl.BlockSp...  17.9 us
    all_to_all x3, starting transfers between devices, on_device(): terms = lax.all_to_all(partial[i], RING, 0, 0, tiled=True)  11.6 us
    pallas_call x1, Pallas kernels, prepare(): pl.pallas_call(first_kernel, grid_spec=pltpu.PrefetchScalarGridSpec(num_s...  6.3 us
    ppermute x4, starting transfers between devices, swapped(): return lax.ppermute(block, axes, [(i, n - 1 - i) for i in range(n)])  3.9 us
    pallas_call x1, Pallas kernels, stay(): pl.pallas_call(second_kernel, grid_spec=pltpu.PrefetchScalarGridSpec(num_...  3.11 us
  transfers between devices with their start and end apart: 15, of which 7 were waited for; matrix products, arithmetic and copies ran while one was open for 2% of the time, Pallas kernels for 17%

profile of v6, /device:TPU:6, one launch (start us, length us, event | category | flops | bytes accessed | tf_op | source)
XLA Modules:
  0.0 132.5 jit_solution(6682781911161340076)
XLA Ops:
  0.0 0.6 pad_add_fusion.place
  0.6 6.3 %prepare.1 = (bf16[2,2,4,64,512]{4,3,2,1,0:T(8,128)(2,1)}, bf16[2,4,4,64,512]{4,3,2,1,0:T(8,128)(2,1)}, bf16[2,4,4,128,128]{4,3,2,1,0:T(8,128)(2,1)}, bf16[2,4,4...) custom-call(s32[3]{0:T(128)} %pad_add_fusion.place, s32[4,64]{1,0:T(4,128)} %live.1, s32[2,128]{1,0:T(2,128)} %bitcast.12, ...), custom_call_target="tpu_custom_call" | custom-call | bytes 13631488 | tf_op jit(solution)/shard_map/prepare/pallas_call | solution.py:253
  6.9 0.5 collective-permute-start.5
  7.4 3.8 %collective-permute-start.1 = (bf16[2,2,4,64,512]{4,3,2,1,0:T(8,128)(2,1)}, bf16[2,2,4,64,512]{4,3,2,1,0:T(8,128)(2,1)}, u32[]{:S(2)}, u32[]{:S(2)}) collective-permute-start(bf16[2,2,4,64,512]{4,3,2,1,0:T(8,128)(2,1)} %get-tuple-element.26.refs_2_), channel_id=1, source_target_pairs={{0,8},{8,16},{16,24},{24,32},{32,40},{40,48},{48,56},{56,64},{64,7... | collective-permute-start | bytes 3145736 | tf_op jit(solution)/shard_map/ppermute | solution.py:24
  11.3 6.1 %collective-permute-start.2 = (bf16[2,2,4,64,512]{4,3,2,1,0:T(8,128)(2,1)}, bf16[2,2,4,64,512]{4,3,2,1,0:T(8,128)(2,1)}, u32[]{:S(2)}, u32[]{:S(2)}) collective-permute-start(bf16[2,2,4,64,512]{4,3,2,1,0:T(8,128)(2,1)} %get-tuple-element.26.refs_2_), channel_id=1, source_target_pairs={{8,0},{16,8},{24,16},{32,24},{40,32},{48,40},{56,48},{64,56},{72,6... | collective-permute-start | bytes 3145736 | tf_op jit(solution)/shard_map/ppermute | solution.py:24
  17.4 3.3 %collective-permute-start.6 = (bf16[2,4,4,128,128]{4,3,2,1,0:T(8,128)(2,1)}, bf16[2,4,4,128,128]{4,3,2,1,0:T(8,128)(2,1)S(1)}, u32[]{:S(2)}, u32[]{:S(2)}) collective-permute-start(bf16[2,4,4,128,128]{4,3,2,1,0:T(8,128)(2,1)} %get-tuple-element.33), channel_id=1, source_target_pairs={{0,4},{4,0},{1,5},{5,1},{2,6},{6,2},{3,7},{7,3},{8,12},{12,8},{9,1... | collective-permute-start | bytes 3145736 | tf_op jit(solution)/shard_map/ppermute | solution.py:31
  20.7 0.1 iota_compare_fusion
  20.9 3.1 %stay.1.refs_6_ = bf16[2,4,4,192,128]{4,3,2,1,0:T(8,128)(2,1)} custom-call(s32[3]{0:T(128)} %pad_add_fusion.place, s32[2,128]{1,0:T(2,128)} %bitcast.13, bf16[2,8,4,320,128]{4,3,2,1,0:T(8,128)(2,1)} %bitcast.9, bf16[2,8,4,320,128]{4,3,2,1,0:T(8,128)(2,1)} %bitcast.10, bf16[2,8,4,320,128]{4,3,2,1,0:T(8,128)(2,1)} %bitcast.11), custom_call_target="tpu_custom_call" | custom-call | bytes 3145728 | tf_op jit(solution)/shard_map/stay/pallas_call | solution.py:300
  24.1 1.9 %collective-permute-start.3 = (bf16[2,2,4,64,512]{4,3,2,1,0:T(8,128)(2,1)S(1)}, bf16[2,2,4,64,512]{4,3,2,1,0:T(8,128)(2,1)S(1)}, u32[]{:S(2)}, u32[]{:S(2)}) collective-permute-start(bf16[2,2,4,64,512]{4,3,2,1,0:T(8,128)(2,1)S(1)} %slice.19), channel_id=1, source_target_pairs={{0,8},{8,16},{16,24},{24,32},{32,40},{40,48},{48,56},{56,64},{64,7... | collective-permute-start | bytes 3145736 | tf_op jit(solution)/shard_map/ppermute | solution.py:24
  26.1 13.6 %collective-permute-done.1.refs_0_ = bf16[2,2,4,64,512]{4,3,2,1,0:T(8,128)(2,1)} collective-permute-done((bf16[2,2,4,64,512]{4,3,2,1,0:T(8,128)(2,1)}, bf16[2,2,4,64,512]{4,3,2,1,0:T(8,128)(2,1)}, u32[]{:S(2)}, u32[]{:S(2)}) %collective-permute-start.1) | collective-permute-done | bytes 1048608 | tf_op jit(solution)/shard_map/ppermute | solution.py:24
  39.7 3.9 %collective-permute-start.4 = (bf16[2,2,4,64,512]{4,3,2,1,0:T(8,128)(2,1)S(1)}, bf16[2,2,4,64,512]{4,3,2,1,0:T(8,128)(2,1)}, u32[]{:S(2)}, u32[]{:S(2)}) collective-permute-start(bf16[2,2,4,64,512]{4,3,2,1,0:T(8,128)(2,1)S(1)} %slice.19), channel_id=1, source_target_pairs={{8,0},{16,8},{24,16},{32,24},{40,32},{48,40},{56,48},{64,56},{72,6... | collective-permute-start | bytes 3145736 | tf_op jit(solution)/shard_map/ppermute | solution.py:24
  43.7 1.4 %dynamic-slice_select_fusion = bf16[2,2,4,64,512]{4,3,2,1,0:T(8,128)(2,1)S(1)} fusion(bf16[2,8,4,64,512]{4,3,2,1,0:T(8,128)(2,1)} %refs_1_.1, s32[]{:T(128)S(6)} %select_n.7, pred[4,64,512]{2,1,0:T(8,128)(4,1)S(1)} %iota_compare_fusion), kind=kLoop, calls=%fused_computation.2 | loop fusion | flops 524288 | bytes 2228228 | tf_op jit(solution)/shard_map/jit(_where)/select_n | solution.py:340
  45.2 1.1 pad_maximum_fusion.refs_2_.refs_3_
  46.3 1.9 %collective-permute-start.8 = (bf16[2,1,8,64,512]{4,3,2,1,0:T(8,128)(2,1)}, bf16[2,1,8,64,512]{4,3,2,1,0:T(8,128)(2,1)}, u32[]{:S(2)}, u32[]{:S(2)}) collective-permute-start(bf16[2,1,8,64,512]{4,3,2,1,0:T(8,128)(2,1)} %pad_maximum_fusion.refs_2_.refs_3_), channel_id=1, source_target_pairs={{0,8},{8,16},{16,24},{24,32},{32,40},{40,48},{48,56},{56,64},{64,7... | collective-permute-start | bytes 3145736 | tf_op jit(solution)/shard_map/ppermute | solution.py:24
  48.4 13.7 %collective-permute-done.3.refs_1_ = bf16[2,2,4,64,512]{4,3,2,1,0:T(8,128)(2,1)S(1)} collective-permute-done((bf16[2,2,4,64,512]{4,3,2,1,0:T(8,128)(2,1)S(1)}, bf16[2,2,4,64,512]{4,3,2,1,0:T(8,128)(2,1)S(1)}, u32[]{:S(2)}, u32[]{:S(2)}) %collective-permute-start.3) | collective-permute-done | bytes 1048608 | tf_op jit(solution)/shard_map/ppermute | solution.py:24
  62.1 4.0 %collective-permute-start.9 = (bf16[2,1,8,64,512]{4,3,2,1,0:T(8,128)(2,1)}, bf16[2,1,8,64,512]{4,3,2,1,0:T(8,128)(2,1)}, u32[]{:S(2)}, u32[]{:S(2)}) collective-permute-start(bf16[2,1,8,64,512]{4,3,2,1,0:T(8,128)(2,1)} %pad_maximum_fusion.refs_2_.refs_3_), channel_id=1, source_target_pairs={{8,0},{16,8},{24,16},{32,24},{40,32},{48,40},{56,48},{64,56},{72,6... | collective-permute-start | bytes 3145736 | tf_op jit(solution)/shard_map/ppermute | solution.py:24
  66.0 1.9 %collective-permute-start.10 = (bf16[2,1,8,64,512]{4,3,2,1,0:T(8,128)(2,1)S(1)}, bf16[2,1,8,64,512]{4,3,2,1,0:T(8,128)(2,1)}, u32[]{:S(2)}, u32[]{:S(2)}) collective-permute-start(bf16[2,1,8,64,512]{4,3,2,1,0:T(8,128)(2,1)S(1)} %pad_maximum_fusion.1.refs_2_.refs_3_), channel_id=1, source_target_pairs={{0,8},{8,16},{16,24},{24,32},{32,40},{40,48},{48,56},{56,64},{64,7... | collective-permute-start | bytes 3145736 | tf_op jit(solution)/shard_map/ppermute | solution.py:24
  68.0 6.0 %collective-permute-start.11 = (bf16[2,1,8,64,512]{4,3,2,1,0:T(8,128)(2,1)S(1)}, bf16[2,1,8,64,512]{4,3,2,1,0:T(8,128)(2,1)}, u32[]{:S(2)}, u32[]{:S(2)}) collective-permute-start(bf16[2,1,8,64,512]{4,3,2,1,0:T(8,128)(2,1)S(1)} %pad_maximum_fusion.1.refs_2_.refs_3_), channel_id=1, source_target_pairs={{8,0},{16,8},{24,16},{32,24},{40,32},{48,40},{56,48},{64,56},{72,6... | collective-permute-start | bytes 3145736 | tf_op jit(solution)/shard_map/ppermute | solution.py:24
  74.1 8.1 %products.3 = s16[8,2,272,128]{3,2,1,0:T(8,128)(2,1)} custom-call(s32[3]{0:T(128)} %pad_add_fusion.place, bf16[2,2,4,64,512]{4,3,2,1,0:T(8,128)(2,1)} %collective-permute-done.1.refs_0_, bf16[2,2,4,64,512]{4,3,2,1,0:T(8,128)(2,1)} %copy-done.5, bf16[2,2,4,64,512]{4,3,2,1,0:T(8,128)(2,1)} %get-tuple-element.26.refs_2_, bf16[2,4,4,64,512]{4,3,2,1,0:T(8,128)(2,1)} %copy-done, ...), custom_call_target="tpu_custom_call" | custom-call | flops 38654705664 | bytes 1048576 | tf_op jit(solution)/shard_map/products/pallas_call | solution.py:121
  82.2 4.5 %all-to-all-start = ((s16[8,2,272,128]{3,2,1,0:T(8,128)(2,1)}), s16[8,2,272,128]{3,2,1,0:T(8,128)(2,1)S(1)}, u32[]{:S(2)}, u32[]{:S(2)}) async-start(s16[8,2,272,128]{3,2,1,0:T(8,128)(2,1)} %products.3), calls=%async_computation | async-start | bytes 2228224 | tf_op jit(solution)/shard_map/all_to_all | solution.py:368
  86.7 3.7 %collective-permute-done.9.refs_4_.refs_5_ = bf16[2,1,8,64,512]{4,3,2,1,0:T(8,128)(2,1)} collective-permute-done((bf16[2,1,8,64,512]{4,3,2,1,0:T(8,128)(2,1)}, bf16[2,1,8,64,512]{4,3,2,1,0:T(8,128)(2,1)}, u32[]{:S(2)}, u32[]{:S(2)}) %collective-permute-start.9) | collective-permute-done | bytes 1048608 | tf_op jit(solution)/shard_map/ppermute | solution.py:24
  90.4 4.9 %products.4 = s16[8,1,272,128]{3,2,1,0:T(8,128)(2,1)} custom-call(s32[3]{0:T(128)} %pad_add_fusion.place, bf16[2,1,8,64,512]{4,3,2,1,0:T(8,128)(2,1)} %collective-permute-done.8.refs_0_.refs_1_, bf16[2,1,8,64,512]{4,3,2,1,0:T(8,128)(2,1)} %collective-permute-done.8.refs_0_.refs_1_, bf16[2,1,8,64,512]{4,3,2,1,0:T(8,128)(2,1)} %pad_maximum_fusion.refs_2_.refs_3_, ...), custom_call_target="tpu_custom_call" | custom-call | flops 19327352832 | bytes 1048576 | tf_op jit(solution)/shard_map/products/pallas_call | solution.py:121
  95.3 8.1 %all-to-all-done.terms = s16[8,2,272,128]{3,2,1,0:T(8,128)(2,1)S(1)} async-done(((s16[8,2,272,128]{3,2,1,0:T(8,128)(2,1)}), s16[8,2,272,128]{3,2,1,0:T(8,128)(2,1)S(1)}, u32[]{:S(2)}, u32[]{:S(2)}) %all-to-all-start) | async-done | bytes 1114144 | tf_op jit(solution)/shard_map/all_to_all | solution.py:368
  103.3 3.5 %all-to-all-start.1 = ((s16[8,1,272,128]{3,2,1,0:T(8,128)(2,1)}), s16[8,1,272,128]{3,2,1,0:T(8,128)(2,1)S(1)}, u32[]{:S(2)}, u32[]{:S(2)}) async-start(s16[8,1,272,128]{3,2,1,0:T(8,128)(2,1)} %products.4), calls=%async_computation.1 | async-start | bytes 1114112 | tf_op jit(solution)/shard_map/all_to_all | solution.py:368
  106.9 4.0 %collective-permute-done.11.refs_4_.refs_5_ = bf16[2,1,8,64,512]{4,3,2,1,0:T(8,128)(2,1)} collective-permute-done((bf16[2,1,8,64,512]{4,3,2,1,0:T(8,128)(2,1)S(1)}, bf16[2,1,8,64,512]{4,3,2,1,0:T(8,128)(2,1)}, u32[]{:S(2)}, u32[]{:S(2)}) %collective-permute-start.11) | collective-permute-done | bytes 1048608 | tf_op jit(solution)/shard_map/ppermute | solution.py:24
  110.9 4.9 %products.5 = s16[8,1,272,128]{3,2,1,0:T(8,128)(2,1)} custom-call(s32[3]{0:T(128)} %pad_add_fusion.place, bf16[2,1,8,64,512]{4,3,2,1,0:T(8,128)(2,1)} %collective-permute-done.10.refs_0_.refs_1_, bf16[2,1,8,64,512]{4,3,2,1,0:T(8,128)(2,1)} %collective-permute-done.10.refs_0_.refs_1_, bf16[2,1,8,64,512]{4,3,2,1,0:T(8,128)(2,1)} %copy-done.1, ...), custom_call_target="tpu_custom_call" | custom-call | flops 19327352832 | bytes 1048576 | tf_op jit(solution)/shard_map/products/pallas_call | solution.py:121
  115.7 1.8 %all-to-all-done.1.terms = s16[8,1,272,128]{3,2,1,0:T(8,128)(2,1)S(1)} async-done(((s16[8,1,272,128]{3,2,1,0:T(8,128)(2,1)}), s16[8,1,272,128]{3,2,1,0:T(8,128)(2,1)S(1)}, u32[]{:S(2)}, u32[]{:S(2)}) %all-to-all-start.1) | async-done | bytes 557088 | tf_op jit(solution)/shard_map/all_to_all | solution.py:368
  117.5 3.5 %all-to-all-start.2 = ((s16[8,1,272,128]{3,2,1,0:T(8,128)(2,1)}), s16[8,1,272,128]{3,2,1,0:T(8,128)(2,1)S(1)}, u32[]{:S(2)}, u32[]{:S(2)}) async-start(s16[8,1,272,128]{3,2,1,0:T(8,128)(2,1)} %products.5), calls=%async_computation.2 | async-start | bytes 1114112 | tf_op jit(solution)/shard_map/all_to_all | solution.py:368
  121.0 1.1 finish.3.refs_0_
  122.1 0.8 finish.4.refs_0_
  122.9 8.8 %all-to-all-done.2.terms = s16[8,1,272,128]{3,2,1,0:T(8,128)(2,1)S(1)} async-done(((s16[8,1,272,128]{3,2,1,0:T(8,128)(2,1)}), s16[8,1,272,128]{3,2,1,0:T(8,128)(2,1)S(1)}, u32[]{:S(2)}, u32[]{:S(2)}) %all-to-all-start.2) | async-done | bytes 557088 | tf_op jit(solution)/shard_map/all_to_all | solution.py:368
  131.7 0.8 finish.5
  (26 shorter events, 0.5 us)
Async XLA Ops:
  0.6 20.1 %copy-start.2 = (s32[4,64]{1,0:T(4,128)S(1)}, s32[4,64]{1,0:T(4,128)}, u32[]{:S(2)}) copy-start(s32[4,64]{1,0:T(4,128)} %live.1) | copy-start | bytes 3076
  6.9 17.1 %collective-permute-start = (bf16[2,4,4,64,512]{4,3,2,1,0:T(8,128)(2,1)}, bf16[2,4,4,64,512]{4,3,2,1,0:T(8,128)(2,1)S(1)}, u32[]{:S(2)}, u32[]{:S(2)}) collective-permute-start(bf16[2,4,4,64,512]{4,3,2,1,0:T(8,128)(2,1)} %get-tuple-element.23), channel_id=1, source_target_pairs={{0,1},{1,0},{2,3},{3,2},{4,5},{5,4},{6,7},{7,6},{8,9},{9,8},{10,11... | collective-permute-start | bytes 6291464 | tf_op jit(solution)/shard_map/ppermute | solution.py:31
  6.9 13.9 %collective-permute-start.5 = (bf16[2,4,4,192,128]{4,3,2,1,0:T(8,128)(2,1)}, bf16[2,4,4,192,128]{4,3,2,1,0:T(8,128)(2,1)}, u32[]{:S(2)}, u32[]{:S(2)}) collective-permute-start(bf16[2,4,4,192,128]{4,3,2,1,0:T(8,128)(2,1)} %get-tuple-element.30), channel_id=1, source_target_pairs={{0,1},{1,0},{2,3},{3,2},{4,5},{5,4},{6,7},{7,6},{8,9},{9,8},{10,11... | collective-permute-start | bytes 4718600 | tf_op jit(solution)/shard_map/ppermute | solution.py:31
  7.4 32.3 %collective-permute-start.1 = (bf16[2,2,4,64,512]{4,3,2,1,0:T(8,128)(2,1)}, bf16[2,2,4,64,512]{4,3,2,1,0:T(8,128)(2,1)}, u32[]{:S(2)}, u32[]{:S(2)}) collective-permute-start(bf16[2,2,4,64,512]{4,3,2,1,0:T(8,128)(2,1)} %get-tuple-element.26.refs_2_), channel_id=1, source_target_pairs={{0,8},{8,16},{16,24},{24,32},{32,40},{40,48},{48,56},{56,64},{64,7... | collective-permute-start | bytes 3145736 | tf_op jit(solution)/shard_map/ppermute | solution.py:24
  11.3 35.1 %collective-permute-start.2 = (bf16[2,2,4,64,512]{4,3,2,1,0:T(8,128)(2,1)}, bf16[2,2,4,64,512]{4,3,2,1,0:T(8,128)(2,1)}, u32[]{:S(2)}, u32[]{:S(2)}) collective-permute-start(bf16[2,2,4,64,512]{4,3,2,1,0:T(8,128)(2,1)} %get-tuple-element.26.refs_2_), channel_id=1, source_target_pairs={{8,0},{16,8},{24,16},{32,24},{40,32},{48,40},{56,48},{64,56},{72,6... | collective-permute-start | bytes 3145736 | tf_op jit(solution)/shard_map/ppermute | solution.py:24
  17.4 48.6 %collective-permute-start.6 = (bf16[2,4,4,128,128]{4,3,2,1,0:T(8,128)(2,1)}, bf16[2,4,4,128,128]{4,3,2,1,0:T(8,128)(2,1)S(1)}, u32[]{:S(2)}, u32[]{:S(2)}) collective-permute-start(bf16[2,4,4,128,128]{4,3,2,1,0:T(8,128)(2,1)} %get-tuple-element.33), channel_id=1, source_target_pairs={{0,4},{4,0},{1,5},{5,1},{2,6},{6,2},{3,7},{7,3},{8,12},{12,8},{9,1... | collective-permute-start | bytes 3145736 | tf_op jit(solution)/shard_map/ppermute | solution.py:31
  20.8 47.2 %collective-permute-start.7 = (bf16[2,4,4,128,128]{4,3,2,1,0:T(8,128)(2,1)}, bf16[2,4,4,128,128]{4,3,2,1,0:T(8,128)(2,1)S(1)}, u32[]{:S(2)}, u32[]{:S(2)}) collective-permute-start(bf16[2,4,4,128,128]{4,3,2,1,0:T(8,128)(2,1)} %get-tuple-element.34), channel_id=1, source_target_pairs={{0,5},{1,4},{4,1},{5,0},{2,7},{3,6},{6,3},{7,2},{8,13},{9,12},{12,... | collective-permute-start | bytes 3145736 | tf_op jit(solution)/shard_map/ppermute | solution.py:31
  24.0 21.0 %copy-start = (bf16[2,4,4,64,512]{4,3,2,1,0:T(8,128)(2,1)}, bf16[2,4,4,64,512]{4,3,2,1,0:T(8,128)(2,1)S(1)}, u32[]{:S(2)}) copy-start(bf16[2,4,4,64,512]{4,3,2,1,0:T(8,128)(2,1)S(1)} %collective-permute-done.refs_3_) | copy-start | bytes 6291460
  24.1 37.9 %collective-permute-start.3 = (bf16[2,2,4,64,512]{4,3,2,1,0:T(8,128)(2,1)S(1)}, bf16[2,2,4,64,512]{4,3,2,1,0:T(8,128)(2,1)S(1)}, u32[]{:S(2)}, u32[]{:S(2)}) collective-permute-start(bf16[2,2,4,64,512]{4,3,2,1,0:T(8,128)(2,1)S(1)} %slice.19), channel_id=1, source_target_pairs={{0,8},{8,16},{16,24},{24,32},{32,40},{40,48},{48,56},{56,64},{64,7... | collective-permute-start | bytes 3145736 | tf_op jit(solution)/shard_map/ppermute | solution.py:24
  39.7 34.3 %collective-permute-start.4 = (bf16[2,2,4,64,512]{4,3,2,1,0:T(8,128)(2,1)S(1)}, bf16[2,2,4,64,512]{4,3,2,1,0:T(8,128)(2,1)}, u32[]{:S(2)}, u32[]{:S(2)}) collective-permute-start(bf16[2,2,4,64,512]{4,3,2,1,0:T(8,128)(2,1)S(1)} %slice.19), channel_id=1, source_target_pairs={{8,0},{16,8},{24,16},{32,24},{40,32},{48,40},{56,48},{64,56},{72,6... | collective-permute-start | bytes 3145736 | tf_op jit(solution)/shard_map/ppermute | solution.py:24
  46.3 40.3 %collective-permute-start.8 = (bf16[2,1,8,64,512]{4,3,2,1,0:T(8,128)(2,1)}, bf16[2,1,8,64,512]{4,3,2,1,0:T(8,128)(2,1)}, u32[]{:S(2)}, u32[]{:S(2)}) collective-permute-start(bf16[2,1,8,64,512]{4,3,2,1,0:T(8,128)(2,1)} %pad_maximum_fusion.refs_2_.refs_3_), channel_id=1, source_target_pairs={{0,8},{8,16},{16,24},{24,32},{32,40},{40,48},{48,56},{56,64},{64,7... | collective-permute-start | bytes 3145736 | tf_op jit(solution)/shard_map/ppermute | solution.py:24
  48.4 33.8 %copy-start.1 = (bf16[2,1,8,64,512]{4,3,2,1,0:T(8,128)(2,1)}, bf16[2,1,8,64,512]{4,3,2,1,0:T(8,128)(2,1)S(1)}, u32[]{:S(2)}) copy-start(bf16[2,1,8,64,512]{4,3,2,1,0:T(8,128)(2,1)S(1)} %pad_maximum_fusion.1.refs_2_.refs_3_) | copy-start | bytes 3145732
  62.1 5.9 %copy-start.5 = (bf16[2,2,4,64,512]{4,3,2,1,0:T(8,128)(2,1)}, bf16[2,2,4,64,512]{4,3,2,1,0:T(8,128)(2,1)S(1)}, u32[]{:S(2)}) copy-start(bf16[2,2,4,64,512]{4,3,2,1,0:T(8,128)(2,1)S(1)} %collective-permute-done.3.refs_1_) | copy-start | bytes 3145732
  62.1 28.3 %collective-permute-start.9 = (bf16[2,1,8,64,512]{4,3,2,1,0:T(8,128)(2,1)}, bf16[2,1,8,64,512]{4,3,2,1,0:T(8,128)(2,1)}, u32[]{:S(2)}, u32[]{:S(2)}) collective-permute-start(bf16[2,1,8,64,512]{4,3,2,1,0:T(8,128)(2,1)} %pad_maximum_fusion.refs_2_.refs_3_), channel_id=1, source_target_pairs={{8,0},{16,8},{24,16},{32,24},{40,32},{48,40},{56,48},{64,56},{72,6... | collective-permute-start | bytes 3145736 | tf_op jit(solution)/shard_map/ppermute | solution.py:24
  66.0 8.0 %copy-start.3 = (bf16[2,4,4,128,128]{4,3,2,1,0:T(8,128)(2,1)}, bf16[2,4,4,128,128]{4,3,2,1,0:T(8,128)(2,1)S(1)}, u32[]{:S(2)}) copy-start(bf16[2,4,4,128,128]{4,3,2,1,0:T(8,128)(2,1)S(1)} %collective-permute-done.6.refs_8_) | copy-start | bytes 3145732
  66.0 40.8 %collective-permute-start.10 = (bf16[2,1,8,64,512]{4,3,2,1,0:T(8,128)(2,1)S(1)}, bf16[2,1,8,64,512]{4,3,2,1,0:T(8,128)(2,1)}, u32[]{:S(2)}, u32[]{:S(2)}) collective-permute-start(bf16[2,1,8,64,512]{4,3,2,1,0:T(8,128)(2,1)S(1)} %pad_maximum_fusion.1.refs_2_.refs_3_), channel_id=1, source_target_pairs={{0,8},{8,16},{16,24},{24,32},{32,40},{40,48},{48,56},{56,64},{64,7... | collective-permute-start | bytes 3145736 | tf_op jit(solution)/shard_map/ppermute | solution.py:24
  68.0 6.1 %copy-start.4 = (bf16[2,4,4,128,128]{4,3,2,1,0:T(8,128)(2,1)}, bf16[2,4,4,128,128]{4,3,2,1,0:T(8,128)(2,1)S(1)}, u32[]{:S(2)}) copy-start(bf16[2,4,4,128,128]{4,3,2,1,0:T(8,128)(2,1)S(1)} %collective-permute-done.7.refs_9_) | copy-start | bytes 3145732
  68.0 42.9 %collective-permute-start.11 = (bf16[2,1,8,64,512]{4,3,2,1,0:T(8,128)(2,1)S(1)}, bf16[2,1,8,64,512]{4,3,2,1,0:T(8,128)(2,1)}, u32[]{:S(2)}, u32[]{:S(2)}) collective-permute-start(bf16[2,1,8,64,512]{4,3,2,1,0:T(8,128)(2,1)S(1)} %pad_maximum_fusion.1.refs_2_.refs_3_), channel_id=1, source_target_pairs={{8,0},{16,8},{24,16},{32,24},{40,32},{48,40},{56,48},{64,56},{72,6... | collective-permute-start | bytes 3145736 | tf_op jit(solution)/shard_map/ppermute | solution.py:24
  82.2 21.1 %all-to-all-start = ((s16[8,2,272,128]{3,2,1,0:T(8,128)(2,1)}), s16[8,2,272,128]{3,2,1,0:T(8,128)(2,1)S(1)}, u32[]{:S(2)}, u32[]{:S(2)}) async-start(s16[8,2,272,128]{3,2,1,0:T(8,128)(2,1)} %products.3), calls=%async_computation | async-start | bytes 2228224 | tf_op jit(solution)/shard_map/all_to_all | solution.py:368
  103.3 14.2 %all-to-all-start.1 = ((s16[8,1,272,128]{3,2,1,0:T(8,128)(2,1)}), s16[8,1,272,128]{3,2,1,0:T(8,128)(2,1)S(1)}, u32[]{:S(2)}, u32[]{:S(2)}) async-start(s16[8,1,272,128]{3,2,1,0:T(8,128)(2,1)} %products.4), calls=%async_computation.1 | async-start | bytes 1114112 | tf_op jit(solution)/shard_map/all_to_all | solution.py:368
  117.5 14.2 %all-to-all-start.2 = ((s16[8,1,272,128]{3,2,1,0:T(8,128)(2,1)}), s16[8,1,272,128]{3,2,1,0:T(8,128)(2,1)S(1)}, u32[]{:S(2)}, u32[]{:S(2)}) async-start(s16[8,1,272,128]{3,2,1,0:T(8,128)(2,1)} %products.5), calls=%async_computation.2 | async-start | bytes 1114112 | tf_op jit(solution)/shard_map/all_to_all | solution.py:368

commit v7 on v6

--- a/solution.py
+++ b/solution.py
@@ -31,10 +31,22 @@
     return lax.ppermute(block, axes, [(i, n - 1 - i) for i in range(n)])
 
 
+def core_of(place):
+    return place[0] & 1
+
+
+def half_of(place):
+    return (place[0] >> 2) & 1
+
+
+def first_of(place, pts):
+    return (place[0] >> 2) * pts - 2 * pts
+
+
 def products_kernel(place, *refs):
     out, total = refs[-2:]
     windows, own, cross = (refs[0:2], refs[2:4], refs[4:6]), refs[6:8], refs[8:10]
-    half = place[0]
+    half = half_of(place)
     upper = half == 1
     pts, recv = windows[0][0].shape[3:]
     shots = own[0].shape[4]
@@ -208,7 +220,7 @@
     @pl.when(pl.program_id(0) == 0)
     def _():
         keep_live(live, kept)
-        keep_inside(place[2], aperture, inside)
+        keep_inside(first_of(place, inside.shape[0] // 5), aperture, inside)
         for part in range(2):
             for freq in range(early.shape[1]):
                 early[part, freq] = mine[part, freq] * kept[...]
@@ -225,7 +237,7 @@
 def second_kernel(place, aperture, below, here, above, staying, inside):
     @pl.when(pl.program_id(0) == 0)
     def _():
-        keep_inside(place[2], aperture, inside)
+        keep_inside(first_of(place, inside.shape[0] // 5), aperture, inside)
 
     for k, source in enumerate((below, here, above)):
         put_masked(source, 0, staying, k, 2 * k, inside)
@@ -242,7 +254,7 @@
 
     def source(other, at, rows):
         def index(i, place):
-            return (0, (place[1] ^ other) * steps + i, 0, at, 0)
+            return (0, (core_of(place) ^ other) * steps + i, 0, at, 0)
 
         return pl.BlockSpec(block(rows, width), index)
 
@@ -258,9 +270,9 @@
             in_specs=[
                 pl.BlockSpec((xs, pts), lambda i, place: (0, 0)),
                 pl.BlockSpec((2, width), lambda i, place: (0, 0)),
-                pl.BlockSpec(block(pts, recv), lambda i, place: (0, place[1] * steps, 0, 0, 0)),
+                pl.BlockSpec(block(pts, recv), lambda i, place: (0, core_of(place) * steps, 0, 0, 0)),
                 pl.BlockSpec(
-                    block(pts, recv), lambda i, place: (0, (1 - place[1]) * steps + i, 0, 0, 0)
+                    block(pts, recv), lambda i, place: (0, (1 - core_of(place)) * steps + i, 0, 0, 0)
                 ),
                 source(0, 1, pts),
                 source(0, 3, pts),
@@ -294,7 +306,7 @@
 
     def source(at):
         return pl.BlockSpec(
-            (2, FIRST, xs, pts, width), lambda i, place: (0, place[1] * steps + i, 0, at, 0)
+            (2, FIRST, xs, pts, width), lambda i, place: (0, core_of(place) * steps + i, 0, at, 0)
         )
 
     return pl.pallas_call(
@@ -321,8 +333,7 @@
     spread = source_gathers.shape[4]
     half, core = lax.axis_index("half"), lax.axis_index("core")
     count = freqs_here // 2
-    first_point = (2 * lax.axis_index("sup") + half) * pts - (spread - pts) // 2
-    place = jnp.stack([half, core, first_point]).astype(jnp.int32)
+    place = lax.axis_index(SHOT + XLINE).astype(jnp.int32).reshape(1)
 
     shots = source_gathers.transpose(0, 1, 3, 4, 2)
     early, leaving, crossing, cross_leaving, shots_leaving = prepare(

time: 133 us -> 132 us (level)
  Pallas kernels: 29.9 us -> 28.5 us
where the time goes in v7:
time: 132 us; the launch traced here: 131 us
  waiting for transfers between devices  54.3 us (41%)
  starting transfers between devices  45.1 us (34%)
  Pallas kernels  28.5 us (22%)
  other arithmetic  2.7 us (2%)
    ppermute x8, waiting for transfers between devices, shifted(): lax.ppermute(block, 'sup', [(i, i + distance) for i in range(n) if 0 <= i...  35.7 us
    ppermute x8, starting transfers between devices, shifted(): lax.ppermute(block, 'sup', [(i, i + distance) for i in range(n) if 0 <= i...  29.6 us
    all_to_all x3, waiting for transfers between devices, on_device(): terms = lax.all_to_all(partial[i], RING, 0, 0, tiled=True)  18.6 us
    pallas_call x3, Pallas kernels, products(): pl.pallas_call(products_kernel, grid=(count, STEPS), in_specs=[pl.BlockSp...  17.8 us
    all_to_all x3, starting transfers between devices, on_device(): terms = lax.all_to_all(partial[i], RING, 0, 0, tiled=True)  11.6 us
    pallas_call x1, Pallas kernels, prepare(): pl.pallas_call(first_kernel, grid_spec=pltpu.PrefetchScalarGridSpec(num_s...  5.6 us
    ppermute x4, starting transfers between devices, swapped(): return lax.ppermute(block, axes, [(i, n - 1 - i) for i in range(n)])  3.9 us
    pallas_call x3, Pallas kernels, finish(): pl.pallas_call(finish_kernel, grid=(size,), in_specs=[pl.BlockSpec((8, 1,...  2.66 us
  transfers between devices with their start and end apart: 15, of which 7 were waited for; matrix products, arithmetic and copies ran while one was open for 2% of the time, Pallas kernels for 17%

profile of v7, /device:TPU:6, one launch (start us, length us, event | category | flops | bytes accessed | tf_op | source)
XLA Modules:
  0.0 131.1 jit_solution(2049247540071526504)
XLA Ops:
  0.0 5.6 %prepare.1 = (bf16[2,2,4,64,512]{4,3,2,1,0:T(8,128)(2,1)}, bf16[2,4,4,64,512]{4,3,2,1,0:T(8,128)(2,1)}, bf16[2,4,4,128,128]{4,3,2,1,0:T(8,128)(2,1)}, bf16[2,4,4...) custom-call(s32[1]{0:T(128)} %bitcast.place, s32[4,64]{1,0:T(4,128)} %live.1, s32[2,128]{1,0:T(2,128)} %bitcast.10, ...), custom_call_target="tpu_custom_call" | custom-call | bytes 13631488 | tf_op jit(solution)/shard_map/prepare/pallas_call | solution.py:265
  5.6 0.5 collective-permute-start.5
  6.1 3.8 %collective-permute-start.1 = (bf16[2,2,4,64,512]{4,3,2,1,0:T(8,128)(2,1)}, bf16[2,2,4,64,512]{4,3,2,1,0:T(8,128)(2,1)}, u32[]{:S(2)}, u32[]{:S(2)}) collective-permute-start(bf16[2,2,4,64,512]{4,3,2,1,0:T(8,128)(2,1)} %get-tuple-element.26.refs_2_), channel_id=1, source_target_pairs={{0,8},{8,16},{16,24},{24,32},{32,40},{40,48},{48,56},{56,64},{64,7... | collective-permute-start | bytes 3145736 | tf_op jit(solution)/shard_map/ppermute | solution.py:24
  10.0 6.1 %collective-permute-start.2 = (bf16[2,2,4,64,512]{4,3,2,1,0:T(8,128)(2,1)}, bf16[2,2,4,64,512]{4,3,2,1,0:T(8,128)(2,1)}, u32[]{:S(2)}, u32[]{:S(2)}) collective-permute-start(bf16[2,2,4,64,512]{4,3,2,1,0:T(8,128)(2,1)} %get-tuple-element.26.refs_2_), channel_id=1, source_target_pairs={{8,0},{16,8},{24,16},{32,24},{40,32},{48,40},{56,48},{64,56},{72,6... | collective-permute-start | bytes 3145736 | tf_op jit(solution)/shard_map/ppermute | solution.py:24
  16.1 3.3 %collective-permute-start.6 = (bf16[2,4,4,128,128]{4,3,2,1,0:T(8,128)(2,1)}, bf16[2,4,4,128,128]{4,3,2,1,0:T(8,128)(2,1)S(1)}, u32[]{:S(2)}, u32[]{:S(2)}) collective-permute-start(bf16[2,4,4,128,128]{4,3,2,1,0:T(8,128)(2,1)} %get-tuple-element.33), channel_id=1, source_target_pairs={{0,4},{4,0},{1,5},{5,1},{2,6},{6,2},{3,7},{7,3},{8,12},{12,8},{9,1... | collective-permute-start | bytes 3145736 | tf_op jit(solution)/shard_map/ppermute | solution.py:31
  19.4 0.1 iota_compare_fusion
  19.6 2.5 %stay.1.refs_6_ = bf16[2,4,4,192,128]{4,3,2,1,0:T(8,128)(2,1)} custom-call(s32[1]{0:T(128)} %bitcast.place, s32[2,128]{1,0:T(2,128)} %bitcast.11, bf16[2,8,4,320,128]{4,3,2,1,0:T(8,128)(2,1)} %bitcast.7, bf16[2,8,4,320,128]{4,3,2,1,0:T(8,128)(2,1)} %bitcast.8, bf16[2,8,4,320,128]{4,3,2,1,0:T(8,128)(2,1)} %bitcast.9), custom_call_target="tpu_custom_call" | custom-call | bytes 3145728 | tf_op jit(solution)/shard_map/stay/pallas_call | solution.py:312
  22.2 1.9 %collective-permute-start.3 = (bf16[2,2,4,64,512]{4,3,2,1,0:T(8,128)(2,1)S(1)}, bf16[2,2,4,64,512]{4,3,2,1,0:T(8,128)(2,1)S(1)}, u32[]{:S(2)}, u32[]{:S(2)}) collective-permute-start(bf16[2,2,4,64,512]{4,3,2,1,0:T(8,128)(2,1)S(1)} %slice.19), channel_id=1, source_target_pairs={{0,8},{8,16},{16,24},{24,32},{32,40},{40,48},{48,56},{56,64},{64,7... | collective-permute-start | bytes 3145736 | tf_op jit(solution)/shard_map/ppermute | solution.py:24
  24.1 14.3 %collective-permute-done.1.refs_0_ = bf16[2,2,4,64,512]{4,3,2,1,0:T(8,128)(2,1)} collective-permute-done((bf16[2,2,4,64,512]{4,3,2,1,0:T(8,128)(2,1)}, bf16[2,2,4,64,512]{4,3,2,1,0:T(8,128)(2,1)}, u32[]{:S(2)}, u32[]{:S(2)}) %collective-permute-start.1) | collective-permute-done | bytes 1048608 | tf_op jit(solution)/shard_map/ppermute | solution.py:24
  38.4 3.9 %collective-permute-start.4 = (bf16[2,2,4,64,512]{4,3,2,1,0:T(8,128)(2,1)S(1)}, bf16[2,2,4,64,512]{4,3,2,1,0:T(8,128)(2,1)}, u32[]{:S(2)}, u32[]{:S(2)}) collective-permute-start(bf16[2,2,4,64,512]{4,3,2,1,0:T(8,128)(2,1)S(1)} %slice.19), channel_id=1, source_target_pairs={{8,0},{16,8},{24,16},{32,24},{40,32},{48,40},{56,48},{64,56},{72,6... | collective-permute-start | bytes 3145736 | tf_op jit(solution)/shard_map/ppermute | solution.py:24
  42.4 1.4 %dynamic-slice_select_fusion = bf16[2,2,4,64,512]{4,3,2,1,0:T(8,128)(2,1)S(1)} fusion(bf16[2,8,4,64,512]{4,3,2,1,0:T(8,128)(2,1)} %refs_1_.1, s32[]{:T(128)S(6)} %select_n.7, pred[4,64,512]{2,1,0:T(8,128)(4,1)S(1)} %iota_compare_fusion), kind=kLoop, calls=%fused_computation.2 | loop fusion | flops 524288 | bytes 2228228 | tf_op jit(solution)/shard_map/jit(_where)/select_n | solution.py:351
  43.9 1.1 pad_maximum_fusion.refs_2_.refs_3_
  45.0 1.9 %collective-permute-start.8 = (bf16[2,1,8,64,512]{4,3,2,1,0:T(8,128)(2,1)}, bf16[2,1,8,64,512]{4,3,2,1,0:T(8,128)(2,1)}, u32[]{:S(2)}, u32[]{:S(2)}) collective-permute-start(bf16[2,1,8,64,512]{4,3,2,1,0:T(8,128)(2,1)} %pad_maximum_fusion.refs_2_.refs_3_), channel_id=1, source_target_pairs={{0,8},{8,16},{16,24},{24,32},{32,40},{40,48},{48,56},{56,64},{64,7... | collective-permute-start | bytes 3145736 | tf_op jit(solution)/shard_map/ppermute | solution.py:24
  47.0 0.1 pad_maximum_fusion.1.refs_2_.refs_3_
  47.1 13.7 %collective-permute-done.3.refs_1_ = bf16[2,2,4,64,512]{4,3,2,1,0:T(8,128)(2,1)S(1)} collective-permute-done((bf16[2,2,4,64,512]{4,3,2,1,0:T(8,128)(2,1)S(1)}, bf16[2,2,4,64,512]{4,3,2,1,0:T(8,128)(2,1)S(1)}, u32[]{:S(2)}, u32[]{:S(2)}) %collective-permute-start.3) | collective-permute-done | bytes 1048608 | tf_op jit(solution)/shard_map/ppermute | solution.py:24
  60.8 4.0 %collective-permute-start.9 = (bf16[2,1,8,64,512]{4,3,2,1,0:T(8,128)(2,1)}, bf16[2,1,8,64,512]{4,3,2,1,0:T(8,128)(2,1)}, u32[]{:S(2)}, u32[]{:S(2)}) collective-permute-start(bf16[2,1,8,64,512]{4,3,2,1,0:T(8,128)(2,1)} %pad_maximum_fusion.refs_2_.refs_3_), channel_id=1, source_target_pairs={{8,0},{16,8},{24,16},{32,24},{40,32},{48,40},{56,48},{64,56},{72,6... | collective-permute-start | bytes 3145736 | tf_op jit(solution)/shard_map/ppermute | solution.py:24
  64.8 1.9 %collective-permute-start.10 = (bf16[2,1,8,64,512]{4,3,2,1,0:T(8,128)(2,1)S(1)}, bf16[2,1,8,64,512]{4,3,2,1,0:T(8,128)(2,1)}, u32[]{:S(2)}, u32[]{:S(2)}) collective-permute-start(bf16[2,1,8,64,512]{4,3,2,1,0:T(8,128)(2,1)S(1)} %pad_maximum_fusion.1.refs_2_.refs_3_), channel_id=1, source_target_pairs={{0,8},{8,16},{16,24},{24,32},{32,40},{40,48},{48,56},{56,64},{64,7... | collective-permute-start | bytes 3145736 | tf_op jit(solution)/shard_map/ppermute | solution.py:24
  66.7 6.0 %collective-permute-start.11 = (bf16[2,1,8,64,512]{4,3,2,1,0:T(8,128)(2,1)S(1)}, bf16[2,1,8,64,512]{4,3,2,1,0:T(8,128)(2,1)}, u32[]{:S(2)}, u32[]{:S(2)}) collective-permute-start(bf16[2,1,8,64,512]{4,3,2,1,0:T(8,128)(2,1)S(1)} %pad_maximum_fusion.1.refs_2_.refs_3_), channel_id=1, source_target_pairs={{8,0},{16,8},{24,16},{32,24},{40,32},{48,40},{56,48},{64,56},{72,6... | collective-permute-start | bytes 3145736 | tf_op jit(solution)/shard_map/ppermute | solution.py:24
  72.8 8.1 %products.3 = s16[8,2,272,128]{3,2,1,0:T(8,128)(2,1)} custom-call(s32[1]{0:T(128)} %bitcast.place, bf16[2,2,4,64,512]{4,3,2,1,0:T(8,128)(2,1)} %collective-permute-done.1.refs_0_, bf16[2,2,4,64,512]{4,3,2,1,0:T(8,128)(2,1)} %copy-done.5, bf16[2,2,4,64,512]{4,3,2,1,0:T(8,128)(2,1)} %get-tuple-element.26.refs_2_, bf16[2,4,4,64,512]{4,3,2,1,0:T(8,128)(2,1)} %copy-done, ...), custom_call_target="tpu_custom_call" | custom-call | flops 38654705664 | bytes 1048576 | tf_op jit(solution)/shard_map/products/pallas_call | solution.py:133
  80.9 4.5 %all-to-all-start = ((s16[8,2,272,128]{3,2,1,0:T(8,128)(2,1)}), s16[8,2,272,128]{3,2,1,0:T(8,128)(2,1)S(1)}, u32[]{:S(2)}, u32[]{:S(2)}) async-start(s16[8,2,272,128]{3,2,1,0:T(8,128)(2,1)} %products.3), calls=%async_computation | async-start | bytes 2228224 | tf_op jit(solution)/shard_map/all_to_all | solution.py:379
  85.4 3.7 %collective-permute-done.9.refs_4_.refs_5_ = bf16[2,1,8,64,512]{4,3,2,1,0:T(8,128)(2,1)} collective-permute-done((bf16[2,1,8,64,512]{4,3,2,1,0:T(8,128)(2,1)}, bf16[2,1,8,64,512]{4,3,2,1,0:T(8,128)(2,1)}, u32[]{:S(2)}, u32[]{:S(2)}) %collective-permute-start.9) | collective-permute-done | bytes 1048608 | tf_op jit(solution)/shard_map/ppermute | solution.py:24
  89.1 4.9 %products.4 = s16[8,1,272,128]{3,2,1,0:T(8,128)(2,1)} custom-call(s32[1]{0:T(128)} %bitcast.place, bf16[2,1,8,64,512]{4,3,2,1,0:T(8,128)(2,1)} %collective-permute-done.8.refs_0_.refs_1_, bf16[2,1,8,64,512]{4,3,2,1,0:T(8,128)(2,1)} %collective-permute-done.8.refs_0_.refs_1_, bf16[2,1,8,64,512]{4,3,2,1,0:T(8,128)(2,1)} %pad_maximum_fusion.refs_2_.refs_3_, ...), custom_call_target="tpu_custom_call" | custom-call | flops 19327352832 | bytes 1048576 | tf_op jit(solution)/shard_map/products/pallas_call | solution.py:133
  93.9 8.1 %all-to-all-done.terms = s16[8,2,272,128]{3,2,1,0:T(8,128)(2,1)S(1)} async-done(((s16[8,2,272,128]{3,2,1,0:T(8,128)(2,1)}), s16[8,2,272,128]{3,2,1,0:T(8,128)(2,1)S(1)}, u32[]{:S(2)}, u32[]{:S(2)}) %all-to-all-start) | async-done | bytes 1114144 | tf_op jit(solution)/shard_map/all_to_all | solution.py:379
  102.0 3.5 %all-to-all-start.1 = ((s16[8,1,272,128]{3,2,1,0:T(8,128)(2,1)}), s16[8,1,272,128]{3,2,1,0:T(8,128)(2,1)S(1)}, u32[]{:S(2)}, u32[]{:S(2)}) async-start(s16[8,1,272,128]{3,2,1,0:T(8,128)(2,1)} %products.4), calls=%async_computation.1 | async-start | bytes 1114112 | tf_op jit(solution)/shard_map/all_to_all | solution.py:379
  105.6 4.0 %collective-permute-done.11.refs_4_.refs_5_ = bf16[2,1,8,64,512]{4,3,2,1,0:T(8,128)(2,1)} collective-permute-done((bf16[2,1,8,64,512]{4,3,2,1,0:T(8,128)(2,1)S(1)}, bf16[2,1,8,64,512]{4,3,2,1,0:T(8,128)(2,1)}, u32[]{:S(2)}, u32[]{:S(2)}) %collective-permute-start.11) | collective-permute-done | bytes 1048608 | tf_op jit(solution)/shard_map/ppermute | solution.py:24
  109.6 4.8 %products.5 = s16[8,1,272,128]{3,2,1,0:T(8,128)(2,1)} custom-call(s32[1]{0:T(128)} %bitcast.place, bf16[2,1,8,64,512]{4,3,2,1,0:T(8,128)(2,1)} %collective-permute-done.10.refs_0_.refs_1_, bf16[2,1,8,64,512]{4,3,2,1,0:T(8,128)(2,1)} %collective-permute-done.10.refs_0_.refs_1_, bf16[2,1,8,64,512]{4,3,2,1,0:T(8,128)(2,1)} %copy-done.1, ...), custom_call_target="tpu_custom_call" | custom-call | flops 19327352832 | bytes 1048576 | tf_op jit(solution)/shard_map/products/pallas_call | solution.py:133
  114.4 1.8 %all-to-all-done.1.terms = s16[8,1,272,128]{3,2,1,0:T(8,128)(2,1)S(1)} async-done(((s16[8,1,272,128]{3,2,1,0:T(8,128)(2,1)}), s16[8,1,272,128]{3,2,1,0:T(8,128)(2,1)S(1)}, u32[]{:S(2)}, u32[]{:S(2)}) %all-to-all-start.1) | async-done | bytes 557088 | tf_op jit(solution)/shard_map/all_to_all | solution.py:379
  116.2 3.5 %all-to-all-start.2 = ((s16[8,1,272,128]{3,2,1,0:T(8,128)(2,1)}), s16[8,1,272,128]{3,2,1,0:T(8,128)(2,1)S(1)}, u32[]{:S(2)}, u32[]{:S(2)}) async-start(s16[8,1,272,128]{3,2,1,0:T(8,128)(2,1)} %products.5), calls=%async_computation.2 | async-start | bytes 1114112 | tf_op jit(solution)/shard_map/all_to_all | solution.py:379
  119.7 1.1 finish.3.refs_0_
  120.8 0.8 finish.4.refs_0_
  121.6 8.8 %all-to-all-done.2.terms = s16[8,1,272,128]{3,2,1,0:T(8,128)(2,1)S(1)} async-done(((s16[8,1,272,128]{3,2,1,0:T(8,128)(2,1)}), s16[8,1,272,128]{3,2,1,0:T(8,128)(2,1)S(1)}, u32[]{:S(2)}, u32[]{:S(2)}) %all-to-all-start.2) | async-done | bytes 557088 | tf_op jit(solution)/shard_map/all_to_all | solution.py:379
  130.3 0.8 finish.5
  (25 shorter events, 0.4 us)
Async XLA Ops:
  0.0 19.4 %copy-start.2 = (s32[4,64]{1,0:T(4,128)S(1)}, s32[4,64]{1,0:T(4,128)}, u32[]{:S(2)}) copy-start(s32[4,64]{1,0:T(4,128)} %live.1) | copy-start | bytes 3076
  5.6 16.5 %collective-permute-start = (bf16[2,4,4,64,512]{4,3,2,1,0:T(8,128)(2,1)}, bf16[2,4,4,64,512]{4,3,2,1,0:T(8,128)(2,1)S(1)}, u32[]{:S(2)}, u32[]{:S(2)}) collective-permute-start(bf16[2,4,4,64,512]{4,3,2,1,0:T(8,128)(2,1)} %get-tuple-element.23), channel_id=1, source_target_pairs={{0,1},{1,0},{2,3},{3,2},{4,5},{5,4},{6,7},{7,6},{8,9},{9,8},{10,11... | collective-permute-start | bytes 6291464 | tf_op jit(solution)/shard_map/ppermute | solution.py:31
  5.6 13.9 %collective-permute-start.5 = (bf16[2,4,4,192,128]{4,3,2,1,0:T(8,128)(2,1)}, bf16[2,4,4,192,128]{4,3,2,1,0:T(8,128)(2,1)}, u32[]{:S(2)}, u32[]{:S(2)}) collective-permute-start(bf16[2,4,4,192,128]{4,3,2,1,0:T(8,128)(2,1)} %get-tuple-element.30), channel_id=1, source_target_pairs={{0,1},{1,0},{2,3},{3,2},{4,5},{5,4},{6,7},{7,6},{8,9},{9,8},{10,11... | collective-permute-start | bytes 4718600 | tf_op jit(solution)/shard_map/ppermute | solution.py:31
  6.1 32.3 %collective-permute-start.1 = (bf16[2,2,4,64,512]{4,3,2,1,0:T(8,128)(2,1)}, bf16[2,2,4,64,512]{4,3,2,1,0:T(8,128)(2,1)}, u32[]{:S(2)}, u32[]{:S(2)}) collective-permute-start(bf16[2,2,4,64,512]{4,3,2,1,0:T(8,128)(2,1)} %get-tuple-element.26.refs_2_), channel_id=1, source_target_pairs={{0,8},{8,16},{16,24},{24,32},{32,40},{40,48},{48,56},{56,64},{64,7... | collective-permute-start | bytes 3145736 | tf_op jit(solution)/shard_map/ppermute | solution.py:24
  10.0 35.1 %collective-permute-start.2 = (bf16[2,2,4,64,512]{4,3,2,1,0:T(8,128)(2,1)}, bf16[2,2,4,64,512]{4,3,2,1,0:T(8,128)(2,1)}, u32[]{:S(2)}, u32[]{:S(2)}) collective-permute-start(bf16[2,2,4,64,512]{4,3,2,1,0:T(8,128)(2,1)} %get-tuple-element.26.refs_2_), channel_id=1, source_target_pairs={{8,0},{16,8},{24,16},{32,24},{40,32},{48,40},{56,48},{64,56},{72,6... | collective-permute-start | bytes 3145736 | tf_op jit(solution)/shard_map/ppermute | solution.py:24
  16.1 48.6 %collective-permute-start.6 = (bf16[2,4,4,128,128]{4,3,2,1,0:T(8,128)(2,1)}, bf16[2,4,4,128,128]{4,3,2,1,0:T(8,128)(2,1)S(1)}, u32[]{:S(2)}, u32[]{:S(2)}) collective-permute-start(bf16[2,4,4,128,128]{4,3,2,1,0:T(8,128)(2,1)} %get-tuple-element.33), channel_id=1, source_target_pairs={{0,4},{4,0},{1,5},{5,1},{2,6},{6,2},{3,7},{7,3},{8,12},{12,8},{9,1... | collective-permute-start | bytes 3145736 | tf_op jit(solution)/shard_map/ppermute | solution.py:31
  19.5 47.2 %collective-permute-start.7 = (bf16[2,4,4,128,128]{4,3,2,1,0:T(8,128)(2,1)}, bf16[2,4,4,128,128]{4,3,2,1,0:T(8,128)(2,1)S(1)}, u32[]{:S(2)}, u32[]{:S(2)}) collective-permute-start(bf16[2,4,4,128,128]{4,3,2,1,0:T(8,128)(2,1)} %get-tuple-element.34), channel_id=1, source_target_pairs={{0,5},{1,4},{4,1},{5,0},{2,7},{3,6},{6,3},{7,2},{8,13},{9,12},{12,... | collective-permute-start | bytes 3145736 | tf_op jit(solution)/shard_map/ppermute | solution.py:31
  22.1 21.6 %copy-start = (bf16[2,4,4,64,512]{4,3,2,1,0:T(8,128)(2,1)}, bf16[2,4,4,64,512]{4,3,2,1,0:T(8,128)(2,1)S(1)}, u32[]{:S(2)}) copy-start(bf16[2,4,4,64,512]{4,3,2,1,0:T(8,128)(2,1)S(1)} %collective-permute-done.refs_3_) | copy-start | bytes 6291460
  22.2 38.6 %collective-permute-start.3 = (bf16[2,2,4,64,512]{4,3,2,1,0:T(8,128)(2,1)S(1)}, bf16[2,2,4,64,512]{4,3,2,1,0:T(8,128)(2,1)S(1)}, u32[]{:S(2)}, u32[]{:S(2)}) collective-permute-start(bf16[2,2,4,64,512]{4,3,2,1,0:T(8,128)(2,1)S(1)} %slice.19), channel_id=1, source_target_pairs={{0,8},{8,16},{16,24},{24,32},{32,40},{40,48},{48,56},{56,64},{64,7... | collective-permute-start | bytes 3145736 | tf_op jit(solution)/shard_map/ppermute | solution.py:24
  38.4 34.3 %collective-permute-start.4 = (bf16[2,2,4,64,512]{4,3,2,1,0:T(8,128)(2,1)S(1)}, bf16[2,2,4,64,512]{4,3,2,1,0:T(8,128)(2,1)}, u32[]{:S(2)}, u32[]{:S(2)}) collective-permute-start(bf16[2,2,4,64,512]{4,3,2,1,0:T(8,128)(2,1)S(1)} %slice.19), channel_id=1, source_target_pairs={{8,0},{16,8},{24,16},{32,24},{40,32},{48,40},{56,48},{64,56},{72,6... | collective-permute-start | bytes 3145736 | tf_op jit(solution)/shard_map/ppermute | solution.py:24
  45.0 40.3 %collective-permute-start.8 = (bf16[2,1,8,64,512]{4,3,2,1,0:T(8,128)(2,1)}, bf16[2,1,8,64,512]{4,3,2,1,0:T(8,128)(2,1)}, u32[]{:S(2)}, u32[]{:S(2)}) collective-permute-start(bf16[2,1,8,64,512]{4,3,2,1,0:T(8,128)(2,1)} %pad_maximum_fusion.refs_2_.refs_3_), channel_id=1, source_target_pairs={{0,8},{8,16},{16,24},{24,32},{32,40},{40,48},{48,56},{56,64},{64,7... | collective-permute-start | bytes 3145736 | tf_op jit(solution)/shard_map/ppermute | solution.py:24
  47.1 33.8 %copy-start.1 = (bf16[2,1,8,64,512]{4,3,2,1,0:T(8,128)(2,1)}, bf16[2,1,8,64,512]{4,3,2,1,0:T(8,128)(2,1)S(1)}, u32[]{:S(2)}) copy-start(bf16[2,1,8,64,512]{4,3,2,1,0:T(8,128)(2,1)S(1)} %pad_maximum_fusion.1.refs_2_.refs_3_) | copy-start | bytes 3145732
  60.8 5.9 %copy-start.5 = (bf16[2,2,4,64,512]{4,3,2,1,0:T(8,128)(2,1)}, bf16[2,2,4,64,512]{4,3,2,1,0:T(8,128)(2,1)S(1)}, u32[]{:S(2)}) copy-start(bf16[2,2,4,64,512]{4,3,2,1,0:T(8,128)(2,1)S(1)} %collective-permute-done.3.refs_1_) | copy-start | bytes 3145732
  60.8 28.3 %collective-permute-start.9 = (bf16[2,1,8,64,512]{4,3,2,1,0:T(8,128)(2,1)}, bf16[2,1,8,64,512]{4,3,2,1,0:T(8,128)(2,1)}, u32[]{:S(2)}, u32[]{:S(2)}) collective-permute-start(bf16[2,1,8,64,512]{4,3,2,1,0:T(8,128)(2,1)} %pad_maximum_fusion.refs_2_.refs_3_), channel_id=1, source_target_pairs={{8,0},{16,8},{24,16},{32,24},{40,32},{48,40},{56,48},{64,56},{72,6... | collective-permute-start | bytes 3145736 | tf_op jit(solution)/shard_map/ppermute | solution.py:24
  64.8 8.0 %copy-start.3 = (bf16[2,4,4,128,128]{4,3,2,1,0:T(8,128)(2,1)}, bf16[2,4,4,128,128]{4,3,2,1,0:T(8,128)(2,1)S(1)}, u32[]{:S(2)}) copy-start(bf16[2,4,4,128,128]{4,3,2,1,0:T(8,128)(2,1)S(1)} %collective-permute-done.6.refs_8_) | copy-start | bytes 3145732
  64.8 40.8 %collective-permute-start.10 = (bf16[2,1,8,64,512]{4,3,2,1,0:T(8,128)(2,1)S(1)}, bf16[2,1,8,64,512]{4,3,2,1,0:T(8,128)(2,1)}, u32[]{:S(2)}, u32[]{:S(2)}) collective-permute-start(bf16[2,1,8,64,512]{4,3,2,1,0:T(8,128)(2,1)S(1)} %pad_maximum_fusion.1.refs_2_.refs_3_), channel_id=1, source_target_pairs={{0,8},{8,16},{16,24},{24,32},{32,40},{40,48},{48,56},{56,64},{64,7... | collective-permute-start | bytes 3145736 | tf_op jit(solution)/shard_map/ppermute | solution.py:24
  66.7 6.1 %copy-start.4 = (bf16[2,4,4,128,128]{4,3,2,1,0:T(8,128)(2,1)}, bf16[2,4,4,128,128]{4,3,2,1,0:T(8,128)(2,1)S(1)}, u32[]{:S(2)}) copy-start(bf16[2,4,4,128,128]{4,3,2,1,0:T(8,128)(2,1)S(1)} %collective-permute-done.7.refs_9_) | copy-start | bytes 3145732
  66.7 42.9 %collective-permute-start.11 = (bf16[2,1,8,64,512]{4,3,2,1,0:T(8,128)(2,1)S(1)}, bf16[2,1,8,64,512]{4,3,2,1,0:T(8,128)(2,1)}, u32[]{:S(2)}, u32[]{:S(2)}) collective-permute-start(bf16[2,1,8,64,512]{4,3,2,1,0:T(8,128)(2,1)S(1)} %pad_maximum_fusion.1.refs_2_.refs_3_), channel_id=1, source_target_pairs={{8,0},{16,8},{24,16},{32,24},{40,32},{48,40},{56,48},{64,56},{72,6... | collective-permute-start | bytes 3145736 | tf_op jit(solution)/shard_map/ppermute | solution.py:24
  80.9 21.2 %all-to-all-start = ((s16[8,2,272,128]{3,2,1,0:T(8,128)(2,1)}), s16[8,2,272,128]{3,2,1,0:T(8,128)(2,1)S(1)}, u32[]{:S(2)}, u32[]{:S(2)}) async-start(s16[8,2,272,128]{3,2,1,0:T(8,128)(2,1)} %products.3), calls=%async_computation | async-start | bytes 2228224 | tf_op jit(solution)/shard_map/all_to_all | solution.py:379
  102.0 14.2 %all-to-all-start.1 = ((s16[8,1,272,128]{3,2,1,0:T(8,128)(2,1)}), s16[8,1,272,128]{3,2,1,0:T(8,128)(2,1)S(1)}, u32[]{:S(2)}, u32[]{:S(2)}) async-start(s16[8,1,272,128]{3,2,1,0:T(8,128)(2,1)} %products.4), calls=%async_computation.1 | async-start | bytes 1114112 | tf_op jit(solution)/shard_map/all_to_all | solution.py:379
  116.2 14.2 %all-to-all-start.2 = ((s16[8,1,272,128]{3,2,1,0:T(8,128)(2,1)}), s16[8,1,272,128]{3,2,1,0:T(8,128)(2,1)S(1)}, u32[]{:S(2)}, u32[]{:S(2)}) async-start(s16[8,1,272,128]{3,2,1,0:T(8,128)(2,1)} %products.5), calls=%async_computation.2 | async-start | bytes 1114112 | tf_op jit(solution)/shard_map/all_to_all | solution.py:379
